TPU v7x, 32 devices: a whole 2x2x4 slice. The times are simulated.
32 devices in a mesh: wide: 8 (over y, x, core), narrow: 4 (over z).
Axes of the slice: x: 2, y: 2, z: 4, core: 2. Of those that a mesh axis runs over, the one named last changes fastest.
Arguments:
- tokens: bfloat16 [32, 2048, 768], P(('wide', 'narrow')), may hold values from -6 to 6
- cotangent: bfloat16 [32, 2048, 768], P(('wide', 'narrow')), may hold values from -6 to 6
- lengths: int32 [32], P(('wide', 'narrow')), may hold values from 256 to 1024
- levels: int32 [32, 64], P(('wide', 'narrow')), may hold values from 0 to 7
- owners: int32 [4], replicated, may hold values from 0 to 7, as said below
- master_slots: float32 [8, 3072, 768], P('wide', 'narrow')
- moment_slots: float32 [8, 3072, 768], P('wide', 'narrow'), may hold values from -0.001953125 to 0.001953125
- square_slots: float32 [8, 3072, 768], P('wide', 'narrow'), may hold values from 7.052775e-08 to 1.128444e-06
- vec_master: float32 [15, 768], replicated
- vec_moment: float32 [15, 768], replicated, may hold values from -0.001953125 to 0.001953125
- vec_square: float32 [15, 768], replicated, may hold values from 7.052775e-08 to 1.128444e-06
Outputs:
- output: bfloat16 [32, 2048, 768], P(('wide', 'narrow'))
- input_grad: float32 [32, 2048, 768], P(('wide', 'narrow'))
- master_new_slots: float32 [8, 3072, 768], P('wide', 'narrow')
- moment_new_slots: float32 [8, 3072, 768], P('wide', 'narrow')
- square_new_slots: float32 [8, 3072, 768], P('wide', 'narrow')
- vec_grad: float32 [15, 768], replicated
- vec_moment_new: float32 [15, 768], replicated
- vec_square_new: float32 [15, 768], replicated
- vec_master_new: float32 [15, 768], replicated
- grad_norm: float32 [1], replicated
Inputs may be any that keep to these rules, and one draw needn't show every extreme that they name: Four different indices of wide, the owners of the query-key-value, output, up and down projections in this order.
All inputs are finite; a program needn't handle non-finite values.
Results may differ from a plain program's by a relative error of at most 0.014.
The roundings to bfloat16 on the way count: a program that leaves them out, or rounds other values in their place, can miss the bound.
Values may be sent and summed in bfloat16 or wider, within the bound.
No kernel may reach another device: no remote copies, remote signals or barrier semaphores. Data moves between devices by JAX's collectives and lax.ppermute only.
A program may use at most 320 MiB of HBM per device.

v0:
```python
from functools import partial

import jax
import jax.numpy as jnp
from jax import lax
from jax.sharding import PartitionSpec as P

D = 768
HEADS = 12
HEAD_DIM = 64
FF = 3072
BLOCK = 16
SEQ = 1024
LEVELS = 8
STEP = 10


ln_eps = 1e-05
learn_rate = 0.05
vector_rate = 0.5
decay_rate = 0.1
moment_decay = 0.5
adam_eps = 1e-08
masked_score = -1e30
rope_base = 10000.0


def spread(value, axis, source):
    kept = jnp.where(lax.axis_index(axis) == source, value, 0).astype(value.dtype)
    return lax.psum(kept, axis)


def shortened(value):

    def short(part):
        return part.astype(jnp.bfloat16) if part.dtype == jnp.float32 else part

    return jax.tree.map(short, value)


def layer_norm(entries, gain):
    centred = entries - jnp.mean(entries, axis=-1, keepdims=True)
    scaling = lax.rsqrt(jnp.mean(centred * centred, axis=-1, keepdims=True) + ln_eps)
    return centred * scaling * gain


def rope_tables(row_count, head_dim):
    positions = (jnp.arange(row_count, dtype=jnp.int32) % SEQ).astype(jnp.float32)
    exponents = jnp.arange(head_dim // 2, dtype=jnp.float32) * (2.0 / head_dim)
    angles = positions[:, None] * (rope_base ** (-exponents))[None, :]
    return (jnp.cos(angles)[:, None, :], jnp.sin(angles)[:, None, :])


def rotate(entries, cos_table, sin_table):
    half_dim = entries.shape[-1] // 2
    front_half = entries[..., :half_dim]
    back_half = entries[..., half_dim:]
    return jnp.concatenate(
        [
            front_half * cos_table - back_half * sin_table,
            back_half * cos_table + front_half * sin_table,
        ],
        axis=-1,
    )


def to_groups(tensor, groups):
    seq_count, row_count, head_count, head_dim = tensor.shape
    return jnp.moveaxis(
        tensor.reshape(seq_count, row_count, groups, head_count // groups, head_dim), 2, 0
    )


def from_groups(tensor):
    groups, seq_count, row_count, per_group, head_dim = tensor.shape
    return jnp.moveaxis(tensor, 0, 2).reshape(seq_count, row_count, groups * per_group * head_dim)


def key_ranges(row_start, block_rows):
    if row_start < SEQ:
        return [(row_start, row_start + block_rows), (SEQ, SEQ + row_start + block_rows)]
    return [(SEQ, row_start + block_rows)]


def block_visible(row_start, block_rows, ranges, lengths):
    query_index = row_start + jnp.arange(block_rows, dtype=jnp.int32)
    key_index = jnp.concatenate(
        [jnp.arange(low_end, high_end, dtype=jnp.int32) for low_end, high_end in ranges]
    )
    query_noised = (query_index < SEQ)[:, None]
    key_noised = (key_index < SEQ)[None, :]
    query_block = (query_index % SEQ // BLOCK)[:, None]
    key_block = (key_index % SEQ // BLOCK)[None, :]
    same = query_noised & key_noised & (query_block == key_block)
    earlier = query_noised & ~key_noised & (key_block < query_block)
    causal = ~query_noised & ~key_noised & (key_block <= query_block)
    layout = same | earlier | causal
    kept = ((key_index % SEQ)[None, None, :] < lengths[:, None, None]) | (
        query_index[:, None] == key_index[None, :]
    )[None]
    return layout[None] & kept


def take_keys(tensor, ranges):
    return jnp.concatenate([tensor[:, :, low_end:high_end] for low_end, high_end in ranges], axis=2)


def forward_group(queries, key_block, value_block, visible):
    scaling = HEAD_DIM ** (-0.5)
    scores = (
        jnp.einsum("bqhd,bkhd->bhqk", queries, key_block, preferred_element_type=jnp.float32)
        * scaling
    )
    scores = jnp.where(visible[:, None], scores, masked_score)
    row_max = jnp.max(scores, axis=-1, keepdims=True)
    expo = jnp.exp(scores - row_max)
    totals = jnp.sum(expo, axis=-1, keepdims=True)
    probs = (expo / totals).astype(jnp.bfloat16)
    attended = jnp.einsum("bhqk,bkhd->bqhd", probs, value_block, preferred_element_type=jnp.float32)
    return (attended, row_max + jnp.log(totals))


def backward_group(queries, key_block, value_block, grad_rows, log_total, visible):
    scaling = HEAD_DIM ** (-0.5)
    scores = (
        jnp.einsum("bqhd,bkhd->bhqk", queries, key_block, preferred_element_type=jnp.float32)
        * scaling
    )
    scores = jnp.where(visible[:, None], scores, masked_score)
    probs = jnp.exp(scores - log_total)
    probs_low = probs.astype(jnp.bfloat16)
    prob_grad = jnp.einsum(
        "bqhd,bkhd->bhqk", grad_rows, value_block, preferred_element_type=jnp.float32
    )
    row_dot = jnp.sum(probs * prob_grad, axis=-1, keepdims=True)
    score_grad = (probs * (prob_grad - row_dot)).astype(jnp.bfloat16)
    query_grad = (
        jnp.einsum("bhqk,bkhd->bqhd", score_grad, key_block, preferred_element_type=jnp.float32)
        * scaling
    )
    key_grad = (
        jnp.einsum("bhqk,bqhd->bkhd", score_grad, queries, preferred_element_type=jnp.float32)
        * scaling
    )
    value_grad = jnp.einsum(
        "bhqk,bqhd->bkhd", probs_low, grad_rows, preferred_element_type=jnp.float32
    )
    return (query_grad, key_grad, value_grad)


def adam(grad, moment, square, master, decay, rate):
    moment_new = moment_decay * moment + (1.0 - moment_decay) * grad
    square_new = moment_decay * square + (1.0 - moment_decay) * grad * grad
    correction = 1.0 - moment_decay**STEP
    master_new = master * (1.0 - rate * decay) - rate * (moment_new / correction) / (
        jnp.sqrt(square_new / correction) + adam_eps
    )
    return (moment_new, square_new, master_new)


def local(
    tokens,
    cotangent,
    lengths,
    levels,
    owners,
    master_slots,
    moment_slots,
    square_slots,
    vec_master,
    vec_moment,
    vec_square,
):
    narrow_count = lax.axis_size("narrow")
    wide_count = lax.axis_size("wide")
    position = lax.axis_index("wide")
    slot_rows = master_slots.shape[1]
    shapes = ((D, 3 * D), (D, D), (D, FF), (FF, D))

    def share_of(slots, index_k):
        rows, cols = shapes[index_k]
        count = rows * cols // (narrow_count * D)
        return slots[0, :count].reshape(rows // narrow_count, cols)

    def owner_share(index_k):
        share = share_of(master_slots, index_k).astype(jnp.bfloat16)
        return spread(share, "wide", owners[index_k])

    shards = tuple((owner_share(index_k) for index_k in range(4)))
    w_qkv, w_out, w_up, w_down = jax.tree.map(
        lambda part, own: part.astype(own.dtype),
        lax.all_gather(shortened(shards), "narrow", axis=0, tiled=True),
        shards,
    )
    seq_count, row_count, model_width = tokens.shape
    groups = 2
    block_rows = min(512, SEQ // 2)
    block_count = row_count // block_rows
    up_rows = FF // D
    block_total = SEQ // BLOCK
    gain_one = vec_master[0]
    gain_two = vec_master[1]
    down_bias = vec_master[2]
    up_bias = vec_master[3 : 3 + up_rows].reshape(FF)
    table_rows = vec_master[3 + up_rows :]
    onehot = (levels[:, :, None] == jnp.arange(LEVELS, dtype=jnp.int32)[None, None, :]).astype(
        jnp.float32
    )
    block_embed = jnp.einsum("bnl,ld->bnd", onehot, table_rows, precision=lax.Precision.HIGHEST)
    level_rows = jnp.broadcast_to(
        block_embed[:, :, None, :], (seq_count, block_total, BLOCK, D)
    ).reshape(seq_count, SEQ, D)
    hidden = tokens.astype(jnp.float32) + jnp.concatenate(
        [level_rows, jnp.zeros_like(level_rows)], axis=1
    )
    normed_one, norm_one_back = jax.vjp(layer_norm, hidden, gain_one)
    attn_in = normed_one.astype(jnp.bfloat16).reshape(seq_count * row_count, D)
    projected = jnp.dot(attn_in, w_qkv, preferred_element_type=jnp.float32).reshape(
        seq_count, row_count, 3, HEADS, HEAD_DIM
    )
    cos_table, sin_table = rope_tables(row_count, HEAD_DIM)
    query_heads = to_groups(
        rotate(projected[:, :, 0], cos_table, sin_table).astype(jnp.bfloat16), groups
    )
    key_heads = to_groups(
        rotate(projected[:, :, 1], cos_table, sin_table).astype(jnp.bfloat16), groups
    )
    value_heads = to_groups(projected[:, :, 2].astype(jnp.bfloat16), groups)
    attended_parts = []
    log_totals = []
    for block_index in range(block_count):
        row_start = block_index * block_rows
        ranges = key_ranges(row_start, block_rows)
        visible = block_visible(row_start, block_rows, ranges, lengths)
        query_block = query_heads[:, :, row_start : row_start + block_rows]

        def forward_items(items, visible=visible):
            return forward_group(items[0], items[1], items[2], visible)

        attended_block, log_total = lax.map(
            forward_items,
            (query_block, take_keys(key_heads, ranges), take_keys(value_heads, ranges)),
        )
        attended_parts.append(attended_block)
        log_totals.append(log_total)
    attended = (
        from_groups(jnp.concatenate(attended_parts, axis=2))
        .astype(jnp.bfloat16)
        .reshape(seq_count * row_count, D)
    )
    attn_out = jnp.dot(attended, w_out, preferred_element_type=jnp.float32).reshape(
        seq_count, row_count, D
    )
    resid = hidden + attn_out
    normed_two, norm_two_back = jax.vjp(layer_norm, resid, gain_two)
    mlp_in = normed_two.astype(jnp.bfloat16).reshape(seq_count * row_count, D)
    pre_act = jnp.dot(mlp_in, w_up, preferred_element_type=jnp.float32) + up_bias
    activated, gelu_back = jax.vjp(partial(jax.nn.gelu, approximate=True), pre_act)
    act_low = activated.astype(jnp.bfloat16)
    mlp_out = jnp.dot(act_low, w_down, preferred_element_type=jnp.float32).reshape(
        seq_count, row_count, D
    )
    output = (resid + mlp_out + down_bias).astype(jnp.bfloat16)
    w_qkv, w_out, w_up, w_down = jax.tree.map(
        lambda part, own: part.astype(own.dtype),
        lax.all_gather(shortened(shards), "narrow", axis=0, tiled=True),
        shards,
    )
    row_scale = 1.0 / (2 * SEQ)
    grad_rows = cotangent.reshape(seq_count * row_count, D)
    down_bias_grad = jnp.sum(cotangent, axis=(0, 1), dtype=jnp.float32)
    down_grad = jnp.einsum("rf,rd->fd", act_low, grad_rows, preferred_element_type=jnp.float32)
    act_grad = jnp.einsum("rd,fd->rf", grad_rows, w_down, preferred_element_type=jnp.float32)
    (pre_grad,) = gelu_back(act_grad)
    up_bias_grad = jnp.sum(pre_grad, axis=0)
    pre_low = pre_grad.astype(jnp.bfloat16)
    up_grad = jnp.einsum("rd,rf->df", mlp_in, pre_low, preferred_element_type=jnp.float32)
    mlp_in_grad = jnp.einsum(
        "rf,df->rd", pre_low, w_up, preferred_element_type=jnp.float32
    ).reshape(seq_count, row_count, D)
    resid_part, gain_two_grad = norm_two_back(mlp_in_grad)
    resid_grad = cotangent.astype(jnp.float32) + resid_part
    resid_low = resid_grad.astype(jnp.bfloat16).reshape(seq_count * row_count, D)
    out_grad = jnp.einsum("rc,rd->cd", attended, resid_low, preferred_element_type=jnp.float32)
    attended_grad = jnp.einsum(
        "rd,cd->rc", resid_low, w_out, preferred_element_type=jnp.float32
    ).astype(jnp.bfloat16)
    attended_grad = to_groups(attended_grad.reshape(seq_count, row_count, HEADS, HEAD_DIM), groups)
    key_total = jnp.zeros(key_heads.shape, jnp.float32)
    value_total = jnp.zeros(value_heads.shape, jnp.float32)
    query_parts = []
    for block_index in range(block_count):
        row_start = block_index * block_rows
        ranges = key_ranges(row_start, block_rows)
        visible = block_visible(row_start, block_rows, ranges, lengths)

        def backward_items(items, visible=visible):
            return backward_group(items[0], items[1], items[2], items[3], items[4], visible)

        query_part, key_part, value_part = lax.map(
            backward_items,
            (
                query_heads[:, :, row_start : row_start + block_rows],
                take_keys(key_heads, ranges),
                take_keys(value_heads, ranges),
                attended_grad[:, :, row_start : row_start + block_rows],
                log_totals[block_index],
            ),
        )
        query_parts.append(query_part)
        offset = 0
        for low_end, high_end in ranges:
            span = high_end - low_end
            key_total = key_total.at[:, :, low_end:high_end].add(
                key_part[:, :, offset : offset + span]
            )
            value_total = value_total.at[:, :, low_end:high_end].add(
                value_part[:, :, offset : offset + span]
            )
            offset = offset + span
    head_shape = (seq_count, row_count, HEADS, HEAD_DIM)
    query_grad = rotate(
        from_groups(jnp.concatenate(query_parts, axis=2)).reshape(head_shape), cos_table, -sin_table
    )
    key_grad = rotate(from_groups(key_total).reshape(head_shape), cos_table, -sin_table)
    value_grad = from_groups(value_total).reshape(head_shape)
    projected_grad = (
        jnp.stack([query_grad, key_grad, value_grad], axis=2)
        .astype(jnp.bfloat16)
        .reshape(seq_count * row_count, 3 * D)
    )
    qkv_grad = jnp.einsum("rd,rc->dc", attn_in, projected_grad, preferred_element_type=jnp.float32)
    attn_in_grad = jnp.einsum(
        "rc,dc->rd", projected_grad, w_qkv, preferred_element_type=jnp.float32
    ).reshape(seq_count, row_count, D)
    hidden_part, gain_one_grad = norm_one_back(attn_in_grad)
    input_grad = resid_grad + hidden_part
    level_sums = input_grad[:, :SEQ].reshape(seq_count, block_total, BLOCK, D).sum(axis=2)
    table_grad = jnp.einsum("bnl,bnd->ld", onehot, level_sums, precision=lax.Precision.HIGHEST)
    vec_local = (
        jnp.concatenate(
            [
                gain_one_grad[None],
                gain_two_grad[None],
                down_bias_grad[None],
                up_bias_grad.reshape(up_rows, D),
                table_grad,
            ],
            axis=0,
        )
        * row_scale
    )
    qkv_share, out_share, up_share, down_share = (
        lax.psum_scatter(
            (qkv_grad * row_scale).astype(jnp.bfloat16), "narrow", scatter_dimension=0, tiled=True
        ).astype(jnp.float32),
        lax.psum_scatter(
            (out_grad * row_scale).astype(jnp.bfloat16), "narrow", scatter_dimension=0, tiled=True
        ).astype(jnp.float32),
        lax.psum_scatter(
            (up_grad * row_scale).astype(jnp.bfloat16), "narrow", scatter_dimension=0, tiled=True
        ).astype(jnp.float32),
        lax.psum_scatter(
            (down_grad * row_scale).astype(jnp.bfloat16), "narrow", scatter_dimension=0, tiled=True
        ).astype(jnp.float32),
    )
    narrow_shares = (qkv_share, out_share, up_share, down_share)
    summed = lax.psum(
        (narrow_shares[0], narrow_shares[1], narrow_shares[2], narrow_shares[3]), "wide"
    )
    pieces = tuple(
        (
            lax.dynamic_slice_in_dim(
                total.reshape(-1),
                position * (total.size // wide_count),
                total.size // wide_count,
                0,
            )
            for total in summed
        )
    )
    square_local = sum((jnp.sum(piece * piece) for piece in pieces))
    vec_total, square_total = lax.psum((vec_local, square_local), ("narrow", "wide"))
    norm_value = jnp.sqrt(square_total + jnp.sum(vec_total * vec_total))
    clip_factor = jnp.minimum(1.0, 1.0 / (norm_value + 1e-06))
    master_out = jnp.zeros((slot_rows, D), jnp.float32)
    moment_out = jnp.zeros((slot_rows, D), jnp.float32)
    square_out = jnp.zeros((slot_rows, D), jnp.float32)
    for index_k in range(4):
        clipped = summed[index_k] * clip_factor
        moment_new, square_new, master_new = adam(
            clipped,
            share_of(moment_slots, index_k),
            share_of(square_slots, index_k),
            share_of(master_slots, index_k),
            decay_rate,
            learn_rate,
        )
        is_owner = position == owners[index_k]
        count = master_new.size // D
        filler = jnp.zeros((slot_rows - count, D), jnp.float32)
        master_out = master_out + jnp.where(
            is_owner, jnp.concatenate([master_new.reshape(count, D), filler], axis=0), 0.0
        )
        moment_out = moment_out + jnp.where(
            is_owner, jnp.concatenate([moment_new.reshape(count, D), filler], axis=0), 0.0
        )
        square_out = square_out + jnp.where(
            is_owner, jnp.concatenate([square_new.reshape(count, D), filler], axis=0), 0.0
        )
    vec_clipped = vec_total * clip_factor
    vec_moment_new, vec_square_new, vec_master_new = adam(
        vec_clipped, vec_moment, vec_square, vec_master, 0.0, vector_rate
    )
    return (
        output,
        input_grad,
        master_out[None],
        moment_out[None],
        square_out[None],
        vec_clipped,
        vec_moment_new,
        vec_square_new,
        vec_master_new,
        norm_value.reshape(1),
    )


def solution(mesh):
    placed = (
        P(("wide", "narrow"), None, None),
        P(("wide", "narrow"), None, None),
        P(("wide", "narrow")),
        P(("wide", "narrow"), None),
        P(),
        P("wide", "narrow", None),
        P("wide", "narrow", None),
        P("wide", "narrow", None),
        P(),
        P(),
        P(),
    )
    return jax.shard_map(
        local,
        mesh=mesh,
        in_specs=placed,
        out_specs=(
            P(("wide", "narrow"), None, None),
            P(("wide", "narrow"), None, None),
            P("wide", "narrow", None),
            P("wide", "narrow", None),
            P("wide", "narrow", None),
            P(),
            P(),
            P(),
            P(),
            P(),
        ),
        check_vma=False,
    )
```

profile of v0, /device:TPU:0, one launch (start us, length us, event | category | flops | bytes accessed | tf_op | source)
XLA Modules:
  0.0 1276.3 jit_solution(14780663839166322795)
XLA Ops:
  18.8 77.2 %all-reduce.15.cloned.1.call-done = (bf16[192,2304]{1,0:T(8,128)(2,1)}, bf16[192,768]{1,0:T(8,128)(2,1)}, bf16[192,3072]{1,0:T(8,128)(2,1)}, bf16[768,768]{1,0:T(8,128)(2,1)}) async-done(((bf16[192,2304]{1,0:T(8,128)(2,1)}, bf16[192,768]{1,0:T(8,128)(2,1)}, bf16[192,3072]{1,0:T(8,128)(2,1)}, bf16[768,768]{1,0:T(8,128)(2,1)}), (bf16[192,2304]{1,0:T(8,128)(2,1)}, bf16[192,768]{1,0:T(8,128)(2,1)}, ...) | async-done | bytes 3538960 | tf_op jit(solution)/shard_map/psum | solution.py:30
  116.7 51.0 %all-gather.5.cloned.1.call-done = bf16[768,2304]{1,0:T(8,128)(2,1)} async-done(((bf16[192,2304]{1,0:T(8,128)(2,1)}), bf16[768,2304]{1,0:T(8,128)(2,1)}) %all-gather.5.cloned.1.call-update) | async-done | bytes 3538960 | tf_op jit(solution)/shard_map/all_gather | solution.py:192
  218.2 41.7 %while.125 = (s32[]{:T(128)}, bf16[2,1,512,6,64]{2,4,3,1,0:T(8,128)(2,1)}, f32[2,1,6,512,1]{3,2,4,1,0:T(8,128)S(1)}, bf16[2,1,1536,6,64]{2,4,3,1,0:T(8,128)(2,1)...) while((s32[]{:T(128)}, ...), condition=%wide.region_10.11_spmd.clone, body=%wide.region_7.10_spmd.clone.sunk | while | flops 1275589632 | bytes 66588348 | solution.py:240
  260.8 27.7 %while.127 = (s32[]{:T(128)}, bf16[2,1,512,6,64]{2,4,3,1,0:T(8,128)(2,1)}, f32[2,1,6,512,1]{3,2,4,1,0:T(8,128)}, bf16[2,1,1024,6,64]{2,4,3,1,0:T(8,128)(2,1)}, b...) while((s32[]{:T(128)}, ...), condition=%wide.region_18.19_spmd.clone, body=%wide.region_15.18_spmd.clone.sunk | while | flops 850392064 | bytes 55310580 | solution.py:240
  292.6 25.3 %while.124 = (s32[]{:T(128)}, bf16[2,1,512,6,64]{2,4,3,1,0:T(8,128)(2,1)}, f32[2,1,6,512,1]{3,2,4,1,0:T(8,128)S(1)}, bf16[2,1,1024,6,64]{2,4,3,1,0:T(8,128)(2,1)...) while((s32[]{:T(128)}, ...), condition=%wide.region_6.7_spmd.clone, body=%wide.region_3.6_spmd.clone.sunk | while | flops 850392064 | bytes 55316716 | solution.py:240
  319.0 14.7 %while.126 = (s32[]{:T(128)}, bf16[2,1,512,6,64]{2,4,3,1,0:T(8,128)(2,1)}, f32[2,1,6,512,1]{3,2,4,1,0:T(8,128)S(1)}, bf16[2,1,512,6,64]{2,4,3,1,0:T(8,128)(2,1)}...) while((s32[]{:T(128)}, ...), condition=%wide.region_14.15_spmd.clone, body=%wide.region_11.14_spmd.clone.sunk | while | flops 425194496 | bytes 31452884 | solution.py:240
  347.3 24.6 %multiply_convert_fusion.4 = (bf16[2048,3072]{1,0:T(8,128)(2,1)}, f32[2048,3072]{1,0:T(8,128)}) fusion(f32[3072]{0:T(1024)S(1)} %copy-done.160, bf16[768,3072]{1,0:T(8,128)(2,1)} %all-gather.9.cloned.1.call-done, f32[1,2048,768]{2,1,0:T(8,128)} %copy-done.23, f32[768]{0:T(1024)S(1)} %copy-done.157, f32[2048]{0:T(1024)S(1)} %fusion.283, ...), kind=kOutput, calls=%fused_computation.261 | convolution fusion | flops 9732882432 | bytes 48790528 | tf_op jit(solution)/shard_map/dot_general | solution.py:257
  377.6 34.3 %fusion.334 = (f32[3072]{0:T(1024)}, bf16[2048,3072]{1,0:T(8,128)(2,1)}) fusion(f32[2048,3072]{1,0:T(8,128)} %get-tuple-element.1217, f32[3072]{0:T(1024)S(1)} %copy-done.160, bf16[3072,768]{1,0:T(8,128)(2,1)} %all-gather.11.cloned.1.call-done, bf16[1,2048,768]{2,1,0:T(8,128)(2,1)} %param.52), kind=kOutput, calls=%fused_computation.530 | convolution fusion | flops 9802085376 | bytes 45637632 | tf_op jit(solution)/shard_map/rd,fd->rf/dot_general | solution.py:273
  411.9 15.9 %fusion.231 = (f32[768]{0:T(1024)}, f32[2048]{0:T(1024)S(1)}, f32[2048,768]{1,0:T(8,128)S(1)}) fusion(f32[1,2048,768]{2,1,0:T(8,128)S(1)} %bitcast.663, f32[2048]{0:T(1024)S(1)} %fusion.283, f32[2048]{0:T(1024)S(1)} %broadcast_multiply_fusion.5, f32[768]{0:T(1024)S(1)} %copy-done.157, bf16[768,3072]{1,0:T(8,128)(2,1)} %all-gather.9.cloned.1.call-done, ...), kind=kOutput, calls=%fused_computation.279 | convolution fusion | flops 9674683392 | bytes 29915136 | tf_op jit(solution)/shard_map/rf,df->rd/dot_general | solution.py:278
  448.2 25.8 %while.130 = (s32[]{:T(128)}, f32[2,1,512,6,64]{2,4,3,1,0:T(8,128)}, f32[2,1,512,6,64]{2,4,3,1,0:T(8,128)}, f32[2,1,512,6,64]{2,4,3,1,0:T(8,128)}, bf16[2,1,512,...) while((s32[]{:T(128)}, f32[2,1,512,6,64]{2,4,3,1,0:T(8,128)}, ...), condition=%wide.region_34.35_spmd.clone, body=%wide.region_32.34_spmd.clone.sunk | while | flops 1034286080 | bytes 75471656 | solution.py:300
  479.8 60.3 %while.131 = (s32[]{:T(128)}, f32[2,1,512,6,64]{2,4,3,1,0:T(8,128)}, f32[2,1,1024,6,64]{2,4,3,1,0:T(8,128)}, f32[2,1,1024,6,64]{2,4,3,1,0:T(8,128)}, bf16[2,1,10...) while((s32[]{:T(128)}, f32[2,1,512,6,64]{2,4,3,1,0:T(8,128)}, ...), condition=%wide.region_37.38_spmd.clone, body=%wide.region_35.37_spmd.clone.sunk | while | flops 2068378624 | bytes 145343824 | solution.py:300
  541.4 106.8 %while.129 = (s32[]{:T(128)}, f32[2,1,512,6,64]{2,4,3,1,0:T(8,128)}, f32[2,1,1536,6,64]{2,4,3,1,0:T(8,128)}, f32[2,1,1536,6,64]{2,4,3,1,0:T(8,128)}, bf16[2,1,15...) while((s32[]{:T(128)}, f32[2,1,512,6,64]{2,4,3,1,0:T(8,128)}, ...), condition=%wide.region_31.32_spmd.clone, body=%wide.region_29.31_spmd.clone.sunk | while | flops 3102471168 | bytes 292281280 | solution.py:300
  560.6 13.9 %multiply_reduce_fusion.16 = (f32[6,512]{1,0:T(8,128)S(1)}, f32[6,512,1536]{2,1,0:T(8,128)}) fusion(f32[6,512,1536]{2,1,0:T(8,128)} %copy-done, f32[6,512]{1,0:T(8,128)S(1)} %dynamic-slice_bitcast_fusion.9, pred[512,1536]{1,0:T(8,128)(4,1)S(1)} %and_bitcast_fusion.15, bf16[2,1,1536,6,64]{2,4,3,1,0:T(8,128)(2,1)S(1)} %copy-done.22, s32[]{:T(128)S(6)} %copy.126, ...), kind=kOutput, calls=%fused_computation.135.clone.1 | convolution fusion | flops 627569664 | bytes 40137728 | tf_op jit(solution)/shard_map/while/body/eval_jaxpr/bqhd,bkhd->bhqk/dot_general | solution.py:132
  613.7 13.8 %multiply_reduce_fusion.16 = (f32[6,512]{1,0:T(8,128)S(1)}, f32[6,512,1536]{2,1,0:T(8,128)}) fusion(f32[6,512,1536]{2,1,0:T(8,128)} %copy-done, f32[6,512]{1,0:T(8,128)S(1)} %dynamic-slice_bitcast_fusion.9, pred[512,1536]{1,0:T(8,128)(4,1)S(1)} %and_bitcast_fusion.15, bf16[2,1,1536,6,64]{2,4,3,1,0:T(8,128)(2,1)S(1)} %copy-done.22, s32[]{:T(128)S(6)} %copy.126, ...), kind=kOutput, calls=%fused_computation.135.clone.1 | convolution fusion | flops 627569664 | bytes 40137728 | tf_op jit(solution)/shard_map/while/body/eval_jaxpr/bqhd,bkhd->bhqk/dot_general | solution.py:132
  653.9 54.0 %while.128 = (s32[]{:T(128)}, f32[2,1,512,6,64]{2,4,3,1,0:T(8,128)}, f32[2,1,1024,6,64]{2,4,3,1,0:T(8,128)}, f32[2,1,1024,6,64]{2,4,3,1,0:T(8,128)}, bf16[2,1,10...) while((s32[]{:T(128)}, f32[2,1,512,6,64]{2,4,3,1,0:T(8,128)}, ...), condition=%wide.region_28.29_spmd.clone, body=%wide.region_26.28_spmd.clone.sunk | while | flops 2068378624 | bytes 148487488 | solution.py:300
  746.8 15.2 %multiply_convert_fusion.7 = bf16[768,2304]{1,0:T(8,128)(2,1)} fusion(bf16[2048,2304]{0,1:T(8,128)(2,1)} %bitcast.670, f32[768]{0:T(1024)S(1)} %copy-done.154, f32[2048]{0:T(1024)S(1)} %copy-done.121, f32[1,1024,768]{2,1,0:T(8,128)S(1)} %bitcast.656, bf16[1,2048,768]{2,1,0:T(8,128)(2,1)} %param.51, f32[2048]{0:T(1024)S(1)} %copy-done.119), kind=kOutput, calls=%fused_computation.269 | convolution fusion | flops 7260733440 | bytes 19287040 | tf_op jit(solution)/shard_map/rd,rc->dc/dot_general | solution.py:332
  762.0 15.4 %multiply_convert_fusion.5 = bf16[3072,768]{1,0:T(8,128)(2,1)} fusion(bf16[2048,3072]{1,0:T(8,128)(2,1)} %get-tuple-element.1216, bf16[1,2048,768]{2,1,0:T(8,128)(2,1)} %param.52), kind=kOutput, calls=%fused_computation.265 | convolution fusion | flops 9668395008 | bytes 20447232 | tf_op jit(solution)/shard_map/rf,rd->fd/dot_general | solution.py:272
  778.1 17.6 %multiply_convert_fusion.6 = bf16[768,3072]{1,0:T(8,128)(2,1)} fusion(bf16[2048,3072]{1,0:T(8,128)(2,1)} %get-tuple-element.1222, f32[1,2048,768]{2,1,0:T(8,128)} %copy-done.23, f32[768]{0:T(1024)S(1)} %copy-done.158, f32[2048]{0:T(1024)S(1)} %copy-done.156, f32[2048]{0:T(1024)S(1)} %copy-done.135), kind=kOutput, calls=%fused_computation.266 | convolution fusion | flops 9674686464 | bytes 23612416 | tf_op jit(solution)/shard_map/rd,rf->df/dot_general | solution.py:277
  832.6 14.5 %fusion.233 = (f32[2048]{0:T(1024)S(1)}, f32[2048,768]{1,0:T(8,128)S(1)}) fusion(f32[768]{0:T(1024)S(1)} %copy-done.154, f32[2048]{0:T(1024)S(1)} %copy-done.119, f32[1,1024,768]{2,1,0:T(8,128)S(1)} %bitcast.657, bf16[1,2048,768]{2,1,0:T(8,128)(2,1)} %param.51, bf16[2048,2304]{0,1:T(8,128)(2,1)} %bitcast.671, ...), kind=kOutput, calls=%fused_computation.283 | convolution fusion | flops 7257192448 | bytes 25578496 | tf_op jit(solution)/shard_map/rc,dc->rd/dot_general | solution.py:333
  861.9 53.1 %reduce-scatter.11.cloned.1.call-done = bf16[768,768]{1,0:T(8,128)(2,1)} async-done(((bf16[3072,768]{1,0:T(8,128)(2,1)}), bf16[768,768]{1,0:T(8,128)(2,1)}) %reduce-scatter.11.cloned.1.call-update) | async-done | bytes 1179664 | tf_op jit(solution)/shard_map/reduce_scatter | solution.py:363
  915.0 88.1 %reduce-scatter.9.cloned.1.call-done = bf16[192,3072]{1,0:T(8,128)(2,1)} async-done(((bf16[768,3072]{1,0:T(8,128)(2,1)}), bf16[192,3072]{1,0:T(8,128)(2,1)}) %reduce-scatter.9.cloned.1.call-update) | async-done | bytes 1179664 | tf_op jit(solution)/shard_map/reduce_scatter | solution.py:360
  1003.1 143.3 %all-reduce.16 = (f32[192,3072]{1,0:T(8,128)S(1)}, f32[192,2304]{1,0:T(8,128)}, f32[192,768]{1,0:T(8,128)S(1)}, f32[768,768]{1,0:T(8,128)}) all-reduce(bf16[192,3072]{1,0:T(8,128)(2,1)} %reduce-scatter.9.cloned.1.call-done, bf16[192,2304]{1,0:T(8,128)(2,1)} %reduce-scatter.5.cloned.1.call-done, ...), channel_id=1, replica_groups=mesh['wide'=8,'narrow'=4] {'wide'}, use_global_device_ids=true, to_apply=%region_47.48 | all-reduce | flops 1769472 | bytes 10616832 | tf_op jit(solution)/shard_map/psum | solution.py:368
  1161.2 16.4 %fusion.236 = bf16[1,2048,768]{2,1,0:T(8,128)(2,1)} fusion(f32[1,2048,768]{2,1,0:T(8,128)} %copy-done.23, bf16[2048,3072]{1,0:T(8,128)(2,1)} %get-tuple-element.1216, bf16[3072,768]{1,0:T(8,128)(2,1)} %all-gather.11.cloned.1.call-done, f32[768]{0:T(1024)S(1)} %copy-done.162), kind=kOutput, calls=%fused_computation.288 | convolution fusion | flops 9668395008 | bytes 26741760 | tf_op jit(solution)/shard_map/dot_general | solution.py:260
  1177.7 40.6 %all-reduce.9 = (f32[]{:T(128)}, f32[15,768]{1,0:T(8,128)S(1)}) all-reduce(f32[]{:T(128)S(6)} %add.797, f32[15,768]{1,0:T(8,128)S(1)} %copy-done.116), channel_id=1, replica_groups=mesh['wide'=8,'narrow'=4] {'narrow','wide'}, use_global_device_ids=true, to_apply=%region_52.53 | all-reduce | flops 11521 | bytes 92168 | tf_op jit(solution)/shard_map/psum | solution.py:383
  (690 shorter events, 613.8 us)
Async XLA Ops:
  7.2 88.8 %all-reduce.15.cloned.1.call-start = ((), (), s32[]{:S(2)}) async-start(), calls=%async_computation.12 | async-start | bytes 7077888 | tf_op jit(solution)/shard_map/psum | solution.py:30
  18.7 82.1 %copy-start.117 = (f32[15,768]{1,0:T(8,128)S(1)}, f32[15,768]{1,0:T(8,128)}, u32[]{:S(2)}) copy-start(f32[15,768]{1,0:T(8,128)} %param.59) | copy-start | bytes 138244
  18.7 89.8 %copy-start.163 = (s32[1,64]{1,0:T(1,128)S(1)}, s32[1,64]{1,0:T(1,128)}, u32[]{:S(2)}) copy-start(s32[1,64]{1,0:T(1,128)} %param.54) | copy-start | bytes 772
  18.7 148.9 %all-gather.5.cloned.1.call-start = ((), (), s32[]{:S(2)}) async-start(), calls=%async_computation.4 | async-start | bytes 4423680 | tf_op jit(solution)/shard_map/all_gather | solution.py:192
  96.0 241.3 %all-gather.7.cloned.1.call-start = ((), (), s32[]{:S(2)}) async-start(), calls=%async_computation.5 | async-start | bytes 1474560 | tf_op jit(solution)/shard_map/all_gather | solution.py:192
  96.7 250.5 %all-gather.9.cloned.1.call-start = ((), (), s32[]{:S(2)}) async-start(), calls=%async_computation.6 | async-start | bytes 5898240 | tf_op jit(solution)/shard_map/all_gather | solution.py:192
  97.3 280.3 %all-gather.11.cloned.1.call-start = ((), (), s32[]{:S(2)}) async-start(), calls=%async_computation.7 | async-start | bytes 5898240 | tf_op jit(solution)/shard_map/all_gather | solution.py:192
  108.5 64.9 %copy-start.153 = (f32[768]{0:T(1024)}, f32[768]{0:T(1024)S(1)}, u32[]{:S(2)}) copy-start(f32[768]{0:T(1024)S(1)} %get-tuple-element.870) | copy-start | bytes 9220
  109.0 64.4 %copy-start.6 = (f32[64,16,768]{2,1,0:T(8,128)}, f32[64,16,768]{2,1,0:T(8,128)S(1)}, u32[]{:S(2)}) copy-start(f32[64,16,768]{2,1,0:T(8,128)S(1)} %broadcast_in_dim.337) | copy-start | bytes 9437188
  114.6 69.9 %copy-start.120 = (f32[2048]{0:T(1024)}, f32[2048]{0:T(1024)S(1)}, u32[]{:S(2)}) copy-start(f32[2048]{0:T(1024)S(1)} %fusion.282) | copy-start | bytes 24580
  116.4 93.0 %copy-start.72 = (f32[2048,32]{0,1:T(8,128)}, f32[2048,32]{0,1:T(8,128)S(1)}, u32[]{:S(2)}) copy-start(f32[2048,32]{0,1:T(8,128)S(1)} %get-tuple-element.1203) | copy-start | bytes 786436
  116.4 745.4 %reduce-scatter.7.cloned.1.call-start = ((), (), s32[]{:S(2)}) async-start(), calls=%async_computation.9 | async-start | bytes 1474560 | tf_op jit(solution)/shard_map/reduce_scatter | solution.py:357
  343.8 84.0 %copy-start.134 = (f32[2048]{0:T(1024)}, f32[2048]{0:T(1024)S(1)}, u32[]{:S(2)}) copy-start(f32[2048]{0:T(1024)S(1)} %broadcast_multiply_fusion.5) | copy-start | bytes 24580
  347.2 80.5 %copy-start.155 = (f32[2048]{0:T(1024)}, f32[2048]{0:T(1024)S(1)}, u32[]{:S(2)}) copy-start(f32[2048]{0:T(1024)S(1)} %fusion.283) | copy-start | bytes 24580
  347.3 64.6 %slice-start = ((s8[6291456]{0:T(1024)(128)(4,1)}), s8[2097152]{0:T(1024)(128)(4,1)S(1)}, s32[]{:S(2)}) async-start(s8[6291456]{0:T(1024)(128)(4,1)} %bitcast.662), calls=%async_computation.13 | async-start | bytes 4194304
  474.1 387.8 %reduce-scatter.5.cloned.1.call-start = ((), (), s32[]{:S(2)}) async-start(), calls=%async_computation.8 | async-start | bytes 4423680 | tf_op jit(solution)/shard_map/reduce_scatter | solution.py:354
  479.7 61.7 %copy-start.2 = (bf16[2,1,1536,6,64]{2,4,3,1,0:T(8,128)(2,1)S(1)}, bf16[2,1,1536,6,64]{2,4,3,1,0:T(8,128)(2,1)}, u32[]{:S(2)}) copy-start(bf16[2,1,1536,6,64]{2,4,3,1,0:T(8,128)(2,1)} %get-tuple-element.2423) | copy-start | bytes 7077892
  479.7 61.7 %copy-start.80 = (s32[1536]{0:T(1024)S(1)}, s32[1536]{0:T(1024)}, u32[]{:S(2)}) copy-start(s32[1536]{0:T(1024)} %copy-done.79) | copy-start | bytes 18436
  479.7 61.7 %copy-start.82 = (s32[1536]{0:T(1024)S(1)}, s32[1536]{0:T(1024)}, u32[]{:S(2)}) copy-start(s32[1536]{0:T(1024)} %copy-done.81) | copy-start | bytes 18436
  479.7 61.7 %copy-start.94 = (f32[2,1,6,512,1]{3,2,4,1,0:T(8,128)S(1)}, f32[2,1,6,512,1]{3,2,4,1,0:T(8,128)}, u32[]{:S(2)}) copy-start(f32[2,1,6,512,1]{3,2,4,1,0:T(8,128)} %copy-done.93) | copy-start | bytes 73732
  479.7 61.7 %copy-start.98 = (s32[512]{0:T(512)S(1)}, s32[512]{0:T(512)}, u32[]{:S(2)}) copy-start(s32[512]{0:T(512)} %copy-done.97) | copy-start | bytes 6148
  479.7 61.7 %copy-start.102 = (s32[512]{0:T(512)S(1)}, s32[512]{0:T(512)}, u32[]{:S(2)}) copy-start(s32[512]{0:T(512)} %copy-done.101) | copy-start | bytes 6148
  762.0 153.0 %reduce-scatter.11.cloned.1.call-start = ((), (), s32[]{:S(2)}) async-start(), calls=%async_computation.11 | async-start | bytes 5898240 | tf_op jit(solution)/shard_map/reduce_scatter | solution.py:363
  777.5 225.7 %reduce-scatter.9.cloned.1.call-start = ((), (), s32[]{:S(2)}) async-start(), calls=%async_computation.10 | async-start | bytes 5898240 | tf_op jit(solution)/shard_map/reduce_scatter | solution.py:360
  (192 other events, 1787.8 us)
Sparse Core Ops, SparseCore 0:
  18.8 77.0 all-reduce.14
  97.5 70.0 all-gather.4
  169.2 29.0 all-gather.6
  199.7 88.5 all-gather.8
  289.7 87.8 all-gather.10
  474.2 27.6 reduce-scatter.6
  762.1 65.0 reduce-scatter.4
  829.5 85.5 reduce-scatter.10
  917.3 85.7 reduce-scatter.8
where the time goes:
time: 1280 us
  matrix products  389 us (30%)
  waiting for transfers between devices  276 us (22%)
  other arithmetic  235 us (18%)
  blocking collectives  184 us (14%)
  local copies, waits for them, and re-layouts  164 us (13%)
  between operations  24.4 us (2%)
    psum x1, blocking collectives, local(): lax.psum((narrow_shares[0], narrow_shares[1], narrow_shares[2], narrow_sh...  143 us
    reduce_scatter x1, waiting for transfers between devices, local(): lax.psum_scatter((up_grad * row_scale).astype(jnp.bfloat16), 'narrow', sc...  88.1 us
    psum x1, waiting for transfers between devices, spread(): return lax.psum(kept, axis)  77.2 us
    dot_general x8, matrix products, backward_group(): jnp.einsum('bqhd,bkhd->bhqk', grad_rows, value_block, preferred_element_t...  63 us
    convert_element_type x8, other arithmetic, backward_group(): score_grad = (probs * (prob_grad - row_dot)).astype(jnp.bfloat16)  58.6 us
    all_gather x4, waiting for transfers between devices, local(): lax.all_gather(shortened(shards), 'narrow', axis=0, tiled=True)  56.7 us
    reduce_scatter x1, waiting for transfers between devices, local(): lax.psum_scatter((down_grad * row_scale).astype(jnp.bfloat16), 'narrow',...  53.1 us
    psum x1, blocking collectives, local(): lax.psum((vec_local, square_local), ('narrow', 'wide'))  40.6 us
  transfers between devices with their start and end apart: 9, of which 5 were waited for; matrix products, arithmetic and copies ran while one was open for 44% of the time, Pallas kernels for 0%

commit v1 on v0

v1 whole, which is shorter than its diff:
```python
from functools import partial

import jax
import jax.numpy as jnp
from jax import lax
from jax.experimental import pallas as pl
from jax.experimental.pallas import tpu as pltpu
from jax.sharding import PartitionSpec as P

D = 768
HEADS = 12
HEAD_DIM = 64
FF = 3072
BLOCK = 16
SEQ = 1024
LEVELS = 8
STEP = 10
ROWS = 2 * SEQ

ln_eps = 1e-05
learn_rate = 0.05
vector_rate = 0.5
decay_rate = 0.1
moment_decay = 0.5
adam_eps = 1e-08
masked_score = -1e30
rope_base = 10000.0
row_scale = 1.0 / (2 * SEQ)

TILE = 256
PAIR = 2 * HEAD_DIM
GROUPS = HEADS // 2
UP_ROWS = FF // D
VROWS = 3 + UP_ROWS + LEVELS
low = jnp.bfloat16
full = jnp.float32


def dot(a, b, dim_a=1, dim_b=0):
    return lax.dot_general(
        a, b, (((dim_a,), (dim_b,)), ((), ())), preferred_element_type=full
    )


def params(limit=56):
    return pltpu.CompilerParams(vmem_limit_bytes=limit * 2**20)


def whole(shape):
    zeros = (0,) * len(shape)
    return pl.BlockSpec(shape, lambda *_: zeros, pipeline_mode=pl.Buffered(1))


def rows_of(width):
    return pl.BlockSpec((TILE, width), lambda i, *_: (i, 0))


def hidden_tile(levels_ref, tokens_ref, vec_ref):
    step = pl.program_id(0)
    per_tile = TILE // BLOCK
    first = lax.rem(step, SEQ // TILE) * per_tile
    rows = []
    for block in range(per_tile):
        level = levels_ref[first + block]
        row = vec_ref[pl.ds(3 + UP_ROWS + level, 1), :]
        rows.append(jnp.broadcast_to(row, (BLOCK, D)))
    embedding = jnp.concatenate(rows, axis=0)
    noised = step < SEQ // TILE
    return tokens_ref[...].astype(full) + jnp.where(noised, embedding, 0.0)


def normalised(entries):
    centred = entries - jnp.mean(entries, axis=-1, keepdims=True)
    scaling = lax.rsqrt(jnp.mean(centred * centred, axis=-1, keepdims=True) + ln_eps)
    return centred * scaling, scaling


def norm_back(normed, scaling, gain, grad):
    inner = grad * gain
    return (
        inner
        - jnp.mean(inner, axis=-1, keepdims=True)
        - normed * jnp.mean(inner * normed, axis=-1, keepdims=True)
    ) * scaling


def eight_rows(entries):
    return entries.reshape(-1, 8, entries.shape[-1]).sum(axis=0)


def norm_one_kernel(levels_ref, tokens_ref, vec_ref, out_ref):
    normed, _ = normalised(hidden_tile(levels_ref, tokens_ref, vec_ref))
    out_ref[...] = (normed * vec_ref[0:1, :]).astype(low)


def norm_one(levels, tokens, vec_master):
    return pl.pallas_call(
        norm_one_kernel,
        grid_spec=pltpu.PrefetchScalarGridSpec(
            num_scalar_prefetch=1,
            grid=(ROWS // TILE,),
            in_specs=[rows_of(D), whole((VROWS, D))],
            out_specs=rows_of(D),
        ),
        out_shape=jax.ShapeDtypeStruct((ROWS, D), low),
        cost_estimate=pl.CostEstimate(
            flops=10 * ROWS * D, bytes_accessed=4 * ROWS * D, transcendentals=0
        ),
        compiler_params=params(),
        name="norm_one",
    )(levels, tokens, vec_master)


def turn(entries, cos, sin):
    return entries * cos + pltpu.roll(entries, HEAD_DIM, 1) * sin


def project_kernel(a_ref, w_ref, cos_ref, sin_ref, out_ref):
    a = a_ref[...]
    cos = cos_ref[...]
    sin = sin_ref[...]
    for part in range(3):
        projected = dot(a, w_ref[:, part * D : (part + 1) * D])
        if part < 2:
            for group in range(GROUPS):
                columns = slice(group * PAIR, (group + 1) * PAIR)
                turned = turn(projected[:, columns], cos, sin).astype(low)
                if part == 0:
                    turned = (turned.astype(full) * HEAD_DIM**-0.5).astype(low)
                out_ref[:, part * D + group * PAIR : part * D + (group + 1) * PAIR] = turned
        else:
            out_ref[:, 2 * D :] = projected.astype(low)


def project(attn_in, w_qkv, cos, sin):
    table = pl.BlockSpec((TILE, PAIR), lambda i: (lax.rem(i, SEQ // TILE), 0))
    return pl.pallas_call(
        project_kernel,
        grid=(ROWS // TILE,),
        in_specs=[rows_of(D), whole((D, 3 * D)), table, table],
        out_specs=rows_of(3 * D),
        out_shape=jax.ShapeDtypeStruct((ROWS, 3 * D), low),
        cost_estimate=pl.CostEstimate(
            flops=6 * ROWS * D * D, bytes_accessed=8 * ROWS * D, transcendentals=0
        ),
        compiler_params=params(),
        name="project",
    )(attn_in, w_qkv, cos, sin)


QT = 256
TILES = SEQ // QT


def fill_bias(length, same_ref, earlier_ref, causal_ref, length_ref):
    key = lax.broadcasted_iota(jnp.int32, (QT, QT), 0)
    query = lax.broadcasted_iota(jnp.int32, (QT, QT), 1)
    key_block = key // BLOCK
    query_block = query // BLOCK
    for tile in range(TILES):
        kept = key + tile * QT < length
        own = kept | (key == query)
        same_ref[tile] = jnp.where((key_block == query_block) & own, 0.0, masked_score)
        earlier_ref[tile] = jnp.where((key_block < query_block) & kept, 0.0, masked_score)
        causal_ref[tile] = jnp.where((key_block <= query_block) & own, 0.0, masked_score)
    position = lax.broadcasted_iota(jnp.int32, (SEQ, QT), 0)
    length_ref[...] = jnp.where(position < length, 0.0, masked_score)


bias_scratch = [
    pltpu.VMEM((TILES, QT, QT), full),
    pltpu.VMEM((TILES, QT, QT), full),
    pltpu.VMEM((TILES, QT, QT), full),
    pltpu.VMEM((SEQ, QT), full),
]


def segments(tile, noised):
    found = []
    if noised:
        found.append((tile * QT, QT, "same"))
        found.append((SEQ + tile * QT, QT, "earlier"))
    else:
        found.append((SEQ + tile * QT, QT, "causal"))
    if tile > 1:
        found.append((SEQ + QT, (tile - 1) * QT, "length"))
    if tile > 0:
        found.append((SEQ, QT, None))
    return found


def masked(scores, kind, tile, start, count, biases):
    same_ref, earlier_ref, causal_ref, length_ref = biases
    if kind == "same":
        return scores + same_ref[tile]
    if kind == "earlier":
        return scores + earlier_ref[tile]
    if kind == "causal":
        return scores + causal_ref[tile]
    if kind == "length":
        return scores + length_ref[start - SEQ : start - SEQ + count, :]
    return scores


def lane_masks(head, rows):
    lane = lax.broadcasted_iota(jnp.int32, (rows, PAIR), 1)
    halves = (lane // (HEAD_DIM // 2)) % 2 == head
    plain = lane // HEAD_DIM == head
    return halves, plain


def attend_kernel(length_ref, q_ref, k_ref, v_ref, o_ref, log_ref, *biases):
    @pl.when(pl.program_id(0) == 0)
    def _():
        fill_bias(length_ref[0], *biases)

    def one_head(head, carry):
        halves, plain = lane_masks(head, QT)
        for tile in range(TILES):
            for noised in (True, False):
                row = tile * QT + (0 if noised else SEQ)
                query = jnp.where(halves, q_ref[row : row + QT, :], jnp.zeros((), low))
                parts = []
                row_max = None
                for start, count, kind in segments(tile, noised):
                    scores = dot(k_ref[start : start + count, :], query, 1, 1)
                    scores = masked(scores, kind, tile, start, count, biases)
                    parts.append((start, count, scores))
                    top = jnp.max(scores, axis=0, keepdims=True)
                    row_max = top if row_max is None else jnp.maximum(row_max, top)
                total = None
                attended = None
                for start, count, scores in parts:
                    expo = jnp.exp(scores - row_max)
                    part_total = jnp.sum(expo, axis=0, keepdims=True)
                    product = dot(expo.astype(low), v_ref[start : start + count, :], 0, 0)
                    total = part_total if total is None else total + part_total
                    attended = product if attended is None else attended + product
                inverse = jnp.transpose(jnp.broadcast_to(1.0 / total, (PAIR, QT)))
                result = (attended * inverse).astype(low)
                o_ref[row : row + QT, :] = jnp.where(plain, result, o_ref[row : row + QT, :])
                log_ref[0, pl.ds(head, 1), row : row + QT] = row_max + jnp.log(total)
        return carry

    lax.fori_loop(0, 2, one_head, 0)


def column_spec(offset):
    return pl.BlockSpec((ROWS, PAIR), lambda g, *_: (0, offset + g))


log_spec = pl.BlockSpec((1, 2, ROWS), lambda g, *_: (g, 0, 0))
PAIRS_SEEN = 1572864


def attend(length, qkv):
    return pl.pallas_call(
        attend_kernel,
        grid_spec=pltpu.PrefetchScalarGridSpec(
            num_scalar_prefetch=1,
            grid=(GROUPS,),
            in_specs=[column_spec(0), column_spec(GROUPS), column_spec(2 * GROUPS)],
            out_specs=[column_spec(0), log_spec],
            scratch_shapes=bias_scratch,
        ),
        out_shape=[
            jax.ShapeDtypeStruct((ROWS, D), low),
            jax.ShapeDtypeStruct((GROUPS, 2, ROWS), full),
        ],
        cost_estimate=pl.CostEstimate(
            flops=16 * PAIRS_SEEN * D, bytes_accessed=8 * ROWS * D, transcendentals=0
        ),
        compiler_params=params(),
        name="attend",
    )(length, qkv, qkv, qkv)


def attend_back_kernel(
    length_ref, q_ref, k_ref, v_ref, o_ref, grad_ref, log_ref, cos_ref, sin_ref,
    dq_ref, dk_ref, dv_ref, q_acc, k_acc, v_acc, delta_acc, *biases
):
    @pl.when(pl.program_id(0) == 0)
    def _():
        fill_bias(length_ref[0], *biases)

    k_acc[...] = jnp.zeros_like(k_acc)
    v_acc[...] = jnp.zeros_like(v_acc)
    for row in range(0, ROWS, QT):
        product = o_ref[row : row + QT, :].astype(full) * grad_ref[row : row + QT, :].astype(full)
        turned = jnp.transpose(product)
        delta_acc[0:1, row : row + QT] = jnp.sum(turned[:HEAD_DIM], axis=0, keepdims=True)
        delta_acc[1:2, row : row + QT] = jnp.sum(turned[HEAD_DIM:], axis=0, keepdims=True)

    def one_head(head, carry):
        halves, plain = lane_masks(head, QT)
        for tile in range(TILES):
            for noised in (True, False):
                row = tile * QT + (0 if noised else SEQ)
                zero = jnp.zeros((), low)
                query = jnp.where(halves, q_ref[row : row + QT, :], zero)
                grad = jnp.where(plain, grad_ref[row : row + QT, :], zero)
                log_total = log_ref[0, pl.ds(head, 1), row : row + QT]
                delta = delta_acc[pl.ds(head, 1), row : row + QT]
                query_grad = None
                for start, count, kind in segments(tile, noised):
                    keys = k_ref[start : start + count, :]
                    scores = dot(keys, query, 1, 1)
                    scores = masked(scores, kind, tile, start, count, biases)
                    probs = jnp.exp(scores - log_total)
                    prob_grad = dot(v_ref[start : start + count, :], grad, 1, 1)
                    score_grad = (probs * (prob_grad - delta)).astype(low)
                    v_acc[start : start + count, :] += dot(probs.astype(low), grad)
                    k_acc[start : start + count, :] += dot(score_grad, query)
                    part = dot(score_grad, keys, 0, 0)
                    query_grad = part if query_grad is None else query_grad + part
                q_acc[row : row + QT, :] = jnp.where(
                    halves, query_grad, q_acc[row : row + QT, :]
                )
        return carry

    lax.fori_loop(0, 2, one_head, 0)
    for row in range(0, ROWS, QT):
        rows = slice(row, row + QT)
        cos = cos_ref[row % SEQ : row % SEQ + QT, :]
        sin = -sin_ref[row % SEQ : row % SEQ + QT, :]
        dq_ref[rows, :] = turn(q_acc[rows, :] * HEAD_DIM**-0.5, cos, sin).astype(low)
        dk_ref[rows, :] = turn(k_acc[rows, :], cos, sin).astype(low)
        dv_ref[rows, :] = v_acc[rows, :].astype(low)


def attend_back(length, qkv, attended, grad, logs, cos, sin):
    table = whole((SEQ, PAIR))
    out = jax.ShapeDtypeStruct((ROWS, D), low)
    return pl.pallas_call(
        attend_back_kernel,
        grid_spec=pltpu.PrefetchScalarGridSpec(
            num_scalar_prefetch=1,
            grid=(GROUPS,),
            in_specs=[
                column_spec(0), column_spec(GROUPS), column_spec(2 * GROUPS),
                column_spec(0), column_spec(0), log_spec, table, table,
            ],
            out_specs=[column_spec(0)] * 3,
            scratch_shapes=[
                pltpu.VMEM((ROWS, PAIR), full),
                pltpu.VMEM((ROWS, PAIR), full),
                pltpu.VMEM((ROWS, PAIR), full),
                pltpu.VMEM((8, ROWS), full),
                *bias_scratch,
            ],
        ),
        out_shape=[out, out, out],
        cost_estimate=pl.CostEstimate(
            flops=40 * PAIRS_SEEN * D, bytes_accessed=16 * ROWS * D, transcendentals=0
        ),
        compiler_params=params(),
        name="attend_back",
    )(length, qkv, qkv, qkv, attended, grad, logs, cos, sin)


root_two_pi = 0.7978845608028654
cubic = 0.044715


def feed_kernel(
    levels_ref, tokens_ref, o_ref, dy_ref, vec_ref, out_w, up_w, down_w,
    y_ref, b_ref, gl_ref, du_ref, dr_ref, drb_ref, do_ref, sums_ref, upsum_ref
):
    @pl.when(pl.program_id(0) == 0)
    def _():
        sums_ref[...] = jnp.zeros_like(sums_ref)
        upsum_ref[...] = jnp.zeros_like(upsum_ref)

    gain = vec_ref[1:2, :]
    resid = hidden_tile(levels_ref, tokens_ref, vec_ref) + dot(o_ref[...], out_w[...])
    normed, scaling = normalised(resid)
    mlp_in = (normed * gain).astype(low)
    b_ref[...] = mlp_in
    dy = dy_ref[...]
    result = resid + vec_ref[2:3, :]
    back = jnp.zeros((TILE, D), full)
    for part in range(UP_ROWS):
        columns = slice(part * D, (part + 1) * D)
        pre = dot(mlp_in, up_w[:, columns]) + vec_ref[3 + part : 4 + part, :]
        square = pre * pre
        bent = jnp.tanh(root_two_pi * (pre + cubic * (pre * square)))
        half = 0.5 * (1.0 + bent)
        act = (pre * half).astype(low)
        slope = half + 0.5 * pre * (1.0 - bent * bent) * (
            root_two_pi + (3.0 * cubic * root_two_pi) * square
        )
        gl_ref[:, columns] = act
        result = result + dot(act, down_w[columns, :])
        pre_grad = dot(dy, down_w[columns, :], 1, 1) * slope
        upsum_ref[:, columns] += eight_rows(pre_grad)
        pre_low = pre_grad.astype(low)
        du_ref[:, columns] = pre_low
        back = back + dot(pre_low, up_w[:, columns], 1, 1)
    y_ref[...] = result.astype(low)
    dy_full = dy.astype(full)
    sums_ref[0:8, :] += eight_rows(back * normed)
    sums_ref[8:16, :] += eight_rows(dy_full)
    resid_grad = dy_full + norm_back(normed, scaling, gain, back)
    dr_ref[...] = resid_grad
    resid_low = resid_grad.astype(low)
    drb_ref[...] = resid_low
    do_ref[...] = dot(resid_low, out_w[...], 1, 1).astype(low)


def feed(levels, tokens, attended, cotangent, vec_master, w_out, w_up, w_down):
    def out(width, kind=low):
        return jax.ShapeDtypeStruct((ROWS, width), kind)

    return pl.pallas_call(
        feed_kernel,
        grid_spec=pltpu.PrefetchScalarGridSpec(
            num_scalar_prefetch=1,
            grid=(ROWS // TILE,),
            in_specs=[
                rows_of(D), rows_of(D), rows_of(D), whole((VROWS, D)),
                whole((D, D)), whole((D, FF)), whole((FF, D)),
            ],
            out_specs=[
                rows_of(D), rows_of(D), rows_of(FF), rows_of(FF), rows_of(D), rows_of(D),
                rows_of(D),
                pl.BlockSpec((16, D), lambda i, *_: (0, 0)),
                pl.BlockSpec((8, FF), lambda i, *_: (0, 0)),
            ],
        ),
        out_shape=[
            out(D), out(D), out(FF), out(FF), out(D, full), out(D), out(D),
            jax.ShapeDtypeStruct((16, D), full), jax.ShapeDtypeStruct((8, FF), full),
        ],
        cost_estimate=pl.CostEstimate(
            flops=ROWS * D * (4 * D + 8 * FF), bytes_accessed=30 * ROWS * D, transcendentals=0
        ),
        compiler_params=params(),
        name="feed",
    )(levels, tokens, attended, cotangent, vec_master, w_out, w_up, w_down)


def weight_kernel(x_ref, y_ref, out_ref):
    out_ref[...] = (dot(x_ref[...], y_ref[...], 0, 0) * row_scale).astype(low)


def weight_grad(x, y, block_x, block_y):
    wide_x, wide_y = x.shape[1], y.shape[1]
    return pl.pallas_call(
        weight_kernel,
        grid=(wide_x // block_x, wide_y // block_y),
        in_specs=[
            pl.BlockSpec((ROWS, block_x), lambda i, j: (0, i)),
            pl.BlockSpec((ROWS, block_y), lambda i, j: (0, j)),
        ],
        out_specs=pl.BlockSpec((block_x, block_y), lambda i, j: (i, j)),
        out_shape=jax.ShapeDtypeStruct((wide_x, wide_y), low),
        cost_estimate=pl.CostEstimate(
            flops=2 * ROWS * wide_x * wide_y,
            bytes_accessed=2 * ROWS * (wide_x + wide_y),
            transcendentals=0,
        ),
        compiler_params=params(),
        name="weight_grad",
    )(x, y)


def entry_kernel(
    levels_ref, tokens_ref, dr_ref, dq_ref, dk_ref, dv_ref, vec_ref, w_ref,
    grad_ref, gain_ref, table_ref
):
    step = pl.program_id(0)

    @pl.when(step == 0)
    def _():
        gain_ref[...] = jnp.zeros_like(gain_ref)
        table_ref[...] = jnp.zeros_like(table_ref)

    normed, scaling = normalised(hidden_tile(levels_ref, tokens_ref, vec_ref))
    back = dot(dq_ref[...], w_ref[:, :D], 1, 1)
    back = back + dot(dk_ref[...], w_ref[:, D : 2 * D], 1, 1)
    back = back + dot(dv_ref[...], w_ref[:, 2 * D :], 1, 1)
    gain_ref[...] += eight_rows(back * normed)
    result = dr_ref[...] + norm_back(normed, scaling, vec_ref[0:1, :], back)
    grad_ref[...] = result

    @pl.when(step < SEQ // TILE)
    def _():
        per_tile = TILE // BLOCK
        sums = result.reshape(per_tile, BLOCK, D).sum(axis=1)
        for block in range(per_tile):
            level = levels_ref[step * per_tile + block]
            table_ref[pl.ds(level, 1), :] += sums[block : block + 1, :]


def entry(levels, tokens, resid_grad, dq, dk, dv, vec_master, w_qkv):
    return pl.pallas_call(
        entry_kernel,
        grid_spec=pltpu.PrefetchScalarGridSpec(
            num_scalar_prefetch=1,
            grid=(ROWS // TILE,),
            in_specs=[rows_of(D)] * 5 + [whole((VROWS, D)), whole((D, 3 * D))],
            out_specs=[
                rows_of(D),
                pl.BlockSpec((8, D), lambda i, *_: (0, 0)),
                pl.BlockSpec((LEVELS, D), lambda i, *_: (0, 0)),
            ],
        ),
        out_shape=[
            jax.ShapeDtypeStruct((ROWS, D), full),
            jax.ShapeDtypeStruct((8, D), full),
            jax.ShapeDtypeStruct((LEVELS, D), full),
        ],
        cost_estimate=pl.CostEstimate(
            flops=6 * ROWS * D * D, bytes_accessed=20 * ROWS * D, transcendentals=0
        ),
        compiler_params=params(),
        name="entry",
    )(levels, tokens, resid_grad, dq, dk, dv, vec_master, w_qkv)


def turn_tables():
    positions = jnp.arange(SEQ, dtype=jnp.int32).astype(full)
    exponents = jnp.arange(HEAD_DIM // 2, dtype=full) * (2.0 / HEAD_DIM)
    angles = positions[:, None] * (rope_base ** (-exponents))[None, :]
    cos = jnp.cos(angles)
    sin = jnp.sin(angles)
    return (
        jnp.concatenate([cos, cos, cos, cos], axis=1),
        jnp.concatenate([-sin, -sin, sin, sin], axis=1),
    )


def swap_halves(matrix):
    rows = matrix.shape[0]
    pairs = matrix.reshape(rows, -1, 2, 2, HEAD_DIM // 2)
    return jnp.swapaxes(pairs, 2, 3).reshape(rows, -1)


def adam(grad, moment, square, master, decay, rate):
    moment_new = moment_decay * moment + (1.0 - moment_decay) * grad
    square_new = moment_decay * square + (1.0 - moment_decay) * grad * grad
    correction = 1.0 - moment_decay**STEP
    master_new = master * (1.0 - rate * decay) - rate * (moment_new / correction) / (
        jnp.sqrt(square_new / correction) + adam_eps
    )
    return (moment_new, square_new, master_new)


def spread(value, axis, source):
    kept = jnp.where(lax.axis_index(axis) == source, value, 0).astype(value.dtype)
    return lax.psum(kept, axis)


def shortened(value):

    def short(part):
        return part.astype(jnp.bfloat16) if part.dtype == jnp.float32 else part

    return jax.tree.map(short, value)


def local(
    tokens,
    cotangent,
    lengths,
    levels,
    owners,
    master_slots,
    moment_slots,
    square_slots,
    vec_master,
    vec_moment,
    vec_square,
):
    narrow_count = lax.axis_size("narrow")
    wide_count = lax.axis_size("wide")
    position = lax.axis_index("wide")
    slot_rows = master_slots.shape[1]
    shapes = ((D, 3 * D), (D, D), (D, FF), (FF, D))

    def share_of(slots, index_k):
        rows, cols = shapes[index_k]
        count = rows * cols // (narrow_count * D)
        return slots[0, :count].reshape(rows // narrow_count, cols)

    def owner_share(index_k):
        share = share_of(master_slots, index_k).astype(jnp.bfloat16)
        if index_k == 0:
            share = jnp.concatenate([swap_halves(share[:, : 2 * D]), share[:, 2 * D :]], axis=1)
        return spread(share, "wide", owners[index_k])

    shards = tuple((owner_share(index_k) for index_k in range(4)))
    w_qkv, w_out, w_up, w_down = lax.all_gather(shards, "narrow", axis=0, tiled=True)
    tokens = tokens.reshape(ROWS, D)
    cotangent = cotangent.reshape(ROWS, D)
    levels = levels.reshape(-1)
    cos, sin = turn_tables()
    attn_in = norm_one(levels, tokens, vec_master)
    qkv = project(attn_in, w_qkv, cos, sin)
    attended, logs = attend(lengths, qkv)
    output, mlp_in, act, pre_grad, resid_grad, resid_low, attended_grad, sums, up_sums = feed(
        levels, tokens, attended, cotangent, vec_master, w_out, w_up, w_down
    )
    down_grad = weight_grad(act, cotangent, 768, 768)
    up_grad = weight_grad(mlp_in, pre_grad, 768, 768)
    out_grad = weight_grad(attended, resid_low, 768, 384)
    dq, dk, dv = attend_back(lengths, qkv, attended, attended_grad, logs, cos, sin)
    q_grad = weight_grad(attn_in, dq, 768, 384)
    k_grad = weight_grad(attn_in, dk, 768, 384)
    v_grad = weight_grad(attn_in, dv, 768, 384)
    qkv_grad = jnp.concatenate([swap_halves(q_grad), swap_halves(k_grad), v_grad], axis=1)
    input_grad, gain_sums, table_grad = entry(
        levels, tokens, resid_grad, dq, dk, dv, vec_master, w_qkv
    )
    vec_local = (
        jnp.concatenate(
            [
                gain_sums.sum(axis=0)[None],
                sums[:8].sum(axis=0)[None],
                sums[8:].sum(axis=0)[None],
                up_sums.sum(axis=0).reshape(UP_ROWS, D),
                table_grad,
            ],
            axis=0,
        )
        * row_scale
    )
    narrow_shares = tuple(
        lax.psum_scatter(grad, "narrow", scatter_dimension=0, tiled=True).astype(full)
        for grad in (qkv_grad, out_grad, up_grad, down_grad)
    )
    summed = lax.psum(
        (narrow_shares[0], narrow_shares[1], narrow_shares[2], narrow_shares[3]), "wide"
    )
    pieces = tuple(
        (
            lax.dynamic_slice_in_dim(
                total.reshape(-1),
                position * (total.size // wide_count),
                total.size // wide_count,
                0,
            )
            for total in summed
        )
    )
    square_local = sum((jnp.sum(piece * piece) for piece in pieces))
    vec_total, square_total = lax.psum((vec_local, square_local), ("narrow", "wide"))
    norm_value = jnp.sqrt(square_total + jnp.sum(vec_total * vec_total))
    clip_factor = jnp.minimum(1.0, 1.0 / (norm_value + 1e-06))
    master_out = jnp.zeros((slot_rows, D), jnp.float32)
    moment_out = jnp.zeros((slot_rows, D), jnp.float32)
    square_out = jnp.zeros((slot_rows, D), jnp.float32)
    for index_k in range(4):
        clipped = summed[index_k] * clip_factor
        moment_new, square_new, master_new = adam(
            clipped,
            share_of(moment_slots, index_k),
            share_of(square_slots, index_k),
            share_of(master_slots, index_k),
            decay_rate,
            learn_rate,
        )
        is_owner = position == owners[index_k]
        count = master_new.size // D
        filler = jnp.zeros((slot_rows - count, D), jnp.float32)
        master_out = master_out + jnp.where(
            is_owner, jnp.concatenate([master_new.reshape(count, D), filler], axis=0), 0.0
        )
        moment_out = moment_out + jnp.where(
            is_owner, jnp.concatenate([moment_new.reshape(count, D), filler], axis=0), 0.0
        )
        square_out = square_out + jnp.where(
            is_owner, jnp.concatenate([square_new.reshape(count, D), filler], axis=0), 0.0
        )
    vec_clipped = vec_total * clip_factor
    vec_moment_new, vec_square_new, vec_master_new = adam(
        vec_clipped, vec_moment, vec_square, vec_master, 0.0, vector_rate
    )
    return (
        output[None],
        input_grad[None],
        master_out[None],
        moment_out[None],
        square_out[None],
        vec_clipped,
        vec_moment_new,
        vec_square_new,
        vec_master_new,
        norm_value.reshape(1),
    )


def solution(mesh):
    placed = (
        P(("wide", "narrow"), None, None),
        P(("wide", "narrow"), None, None),
        P(("wide", "narrow")),
        P(("wide", "narrow"), None),
        P(),
        P("wide", "narrow", None),
        P("wide", "narrow", None),
        P("wide", "narrow", None),
        P(),
        P(),
        P(),
    )
    return jax.shard_map(
        local,
        mesh=mesh,
        in_specs=placed,
        out_specs=(
            P(("wide", "narrow"), None, None),
            P(("wide", "narrow"), None, None),
            P("wide", "narrow", None),
            P("wide", "narrow", None),
            P("wide", "narrow", None),
            P(),
            P(),
            P(),
            P(),
            P(),
        ),
        check_vma=False,
    )
```

time: 1280 us -> 1090 us (0.85)
  matrix products: 389 us -> 0 us
  Pallas kernels: 0 us -> 308 us
  other arithmetic: 235 us -> 61.7 us
  waiting for transfers between devices: 276 us -> 437 us
  local copies, waits for them, and re-layouts: 164 us -> 65 us
    dot_general x70 -> x0, matrix products: 389 us -> none  [the longest x8 63 us: backward_group(): jnp.einsum('bqhd,bkhd->bhqk', grad_rows, value_block, preferred_element_t...]
    pallas_call x0 -> x12, Pallas kernels: none -> 308 us  [the longest x1 89.6 us: attend_back(): pl.pallas_call(attend_back_kernel, grid_spec=pltpu.PrefetchScalarGridSpec...]
    all_gather x4, waiting for transfers between devices: 56.7 us -> 199 us  [local(): lax.all_gather(shards, 'narrow', axis=0, tiled=True)]
    convert_element_type x11 -> x1, other arithmetic: 71.9 us -> 0.01 us  [turn_tables(): positions = jnp.arange(SEQ, dtype=jnp.int32).astype(full)]
    reduce_sum x15 -> x3, other arithmetic: 46 us -> 0.8 us  [the longest x1 0.75 us: local(): gain_sums.sum(axis=0)[None]]
    while x136 -> x0, local copies, waits for them, and re-layouts: 27.7 us -> none
    broadcast_in_dim x16 -> x0, other arithmetic: 27.4 us -> none  [the longest x8 13.7 us: forward_group(): scores = jnp.where(visible[:, None], scores, masked_score)]
    unnamed x282 -> x23, local copies, waits for them, and re-layouts: 30.7 us -> 5.17 us
  transfers between devices with their start and end apart: 9 -> 9, of which waited for: 5 -> 6; matrix products, arithmetic and copies ran while one was open for 44% -> 4% of each run, Pallas kernels for 0% -> 22%
where the time goes in v1:
time: 1090 us; the launch traced here: 1080 us
  waiting for transfers between devices  437 us (40%)
  Pallas kernels  308 us (28%)
  blocking collectives  184 us (17%)
  local copies, waits for them, and re-layouts  65 us (6%)
  other arithmetic  61.7 us (6%)
  between operations  22.9 us (2%)
    all_gather x4, waiting for transfers between devices, local(): lax.all_gather(shards, 'narrow', axis=0, tiled=True)  199 us
    reduce_scatter x4, waiting for transfers between devices, local(): lax.psum_scatter(grad, 'narrow', scatter_dimension=0, tiled=True)  159 us
    psum x1, blocking collectives, local(): lax.psum((narrow_shares[0], narrow_shares[1], narrow_shares[2], narrow_sh...  144 us
    pallas_call x1, Pallas kernels, attend_back(): pl.pallas_call(attend_back_kernel, grid_spec=pltpu.PrefetchScalarGridSpec...  89.6 us
    psum x1, waiting for transfers between devices, spread(): return lax.psum(kept, axis)  77.2 us
    pallas_call x1, Pallas kernels, feed(): pl.pallas_call(feed_kernel, grid_spec=pltpu.PrefetchScalarGridSpec(num_sc...  67.3 us
    pallas_call x6, Pallas kernels, weight_grad(): pl.pallas_call(weight_kernel, grid=(wide_x // block_x, wide_y // block_y)...  56.8 us
    pallas_call x1, Pallas kernels, attend(): pl.pallas_call(attend_kernel, grid_spec=pltpu.PrefetchScalarGridSpec(num_...  54.6 us
  transfers between devices with their start and end apart: 9, of which 6 were waited for; matrix products, arithmetic and copies ran while one was open for 4% of the time, Pallas kernels for 22%

profile of v1, /device:TPU:0, one launch (start us, length us, event | category | flops | bytes accessed | tf_op | source)
XLA Modules:
  0.0 1079.2 jit_solution(17936533842919775326)
XLA Ops:
  23.9 77.2 %all-reduce.12.cloned.1.call-done = (bf16[192,2304]{1,0:T(8,128)(2,1)}, bf16[192,768]{1,0:T(8,128)(2,1)}, bf16[192,3072]{1,0:T(8,128)(2,1)}, bf16[768,768]{1,0:T(8,128)(2,1)}) async-done(((bf16[192,2304]{1,0:T(8,128)(2,1)}, bf16[192,768]{1,0:T(8,128)(2,1)}, bf16[192,3072]{1,0:T(8,128)(2,1)}, bf16[768,768]{1,0:T(8,128)(2,1)}), (bf16[192,2304]{1,0:T(8,128)(2,1)}, bf16[192,768]{1,0:T(8,128)(2,1)}, ...) | async-done | bytes 3538960 | tf_op jit(solution)/shard_map/psum | solution.py:551
  103.7 7.8 norm_one.1.a_ref.x_ref
  115.2 57.5 %all-gather.5.cloned.1.call-done.w_ref = bf16[768,2304]{1,0:T(8,128)(2,1)} async-done(((bf16[192,2304]{1,0:T(8,128)(2,1)}), bf16[768,2304]{1,0:T(8,128)(2,1)}) %all-gather.5.cloned.1.call-update) | async-done | bytes 3538960 | tf_op jit(solution)/shard_map/all_gather | solution.py:593
  172.7 13.4 %project.1.q_ref.k_ref.v_ref = bf16[2048,2304]{1,0:T(8,128)(2,1)} custom-call(bf16[2048,768]{1,0:T(8,128)(2,1)} %norm_one.1.a_ref.x_ref, bf16[768,2304]{1,0:T(8,128)(2,1)} %all-gather.5.cloned.1.call-done.w_ref, f32[1024,128]{1,0:T(8,128)} %get-tuple-element.81.cos_ref, f32[1024,128]{1,0:T(8,128)} %get-tuple-element.82.sin_ref), custom_call_target="tpu_custom_call" | custom-call | flops 7247757312 | bytes 12582912 | tf_op jit(solution)/shard_map/project/pallas_call | solution.py:137
  186.2 54.6 %attend.1 = (bf16[2048,768]{1,0:T(8,128)(2,1)}, f32[6,2,2048]{2,1,0:T(2,128)}) custom-call(s32[1]{0:T(128)S(6)} %copy.56.length_ref, bf16[2048,2304]{1,0:T(8,128)(2,1)} %project.1.q_ref.k_ref.v_ref, bf16[2048,2304]{1,0:T(8,128)(2,1)} %project.1.q_ref.k_ref.v_ref, bf16[2048,2304]{1,0:T(8,128)(2,1)} %project.1.q_ref.k_ref.v_ref), custom_call_target="tpu_custom_call" | custom-call | flops 19327352832 | bytes 12582912 | tf_op jit(solution)/shard_map/attend/pallas_call | solution.py:257
  240.8 52.6 %all-gather.11.cloned.1.call-done.down_w = bf16[3072,768]{1,0:T(8,128)(2,1)} async-done(((bf16[768,768]{1,0:T(8,128)(2,1)}), bf16[3072,768]{1,0:T(8,128)(2,1)}) %all-gather.11.cloned.1.call-update) | async-done | bytes 4718608 | tf_op jit(solution)/shard_map/all_gather | solution.py:593
  293.4 89.3 %all-gather.9.cloned.1.call-done.up_w = bf16[768,3072]{1,0:T(8,128)(2,1)} async-done(((bf16[192,3072]{1,0:T(8,128)(2,1)}), bf16[768,3072]{1,0:T(8,128)(2,1)}) %all-gather.9.cloned.1.call-update) | async-done | bytes 4718608 | tf_op jit(solution)/shard_map/all_gather | solution.py:593
  382.7 67.3 %feed.1 = (bf16[2048,768]{1,0:T(8,128)(2,1)}, bf16[2048,768]{1,0:T(8,128)(2,1)}, bf16[2048,3072]{1,0:T(8,128)(2,1)}, bf16[2048,3072]{1,0:T(8,128)(2,1)}, f32[204...) custom-call(s32[64]{0:T(128)} %bitcast.74, ...), custom_call_target="tpu_custom_call" | custom-call | flops 43486543872 | bytes 47185920 | tf_op jit(solution)/shard_map/feed/pallas_call | solution.py:414
  450.0 6.9 weight_grad.9
  457.0 89.6 %attend_back.1 = (bf16[2048,768]{1,0:T(8,128)(2,1)}, bf16[2048,768]{1,0:T(8,128)(2,1)}, bf16[2048,768]{1,0:T(8,128)(2,1)}) custom-call(s32[1]{0:T(128)S(6)} %copy.56.length_ref, bf16[2048,2304]{1,0:T(8,128)(2,1)} %project.1.q_ref.k_ref.v_ref, bf16[2048,2304]{1,0:T(8,128)(2,1)} %project.1.q_ref.k_ref.v_ref, bf16[2048,2304]{1,0:T(8,128)(2,1)} %project.1.q_ref.k_ref.v_ref, ...), custom_call_target="tpu_custom_call" | custom-call | flops 48318382080 | bytes 25165824 | tf_op jit(solution)/shard_map/attend_back/pallas_call | solution.py:334
  546.6 6.9 weight_grad.6
  555.7 6.9 weight_grad.7
  564.9 7.1 weight_grad.8
  575.1 14.6 %weight_grad.10 = bf16[768,3072]{1,0:T(8,128)(2,1)} custom-call(bf16[2048,768]{1,0:T(8,128)(2,1)} %get-tuple-element.37.x_ref, bf16[2048,3072]{1,0:T(8,128)(2,1)} %get-tuple-element.38.y_ref), custom_call_target="tpu_custom_call" | custom-call | flops 9663676416 | bytes 15728640 | tf_op jit(solution)/shard_map/weight_grad/pallas_call | solution.py:448
  589.8 14.6 %weight_grad.11 = bf16[3072,768]{1,0:T(8,128)(2,1)} custom-call(bf16[2048,3072]{1,0:T(8,128)(2,1)} %get-tuple-element.39.x_ref, bf16[2048,768]{1,0:T(8,128)(2,1)} %bitcast.77), custom_call_target="tpu_custom_call" | custom-call | flops 9663676416 | bytes 15728640 | tf_op jit(solution)/shard_map/weight_grad/pallas_call | solution.py:448
  636.5 18.3 %entry.1 = (f32[2048,768]{1,0:T(8,128)}, f32[8,768]{1,0:T(8,128)}, f32[8,768]{1,0:T(8,128)}) custom-call(s32[64]{0:T(128)} %bitcast.75, bf16[2048,768]{1,0:T(8,128)(2,1)} %bitcast.69, f32[2048,768]{1,0:T(8,128)} %get-tuple-element.29.dr_ref, bf16[2048,768]{1,0:T(8,128)(2,1)} %get-tuple-element.32.dq_ref.y_ref, ...), custom_call_target="tpu_custom_call" | custom-call | flops 7247757312 | bytes 31457280 | tf_op jit(solution)/shard_map/entry/pallas_call | solution.py:496
  657.2 70.8 %reduce-scatter.9.cloned.1.call-done = bf16[192,3072]{1,0:T(8,128)(2,1)} async-done(((bf16[768,3072]{1,0:T(8,128)(2,1)}), bf16[192,3072]{1,0:T(8,128)(2,1)}) %reduce-scatter.9.cloned.1.call-update) | async-done | bytes 1179664 | tf_op jit(solution)/shard_map/reduce_scatter | solution.py:629
  728.0 88.1 %reduce-scatter.11.cloned.1.call-done = bf16[768,768]{1,0:T(8,128)(2,1)} async-done(((bf16[3072,768]{1,0:T(8,128)(2,1)}), bf16[768,768]{1,0:T(8,128)(2,1)}) %reduce-scatter.11.cloned.1.call-update) | async-done | bytes 1179664 | tf_op jit(solution)/shard_map/reduce_scatter | solution.py:629
  816.1 143.7 %all-reduce.13 = (f32[192,3072]{1,0:T(8,128)}, f32[192,2304]{1,0:T(8,128)}, f32[192,768]{1,0:T(8,128)S(1)}, f32[768,768]{1,0:T(8,128)}) all-reduce(bf16[192,3072]{1,0:T(8,128)(2,1)} %reduce-scatter.9.cloned.1.call-done, bf16[192,2304]{1,0:T(8,128)(2,1)} %reduce-scatter.5.cloned.1.call-done, ...), channel_id=1, replica_groups=mesh['wide'=8,'narrow'=4] {'wide'}, use_global_device_ids=true, to_apply=%region_11.12 | all-reduce | flops 1769472 | bytes 10616832 | tf_op jit(solution)/shard_map/psum | solution.py:632
  980.6 40.3 %all-reduce.6 = (f32[]{:T(128)}, f32[15,768]{1,0:T(8,128)S(1)}) all-reduce(f32[]{:T(128)S(6)} %add.157, f32[15,768]{1,0:T(8,128)S(1)} %copy-done.7), channel_id=1, replica_groups=mesh['wide'=8,'narrow'=4] {'narrow','wide'}, use_global_device_ids=true, to_apply=%region_16.17 | all-reduce | flops 11521 | bytes 92168 | tf_op jit(solution)/shard_map/psum | solution.py:647
  1025.7 5.1 divide_subtract_fusion
  1039.1 8.8 broadcast_select_fusion
  1054.9 3.5 select_n.149
  1060.0 11.1 %add_bitcast_fusion = (f32[1,768,768]{2,1,0:T(8,128)}, f32[1,768,768]{2,1,0:T(8,128)}, f32[1,768,768]{2,1,0:T(8,128)}) fusion(f32[768,768]{1,0:T(8,128)} %select_n.149, f32[192,768]{1,0:T(8,128)} %get-tuple-element.65, f32[576,768]{1,0:T(8,128)} %reshape.149, pred[]{:T(512)S(6)} %eq.19, pred[]{:T(512)S(6)} %eq.17, pred[]{:T(512)S(6)} %eq.16, ...), kind=kLoop, calls=%fused_computation.13 | loop fusion | flops 18284544 | bytes 30670856 | tf_op jit(solution)/shard_map/broadcast_in_dim | solution.py:684
  (104 shorter events, 100.4 us)
Async XLA Ops:
  7.2 93.9 %all-reduce.12.cloned.1.call-start = ((), (), s32[]{:S(2)}) async-start(), calls=%async_computation.12 | async-start | bytes 7077888 | tf_op jit(solution)/shard_map/psum | solution.py:551
  7.2 5.1 copy-start.10
  7.2 7.0 copy-start
  11.4 2.2 copy-start.4
  17.6 5.1 slice-start
  23.8 148.9 %all-gather.5.cloned.1.call-start = ((), (), s32[]{:S(2)}) async-start(), calls=%async_computation.4 | async-start | bytes 4423680 | tf_op jit(solution)/shard_map/all_gather | solution.py:593
  101.1 139.7 %all-gather.7.cloned.1.call-start = ((), (), s32[]{:S(2)}) async-start(), calls=%async_computation.5 | async-start | bytes 1474560 | tf_op jit(solution)/shard_map/all_gather | solution.py:593
  101.8 191.6 %all-gather.11.cloned.1.call-start = ((), (), s32[]{:S(2)}) async-start(), calls=%async_computation.7 | async-start | bytes 5898240 | tf_op jit(solution)/shard_map/all_gather | solution.py:593
  102.4 280.3 %all-gather.9.cloned.1.call-start = ((), (), s32[]{:S(2)}) async-start(), calls=%async_computation.6 | async-start | bytes 5898240 | tf_op jit(solution)/shard_map/all_gather | solution.py:593
  103.0 554.2 %reduce-scatter.7.cloned.1.call-start = ((), (), s32[]{:S(2)}) async-start(), calls=%async_computation.9 | async-start | bytes 1474560 | tf_op jit(solution)/shard_map/reduce_scatter | solution.py:629
  456.9 200.3 %reduce-scatter.5.cloned.1.call-start = ((), (), s32[]{:S(2)}) async-start(), calls=%async_computation.8 | async-start | bytes 4423680 | tf_op jit(solution)/shard_map/reduce_scatter | solution.py:629
  575.1 152.9 %reduce-scatter.9.cloned.1.call-start = ((), (), s32[]{:S(2)}) async-start(), calls=%async_computation.10 | async-start | bytes 5898240 | tf_op jit(solution)/shard_map/reduce_scatter | solution.py:629
  589.8 226.3 %reduce-scatter.11.cloned.1.call-start = ((), (), s32[]{:S(2)}) async-start(), calls=%async_computation.11 | async-start | bytes 5898240 | tf_op jit(solution)/shard_map/reduce_scatter | solution.py:629
  604.4 1.7 copy-start.1
  636.5 19.0 %copy-start.8 = (f32[8,3072]{1,0:T(8,128)S(1)}, f32[8,3072]{1,0:T(8,128)}, u32[]{:S(2)}) copy-start(f32[8,3072]{1,0:T(8,128)} %get-tuple-element.42) | copy-start | bytes 294916
  636.5 19.1 %copy-start.9 = (f32[16,768]{1,0:T(8,128)S(1)}, f32[16,768]{1,0:T(8,128)}, u32[]{:S(2)}) copy-start(f32[16,768]{1,0:T(8,128)} %get-tuple-element.41) | copy-start | bytes 147460
  977.2 3.4 copy-start.7
  1020.9 2.0 copy-start.6
  1022.9 2.8 copy-start.2
  1022.9 2.8 copy-start.3
  1054.9 5.1 copy-start.5
Sparse Core Ops, SparseCore 0:
  23.9 77.0 all-reduce.11
  102.6 70.0 all-gather.4
  174.3 29.0 all-gather.6
  204.8 88.5 all-gather.10
  294.8 87.8 all-gather.8
  457.0 27.6 reduce-scatter.6
  575.2 64.8 reduce-scatter.4
  642.4 85.5 reduce-scatter.8
  730.3 85.7 reduce-scatter.10

commit v2 on v1

v2 whole, which is shorter than its diff:
```python
from functools import partial

import jax
import jax.numpy as jnp
from jax import lax
from jax.experimental import pallas as pl
from jax.experimental.pallas import tpu as pltpu
from jax.sharding import PartitionSpec as P

D = 768
HEADS = 12
HEAD_DIM = 64
FF = 3072
BLOCK = 16
SEQ = 1024
LEVELS = 8
STEP = 10
ROWS = 2 * SEQ

ln_eps = 1e-05
learn_rate = 0.05
vector_rate = 0.5
decay_rate = 0.1
moment_decay = 0.5
adam_eps = 1e-08
masked_score = -1e30
rope_base = 10000.0
row_scale = 1.0 / (2 * SEQ)

TILE = 256
PAIR = 2 * HEAD_DIM
GROUPS = HEADS // 2
UP_ROWS = FF // D
VROWS = 3 + UP_ROWS + LEVELS
low = jnp.bfloat16
full = jnp.float32


def dot(a, b, dim_a=1, dim_b=0):
    return lax.dot_general(
        a, b, (((dim_a,), (dim_b,)), ((), ())), preferred_element_type=full
    )


def came_from(here, place, narrow):
    return lax.rem(here - place + narrow, narrow) if narrow > 1 else 0


anywhere = pl.BlockSpec(memory_space=pl.ANY)


def copies_in_order(source, target, here, semaphores):
    planes, narrow, _, rows, _ = source.shape
    found = []
    for place in range(narrow):
        for plane in range(planes):
            found.append(
                pltpu.make_async_copy(
                    source.at[plane, came_from(here, place, narrow)],
                    target.at[:, pl.ds((place * planes + plane) * rows, rows), :],
                    semaphores.at[place * planes + plane],
                )
            )
    return found


def bring(sources, targets, here, semaphores):
    found = []
    for index, (source, target) in enumerate(zip(sources, targets)):
        found += copies_in_order(source, target, here, semaphores.at[index])
    for copy in found:
        copy.start()
    for copy in found:
        copy.wait()


def ordered_shape(weight):
    planes, narrow, parts, rows, columns = weight.shape
    return (parts, planes * narrow * rows, columns)


def ordered_scratch(weights):
    return [pltpu.VMEM(ordered_shape(weight), low) for weight in weights] + [
        pltpu.SemaphoreType.DMA((len(weights), 16))
    ]


def side_by_side(ref, parts):
    return jnp.concatenate([ref[part] for part in parts], axis=1)


def params(limit=56):
    return pltpu.CompilerParams(vmem_limit_bytes=limit * 2**20)


def whole(shape):
    zeros = (0,) * len(shape)
    return pl.BlockSpec(shape, lambda *_: zeros, pipeline_mode=pl.Buffered(1))


def rows_of(width, rows=TILE):
    return pl.BlockSpec((rows, width), lambda i, *_: (i, 0))


def hidden_tile(levels_ref, tokens, vec_ref, sub=0, subs=1):
    count = tokens.shape[0]
    step = pl.program_id(0) * subs + sub
    per_tile = count // BLOCK
    first = lax.rem(step, SEQ // count) * per_tile
    rows = []
    for block in range(per_tile):
        level = levels_ref[first + block]
        row = vec_ref[pl.ds(3 + UP_ROWS + level, 1), :]
        rows.append(jnp.broadcast_to(row, (BLOCK, D)))
    embedding = jnp.concatenate(rows, axis=0)
    noised = step < SEQ // count
    return tokens.astype(full) + jnp.where(noised, embedding, 0.0)


def normalised(entries):
    centred = entries - jnp.mean(entries, axis=-1, keepdims=True)
    scaling = lax.rsqrt(jnp.mean(centred * centred, axis=-1, keepdims=True) + ln_eps)
    return centred * scaling, scaling


def norm_back(normed, scaling, gain, grad):
    inner = grad * gain
    return (
        inner
        - jnp.mean(inner, axis=-1, keepdims=True)
        - normed * jnp.mean(inner * normed, axis=-1, keepdims=True)
    ) * scaling


def eight_rows(entries):
    return entries.reshape(-1, 8, entries.shape[-1]).sum(axis=0)


def norm_one_kernel(levels_ref, tokens_ref, vec_ref, out_ref):
    normed, _ = normalised(hidden_tile(levels_ref, tokens_ref[...], vec_ref))
    out_ref[...] = (normed * vec_ref[0:1, :]).astype(low)


def norm_one(levels, tokens, vec_master):
    return pl.pallas_call(
        norm_one_kernel,
        grid_spec=pltpu.PrefetchScalarGridSpec(
            num_scalar_prefetch=1,
            grid=(ROWS // TILE,),
            in_specs=[rows_of(D), whole((VROWS, D))],
            out_specs=rows_of(D),
        ),
        out_shape=jax.ShapeDtypeStruct((ROWS, D), low),
        cost_estimate=pl.CostEstimate(
            flops=10 * ROWS * D, bytes_accessed=4 * ROWS * D, transcendentals=0
        ),
        compiler_params=params(),
        name="norm_one",
    )(levels, tokens, vec_master)


def turn(entries, cos, sin):
    return entries * cos + pltpu.roll(entries, HEAD_DIM, 1) * sin


PROJECT_TILE = 512


def project_kernel(pairs, place_ref, a_ref, w_hbm, cos_ref, sin_ref, out_ref, w_ref, semaphores):
    @pl.when(pl.program_id(0) == 0)
    def _():
        bring([w_hbm], [w_ref], place_ref[1], semaphores)

    weights = side_by_side(w_ref, range(3))
    for sub in range(PROJECT_TILE // TILE):
        rows = slice(sub * TILE, (sub + 1) * TILE)
        cos = cos_ref[rows, :]
        sin = sin_ref[rows, :]
        projected = dot(a_ref[rows, :], weights)
        for part in range(3):
            for pair in range(pairs):
                start = (part * pairs + pair) * PAIR
                columns = slice(start, start + PAIR)
                result = projected[:, columns]
                if part < 2:
                    result = turn(result, cos, sin).astype(low)
                if part == 0:
                    result = result.astype(full) * HEAD_DIM**-0.5
                out_ref[rows, columns] = result.astype(low)


def project(places, attn_in, w_part, cos, sin):
    width = 3 * w_part.shape[4]
    table = pl.BlockSpec(
        (PROJECT_TILE, PAIR), lambda i, *_: (lax.rem(i, SEQ // PROJECT_TILE), 0)
    )
    return pl.pallas_call(
        partial(project_kernel, width // (3 * PAIR)),
        grid_spec=pltpu.PrefetchScalarGridSpec(
            num_scalar_prefetch=1,
            grid=(ROWS // PROJECT_TILE,),
            in_specs=[rows_of(D, PROJECT_TILE), anywhere, table, table],
            out_specs=rows_of(width, PROJECT_TILE),
            scratch_shapes=ordered_scratch([w_part]),
        ),
        out_shape=jax.ShapeDtypeStruct((ROWS, width), low),
        cost_estimate=pl.CostEstimate(
            flops=2 * ROWS * D * width, bytes_accessed=8 * ROWS * D, transcendentals=0
        ),
        compiler_params=params(),
        name="project",
    )(places, attn_in, w_part, cos, sin)


QT = 256
TILES = SEQ // QT
SHORTEST = 256


def fill_bias(length, same_ref, earlier_ref, causal_ref, length_ref):
    key = lax.broadcasted_iota(jnp.int32, (QT, QT), 0)
    query = lax.broadcasted_iota(jnp.int32, (QT, QT), 1)
    key_block = key // BLOCK
    query_block = query // BLOCK
    for tile in range(TILES):
        kept = key + tile * QT < length
        own = kept | (key == query)
        same_ref[tile] = jnp.where((key_block == query_block) & own, 0.0, masked_score)
        earlier_ref[tile] = jnp.where((key_block < query_block) & kept, 0.0, masked_score)
        causal_ref[tile] = jnp.where((key_block <= query_block) & own, 0.0, masked_score)
    position = lax.broadcasted_iota(jnp.int32, (SEQ, QT), 0)
    length_ref[...] = jnp.where(position < length, 0.0, masked_score)


bias_scratch = [
    pltpu.VMEM((TILES, QT, QT), full),
    pltpu.VMEM((TILES, QT, QT), full),
    pltpu.VMEM((TILES, QT, QT), full),
    pltpu.VMEM((SEQ, QT), full),
]


def segments(tile, noised):
    found = []
    if noised:
        found.append((tile * QT, QT, "same"))
        found.append((SEQ + tile * QT, QT, "earlier"))
    else:
        found.append((SEQ + tile * QT, QT, "causal"))
    before = tile * QT
    free = min(before, SHORTEST)
    if before > free:
        found.append((SEQ + free, before - free, "length"))
    if free > 0:
        found.append((SEQ, free, None))
    return found


def masked(scores, kind, tile, start, count, biases):
    same_ref, earlier_ref, causal_ref, length_ref = biases
    if kind == "same":
        return scores + same_ref[tile]
    if kind == "earlier":
        return scores + earlier_ref[tile]
    if kind == "causal":
        return scores + causal_ref[tile]
    if kind == "length":
        return scores + length_ref[start - SEQ : start - SEQ + count, :]
    return scores


def lane_masks(head, rows):
    lane = lax.broadcasted_iota(jnp.int32, (rows, PAIR), 1)
    halves = (lane // (HEAD_DIM // 2)) % 2 == head
    plain = lane // HEAD_DIM == head
    return halves, plain


def attend_kernel(aliased, scalar_ref, q_ref, k_ref, v_ref, *refs):
    o_ref, log_ref, *biases = refs[2:] if aliased else refs

    @pl.when(pl.program_id(0) == 0)
    def _():
        fill_bias(scalar_ref[0], *biases)

    units = [
        (head, tile, noised)
        for head in range(2)
        for tile in range(TILES)
        for noised in (True, False)
    ]

    def score(head, tile, noised):
        halves, _ = lane_masks(head, QT)
        row = tile * QT + (0 if noised else SEQ)
        query = jnp.where(halves, q_ref[row : row + QT, :], jnp.zeros((), low))
        parts = []
        for start, count, kind in segments(tile, noised):
            scores = dot(k_ref[start : start + count, :], query, 1, 1)
            parts.append((start, count, masked(scores, kind, tile, start, count, biases)))
        return parts

    def weigh(head, tile, noised, parts):
        row = tile * QT + (0 if noised else SEQ)
        row_max = None
        for start, count, scores in parts:
            top = jnp.max(scores, axis=0, keepdims=True)
            row_max = top if row_max is None else jnp.maximum(row_max, top)
        total = None
        weights = []
        for start, count, scores in parts:
            expo = jnp.exp(scores - row_max)
            part_total = jnp.sum(expo, axis=0, keepdims=True)
            total = part_total if total is None else total + part_total
            weights.append((start, count, expo.astype(low)))
        log_ref[0, head : head + 1, row : row + QT] = row_max + jnp.log(total)
        return weights, total

    def finish(head, tile, noised, weights, total):
        _, plain = lane_masks(head, QT)
        row = tile * QT + (0 if noised else SEQ)
        attended = None
        for start, count, expo in weights:
            product = dot(expo, v_ref[start : start + count, :], 0, 0)
            attended = product if attended is None else attended + product
        inverse = jnp.transpose(jnp.broadcast_to(1.0 / total, (PAIR, QT)))
        result = (attended * inverse).astype(low)
        o_ref[row : row + QT, :] = jnp.where(plain, result, o_ref[row : row + QT, :])

    parts = score(*units[0])
    held = None
    for index, unit in enumerate(units):
        following = score(*units[index + 1]) if index + 1 < len(units) else None
        weights = weigh(*unit, parts)
        if held is not None:
            finish(*held)
        held = (*unit, *weights)
        parts = following
    finish(*held)


def column_spec(offset):
    return pl.BlockSpec((ROWS, PAIR), lambda g, *_: (0, offset + g))


pair_spec = pl.BlockSpec((ROWS, PAIR), lambda g, scalars: (0, scalars[1] + g))
log_spec = pl.BlockSpec((1, 2, ROWS), lambda g, scalars: (scalars[1] + g, 0, 0))
PAIRS_SEEN = 1572864


def attend(scalars, qkv, before):
    pairs = qkv.shape[1] // (3 * PAIR)
    aliased = before is not None
    kept = [pl.BlockSpec(memory_space=pl.ANY)] * 2 if aliased else []
    return pl.pallas_call(
        partial(attend_kernel, aliased),
        grid_spec=pltpu.PrefetchScalarGridSpec(
            num_scalar_prefetch=1,
            grid=(pairs,),
            in_specs=[column_spec(0), column_spec(pairs), column_spec(2 * pairs), *kept],
            out_specs=[pair_spec, log_spec],
            scratch_shapes=bias_scratch,
        ),
        out_shape=[
            jax.ShapeDtypeStruct((ROWS, D), low),
            jax.ShapeDtypeStruct((GROUPS, 2, ROWS), full),
        ],
        input_output_aliases={4: 0, 5: 1} if aliased else {},
        cost_estimate=pl.CostEstimate(
            flops=16 * PAIRS_SEEN * PAIR * pairs,
            bytes_accessed=8 * ROWS * PAIR * pairs,
            transcendentals=0,
        ),
        compiler_params=params(),
        name="attend",
    )(scalars, qkv, qkv, qkv, *(before or ()))


def attend_back_kernel(
    scalar_ref, q_ref, k_ref, v_ref, o_ref, grad_ref, log_ref, cos_ref, sin_ref,
    grad_out_ref, q_acc, k_acc, v_acc, delta_acc, prob_ref, score_ref, own_prob_ref,
    own_score_ref, *biases
):
    @pl.when(pl.program_id(0) == 0)
    def _():
        fill_bias(scalar_ref[0], *biases)

    for row in range(0, ROWS, QT):
        product = o_ref[row : row + QT, :].astype(full) * grad_ref[row : row + QT, :].astype(full)
        turned = jnp.transpose(product)
        delta_acc[0:1, row : row + QT] = jnp.sum(turned[:HEAD_DIM], axis=0, keepdims=True)
        delta_acc[1:2, row : row + QT] = jnp.sum(turned[HEAD_DIM:], axis=0, keepdims=True)

    def products(head, tile, noised, start, count):
        halves, plain = lane_masks(head, QT)
        row = tile * QT + (0 if noised else SEQ)
        zero = jnp.zeros((), low)
        query = jnp.where(halves, q_ref[row : row + QT, :], zero)
        grad = jnp.where(plain, grad_ref[row : row + QT, :], zero)
        scores = dot(k_ref[start : start + count, :], query, 1, 1)
        return scores, dot(v_ref[start : start + count, :], grad, 1, 1)

    def keep(head, tile, noised, start, count, kind, pair):
        row = tile * QT + (0 if noised else SEQ)
        scores, prob_grad = pair
        scores = masked(scores, kind, tile, start, count, biases)
        probs = jnp.exp(scores - log_ref[0, head : head + 1, row : row + QT])
        delta = delta_acc[head : head + 1, row : row + QT]
        score_grad = (probs * (prob_grad - delta)).astype(low)
        if kind == "same":
            own_prob_ref[start : start + count, :] = probs.astype(low)
            own_score_ref[start : start + count, :] = score_grad
        else:
            key = start - SEQ
            prob_ref[key : key + count, row : row + QT] = probs.astype(low)
            score_ref[key : key + count, row : row + QT] = score_grad

    def put(ref, row, mask, value):
        ref[row : row + QT, :] = jnp.where(mask, value, ref[row : row + QT, :])

    def sums(head, tile):
        halves, plain = lane_masks(head, QT)
        row = tile * QT
        rows, clean_rows = slice(row, row + QT), slice(SEQ + row, SEQ + row + QT)
        seen = (slice(row, SEQ), slice(SEQ + row, ROWS))
        put(v_acc, row, plain, dot(own_prob_ref[rows, :], grad_ref[rows, :]))
        put(k_acc, row, halves, dot(own_score_ref[rows, :], q_ref[rows, :]))
        put(
            v_acc, SEQ + row, plain,
            dot(prob_ref[rows, seen[0]], grad_ref[seen[0], :])
            + dot(prob_ref[rows, seen[1]], grad_ref[seen[1], :]),
        )
        put(
            k_acc, SEQ + row, halves,
            dot(score_ref[rows, seen[0]], q_ref[seen[0], :])
            + dot(score_ref[rows, seen[1]], q_ref[seen[1], :]),
        )
        keys = k_ref[SEQ : SEQ + row + QT, :]
        put(
            q_acc, row, halves,
            dot(score_ref[: row + QT, rows], keys, 0, 0)
            + dot(own_score_ref[rows, :], k_ref[rows, :], 0, 0),
        )
        put(q_acc, SEQ + row, halves, dot(score_ref[: row + QT, clean_rows], keys, 0, 0))

    items = []
    for head in range(2):
        for tile in reversed(range(TILES)):
            for noised in (True, False):
                for start, count, kind in segments(tile, noised):
                    items.append((head, tile, noised, start, count, kind))
    waiting = []
    pair = products(*items[0][:5])
    for index, item in enumerate(items):
        following = None
        if index + 1 < len(items):
            following = products(*items[index + 1][:5])
        keep(*item, pair)
        pair = following
        if index + 1 == len(items) or items[index + 1][:2] != item[:2]:
            sums(*item[:2])
    for row in range(0, ROWS, QT):
        rows = slice(row, row + QT)
        cos = cos_ref[row % SEQ : row % SEQ + QT, :]
        sin = -sin_ref[row % SEQ : row % SEQ + QT, :]
        grad_out_ref[0, rows, :] = turn(q_acc[rows, :] * HEAD_DIM**-0.5, cos, sin).astype(low)
        grad_out_ref[1, rows, :] = turn(k_acc[rows, :], cos, sin).astype(low)
        grad_out_ref[2, rows, :] = v_acc[rows, :].astype(low)


def attend_back(scalars, qkv, attended, grad, logs, cos, sin):
    pairs = qkv.shape[1] // (3 * PAIR)
    table = whole((SEQ, PAIR))
    return pl.pallas_call(
        attend_back_kernel,
        grid_spec=pltpu.PrefetchScalarGridSpec(
            num_scalar_prefetch=1,
            grid=(pairs,),
            in_specs=[
                column_spec(0), column_spec(pairs), column_spec(2 * pairs),
                pair_spec, pair_spec, log_spec, table, table,
            ],
            out_specs=pl.BlockSpec((3, ROWS, PAIR), lambda g, *_: (0, 0, g)),
            scratch_shapes=[
                pltpu.VMEM((ROWS, PAIR), full),
                pltpu.VMEM((ROWS, PAIR), full),
                pltpu.VMEM((ROWS, PAIR), full),
                pltpu.VMEM((8, ROWS), full),
                pltpu.VMEM((SEQ, ROWS), low),
                pltpu.VMEM((SEQ, ROWS), low),
                pltpu.VMEM((SEQ, QT), low),
                pltpu.VMEM((SEQ, QT), low),
                *bias_scratch,
            ],
        ),
        out_shape=jax.ShapeDtypeStruct((3, ROWS, pairs * PAIR), low),
        cost_estimate=pl.CostEstimate(
            flops=40 * PAIRS_SEEN * PAIR * pairs,
            bytes_accessed=16 * ROWS * PAIR * pairs,
            transcendentals=0,
        ),
        compiler_params=params(),
        name="attend_back",
    )(scalars, qkv, qkv, qkv, attended, grad, logs, cos, sin)


root_two_pi = 0.7978845608028654
cubic = 0.044715


HALF = D // 2
FF_HALF = FF // 2


FEED_TILE = 512
SUB = 256


def feed_kernel(
    levels_ref, side_ref, tokens_ref, o_ref, dy_ref, vec_ref, bias_ref,
    wide_mine_hbm, wide_other_hbm, down_mine_hbm, down_other_hbm,
    y_ref, b_ref, gl_ref, du_ref, dr_ref, drb_ref, do_ref, sums_ref, upsum_ref,
    wide_mine, wide_other, down_mine, down_other, semaphores
):
    @pl.when(pl.program_id(0) == 0)
    def _():
        sums_ref[...] = jnp.zeros_like(sums_ref)
        upsum_ref[...] = jnp.zeros_like(upsum_ref)
        bring(
            [wide_mine_hbm, wide_other_hbm, down_mine_hbm, down_other_hbm],
            [wide_mine, wide_other, down_mine, down_other],
            side_ref[1],
            semaphores,
        )

    swapped = side_ref[0] == 1
    gain = vec_ref[1:2, :]
    subs = FEED_TILE // SUB

    def in_order(mine, other):
        return jnp.concatenate(
            [jnp.where(swapped, other, mine), jnp.where(swapped, mine, other)], axis=1
        )

    def weights(part):
        wide_ref, down_ref = (wide_mine, down_mine) if part < 2 else (wide_other, down_other)
        inner = part % 2
        up = side_by_side(wide_ref, (inner * 2, inner * 2 + 1))
        return up, down_ref[0, inner * D : (inner + 1) * D, :]

    def head(sub):
        rows = slice(sub * SUB, (sub + 1) * SUB)
        attended = o_ref[rows, :]
        hidden = hidden_tile(levels_ref, tokens_ref[rows, :], vec_ref, sub, subs)
        resid = hidden + in_order(
            dot(attended, wide_mine[UP_ROWS]), dot(attended, wide_other[UP_ROWS])
        )
        normed, scaling = normalised(resid)
        mlp_in = (normed * gain).astype(low)
        b_ref[rows, :] = mlp_in
        return normed, scaling, mlp_in, resid + vec_ref[2:3, :]

    def products(sub, part, mlp_in):
        up, down = weights(part)
        rows = slice(sub * SUB, (sub + 1) * SUB)
        columns = slice(part * D, (part + 1) * D)
        return dot(mlp_in, up) + bias_ref[:, columns], dot(dy_ref[rows, :], down, 1, 1)

    def bend(sub, part, pre, act_grad):
        rows = slice(sub * SUB, (sub + 1) * SUB)
        columns = slice(part * D, (part + 1) * D)
        square = pre * pre
        bent = jnp.tanh(pre * (root_two_pi + (cubic * root_two_pi) * square))
        half = 0.5 + 0.5 * bent
        act = (pre * half).astype(low)
        slope = half + (0.5 * pre) * (1.0 - bent * bent) * (
            root_two_pi + (3.0 * cubic * root_two_pi) * square
        )
        pre_grad = act_grad * slope
        pre_low = pre_grad.astype(low)
        gl_ref[rows, columns] = act
        du_ref[rows, columns] = pre_low
        upsum_ref[:, columns] += eight_rows(pre_grad)
        return act, pre_low

    def main(sub, mlp_in, result):
        back = None
        ahead = products(sub, 0, mlp_in)
        for part in range(UP_ROWS):
            pair = ahead
            if part + 1 < UP_ROWS:
                ahead = products(sub, part + 1, mlp_in)
            act, pre_low = bend(sub, part, *pair)
            up, down = weights(part)
            result = result + dot(act, down)
            term = dot(pre_low, up, 1, 1)
            back = term if back is None else back + term
        return result, back

    def tail(sub, normed, scaling, result, back):
        rows = slice(sub * SUB, (sub + 1) * SUB)
        y_ref[rows, :] = result.astype(low)
        dy_full = dy_ref[rows, :].astype(full)
        sums_ref[0:8, :] += eight_rows(back * normed)
        sums_ref[8:16, :] += eight_rows(dy_full)
        resid_grad = dy_full + norm_back(normed, scaling, gain, back)
        dr_ref[rows, :] = resid_grad
        drb_ref[rows, :] = resid_grad.astype(low)
        first, second = resid_grad[:, :HALF], resid_grad[:, HALF:]
        mine = jnp.where(swapped, second, first).astype(low)
        other = jnp.where(swapped, first, second).astype(low)
        do_ref[rows, :] = (
            dot(mine, wide_mine[UP_ROWS], 1, 1) + dot(other, wide_other[UP_ROWS], 1, 1)
        ).astype(low)

    state = head(0)
    for sub in range(subs):
        normed, scaling, mlp_in, result = state
        result, back = main(sub, mlp_in, result)
        if sub + 1 < subs:
            state = head(sub + 1)
        tail(sub, normed, scaling, result, back)


def feed(levels, side, tokens, attended, cotangent, vec_master, bias, weights):
    def out(width, kind=low):
        return jax.ShapeDtypeStruct((ROWS, width), kind)

    def rows(width):
        return rows_of(width, FEED_TILE)

    return pl.pallas_call(
        feed_kernel,
        grid_spec=pltpu.PrefetchScalarGridSpec(
            num_scalar_prefetch=2,
            grid=(ROWS // FEED_TILE,),
            in_specs=[
                rows(D), rows(D), rows(D), whole((VROWS, D)), whole((1, FF)), *[anywhere] * 4
            ],
            out_specs=[
                rows(D), rows(D), rows(FF), rows(FF), rows(D), rows(D), rows(D),
                pl.BlockSpec((16, D), lambda i, *_: (0, 0)),
                pl.BlockSpec((8, FF), lambda i, *_: (0, 0)),
            ],
            scratch_shapes=ordered_scratch(weights),
        ),
        out_shape=[
            out(D), out(D), out(FF), out(FF), out(D, full), out(D), out(D),
            jax.ShapeDtypeStruct((16, D), full), jax.ShapeDtypeStruct((8, FF), full),
        ],
        cost_estimate=pl.CostEstimate(
            flops=ROWS * D * (4 * D + 8 * FF), bytes_accessed=30 * ROWS * D, transcendentals=0
        ),
        compiler_params=params(),
        name="feed",
    )(levels, side, tokens, attended, cotangent, vec_master, bias, *weights)


def weight_kernel(added, scalar_ref, x_ref, y_ref, *refs):
    out_ref = refs[-1]
    result = dot(x_ref[...], y_ref[...], 0, 0) * row_scale
    planes, narrow, _, rows, _ = out_ref.shape
    for place in range(narrow):
        for plane in range(planes):
            start = (place * planes + plane) * rows
            block = result[start : start + rows]
            if added:
                block = block + refs[0][plane, place, 0].astype(full)
            out_ref[plane, place, 0] = block.astype(low)


def weight_call(name, count, x_spec, y_spec, out_spec, shape, first, x, y, added):
    return pl.pallas_call(
        partial(weight_kernel, added is not None),
        grid_spec=pltpu.PrefetchScalarGridSpec(
            num_scalar_prefetch=1,
            grid=(count,),
            in_specs=[x_spec, y_spec, *([out_spec] if added is not None else [])],
            out_specs=out_spec,
        ),
        out_shape=jax.ShapeDtypeStruct(shape, low),
        cost_estimate=pl.CostEstimate(
            flops=4 * ROWS * count * D * HALF, bytes_accessed=8 * ROWS * D, transcendentals=0
        ),
        compiler_params=params(),
        name=name,
    )(jnp.asarray(first, jnp.int32).reshape(1), x, y, *([added] if added is not None else []))


def grad_of_columns(blocks, x, y, first, count, added=None):
    planes, narrow = blocks
    rows = D // (planes * narrow)
    if y.ndim == 3:
        y_spec = pl.BlockSpec((None, ROWS, HALF), lambda j, s: (s[0] + j, 0, 0))
    else:
        y_spec = pl.BlockSpec((ROWS, HALF), lambda j, s: (0, s[0] + j))
    return weight_call(
        "grad_of_columns",
        count,
        pl.BlockSpec((ROWS, D), lambda j, s: (0, 0)),
        y_spec,
        pl.BlockSpec((planes, narrow, 1, rows, HALF), lambda j, s: (0, 0, j, 0, 0)),
        (planes, narrow, count, rows, HALF),
        first, x, y, added,
    )


def wide_kernel(added, side_ref, x_ref, y_ref, o_hbm, dr_hbm, *refs):
    out_ref, o_ref, dr_ref, semaphores = refs[-4:]
    step = pl.program_id(0)
    column = pl.multiple_of(side_ref[1] * HALF, HALF)
    copies = [
        pltpu.make_async_copy(o_hbm, o_ref, semaphores.at[0]),
        pltpu.make_async_copy(dr_hbm.at[:, pl.ds(column, HALF)], dr_ref, semaphores.at[1]),
    ]

    def store(result):
        planes, narrow, _, rows, _ = out_ref.shape
        for place in range(narrow):
            for plane in range(planes):
                start = (place * planes + plane) * rows
                block = result[start : start + rows] * row_scale
                if added:
                    block = block + refs[0][plane, place, 0].astype(full)
                out_ref[plane, place, 0] = block.astype(low)

    @pl.when(step == 0)
    def _():
        for copy in copies:
            copy.start()

    @pl.when(step < UP_ROWS)
    def _():
        store(dot(x_ref[...], y_ref[...], 0, 0))

    @pl.when(step == UP_ROWS)
    def _():
        for copy in copies:
            copy.wait()
        store(dot(o_ref[...], dr_ref[...], 0, 0))


def grad_of_wide(blocks, x, y, first, attended, resid_low, side, added=None):
    planes, narrow = blocks
    rows = D // (planes * narrow)
    count = UP_ROWS + 1
    out_spec = pl.BlockSpec((planes, narrow, 1, rows, HALF), lambda j, s: (0, 0, j, 0, 0))
    return pl.pallas_call(
        partial(wide_kernel, added is not None),
        grid_spec=pltpu.PrefetchScalarGridSpec(
            num_scalar_prefetch=1,
            grid=(count,),
            in_specs=[
                whole((ROWS, D)),
                pl.BlockSpec(
                    (ROWS, HALF), lambda j, s: (0, s[0] + jnp.minimum(j, UP_ROWS - 1))
                ),
                anywhere,
                anywhere,
                *([out_spec] if added is not None else []),
            ],
            out_specs=out_spec,
            scratch_shapes=[
                pltpu.VMEM((ROWS, D), low),
                pltpu.VMEM((ROWS, HALF), low),
                pltpu.SemaphoreType.DMA((2,)),
            ],
        ),
        out_shape=jax.ShapeDtypeStruct((planes, narrow, count, rows, HALF), low),
        cost_estimate=pl.CostEstimate(
            flops=4 * ROWS * count * D * HALF, bytes_accessed=8 * ROWS * D, transcendentals=0
        ),
        compiler_params=params(),
        name="grad_of_wide",
    )(
        jnp.stack([jnp.int32(first), side]), x, y, attended, resid_low,
        *([added] if added is not None else []),
    )


def grad_of_rows(blocks, x, y, first, count, added=None):
    planes, narrow = blocks
    if planes == 1:
        rows = HALF
        out_spec = pl.BlockSpec((1, 1, 1, rows, D), lambda i, s: (0, 0, 0, i, 0))
        shape = (1, 1, 1, count * HALF, D)
    else:
        rows = HALF // planes
        out_spec = pl.BlockSpec((planes, 1, 1, rows, D), lambda i, s: (0, i, 0, 0, 0))
        shape = (planes, count, 1, rows, D)
    return weight_call(
        "grad_of_rows",
        count,
        pl.BlockSpec((ROWS, HALF), lambda i, s: (0, s[0] + i)),
        pl.BlockSpec((ROWS, D), lambda i, s: (0, 0)),
        out_spec,
        shape,
        first, x, y, added,
    )


ENTRY_TILE = 512


def entry_kernel(count, levels_ref, place_ref, tokens_ref, dr_ref, vec_ref, *refs):
    step = pl.program_id(0)
    grads, sources = refs[:count], refs[count : 2 * count]
    grad_ref, gain_ref, table_ref = refs[2 * count : 2 * count + 3]
    weights, semaphores = refs[2 * count + 3 : -1], refs[-1]

    @pl.when(step == 0)
    def _():
        gain_ref[...] = jnp.zeros_like(gain_ref)
        table_ref[...] = jnp.zeros_like(table_ref)
        bring(sources, weights, place_ref[1], semaphores)

    matrices = [side_by_side(weight, range(3)) for weight in weights]
    per_tile = TILE // BLOCK
    subs = ENTRY_TILE // TILE
    for sub in range(subs):
        rows = slice(sub * TILE, (sub + 1) * TILE)
        back = None
        for grad, matrix in zip(grads, matrices):
            parts = jnp.concatenate([grad[part, rows, :] for part in range(3)], axis=1)
            term = dot(parts, matrix, 1, 1)
            back = term if back is None else back + term
        hidden = hidden_tile(levels_ref, tokens_ref[rows, :], vec_ref, sub, subs)
        normed, scaling = normalised(hidden)
        gain_ref[...] += eight_rows(back * normed)
        result = dr_ref[rows, :] + norm_back(normed, scaling, vec_ref[0:1, :], back)
        grad_ref[rows, :] = result

    @pl.when(step < SEQ // ENTRY_TILE)
    def _():
        for sub in range(subs):
            sums = grad_ref[sub * TILE : (sub + 1) * TILE, :]
            sums = sums.reshape(per_tile, BLOCK, D).sum(axis=1)
            for block in range(per_tile):
                level = levels_ref[(step * subs + sub) * per_tile + block]
                table_ref[pl.ds(level, 1), :] += sums[block : block + 1, :]


def entry(levels, places, tokens, resid_grad, vec_master, grads, weights):
    count = len(weights)
    return pl.pallas_call(
        partial(entry_kernel, count),
        grid_spec=pltpu.PrefetchScalarGridSpec(
            num_scalar_prefetch=2,
            grid=(ROWS // ENTRY_TILE,),
            in_specs=[rows_of(D, ENTRY_TILE), rows_of(D, ENTRY_TILE), whole((VROWS, D))]
            + [
                pl.BlockSpec((3, ENTRY_TILE, grad.shape[2]), lambda i, *_: (0, i, 0))
                for grad in grads
            ]
            + [anywhere] * count,
            out_specs=[
                rows_of(D, ENTRY_TILE),
                pl.BlockSpec((8, D), lambda i, *_: (0, 0)),
                pl.BlockSpec((LEVELS, D), lambda i, *_: (0, 0)),
            ],
            scratch_shapes=ordered_scratch(weights),
        ),
        out_shape=[
            jax.ShapeDtypeStruct((ROWS, D), full),
            jax.ShapeDtypeStruct((8, D), full),
            jax.ShapeDtypeStruct((LEVELS, D), full),
        ],
        cost_estimate=pl.CostEstimate(
            flops=6 * ROWS * D * D, bytes_accessed=20 * ROWS * D, transcendentals=0
        ),
        compiler_params=params(),
        name="entry",
    )(levels, places, tokens, resid_grad, vec_master, *grads, *weights)


PARTS = (3, 1, 4)


def swapped_halves(entries):
    lane = lax.broadcasted_iota(jnp.int32, entries.shape, 1) % PAIR
    quarter = HEAD_DIM // 2
    width = entries.shape[1]
    ahead = pltpu.roll(entries, width - quarter, 1)
    behind = pltpu.roll(entries, quarter, 1)
    second = (lane >= quarter) & (lane < 2 * quarter)
    third = (lane >= 2 * quarter) & (lane < 3 * quarter)
    return jnp.where(second, ahead, jnp.where(third, behind, entries))


def slot_pieces(kind, wide):
    planes = wide // 2
    found = []
    for plane in range(planes):
        for half in range(2):
            place = 2 * plane + half
            if kind < 3:
                parts, rows = PARTS[kind], D // 4 // planes
                for part in range(parts):
                    where = pl.ds(plane * rows * parts + part, rows, stride=parts)
                    found.append((place, part, part * rows, rows, where, half * HALF))
            else:
                rows = HALF // planes
                for column in range(2):
                    where = pl.ds(half * HALF + plane * rows, rows)
                    found.append((place, 2, column * rows, rows, where, column * HALF))
    return found


LANES = 128


def pack_kernel(owners_ref, slot_ref, out_ref, stage_ref):
    place = lax.axis_index("wide")
    wide = out_ref.shape[0]
    for index in range(D // LANES):
        stage_ref[index] = slot_ref[:, index * LANES : (index + 1) * LANES]
    for kind in range(4):

        @pl.when(owners_ref[kind] == place)
        def _(kind=kind):
            for target, part, start, rows, where, column in slot_pieces(kind, wide):
                for index in range(HALF // LANES):
                    block = stage_ref[column // LANES + index, where, :]
                    if kind == 0 and part < 2:
                        block = swapped_halves(block)
                    columns = slice(index * LANES, (index + 1) * LANES)
                    out_ref[target, start : start + rows, columns] = block.astype(low)


def pack(owners, slot):
    wide = lax.axis_size("wide")
    shape = (wide, 2 * D // wide, HALF)
    return pl.pallas_call(
        pack_kernel,
        grid_spec=pltpu.PrefetchScalarGridSpec(
            num_scalar_prefetch=1,
            grid=(1,),
            in_specs=[whole(slot.shape)],
            out_specs=whole(shape),
            scratch_shapes=[pltpu.VMEM((D // LANES, slot.shape[0], LANES), full)],
        ),
        out_shape=jax.ShapeDtypeStruct(shape, low),
        cost_estimate=pl.CostEstimate(
            flops=D * D, bytes_accessed=6 * D * D, transcendentals=0
        ),
        compiler_params=params(),
        name="pack",
    )(owners, slot)


def settle_kernel(owners_ref, qkv_ref, wide_ref, down_ref, out_ref, square_ref):
    squares = jnp.zeros((8, HALF), full)

    def summed(ref, part):
        result = ref[0, part].astype(full)
        for index in range(1, ref.shape[0]):
            result = result + ref[index, part].astype(full)
        return result.astype(low)

    out_ref[...] = jnp.zeros_like(out_ref)
    for kind in range(4):
        target = owners_ref[kind]
        for part in range((3, 1, 4, 1)[kind]):
            if kind == 0:
                share = summed(qkv_ref, part)
            elif kind < 3:
                share = summed(wide_ref, UP_ROWS if kind == 1 else part)
            else:
                share = summed(down_ref, 0)
            rows = share.shape[0]
            for column in range(share.shape[1] // HALF):
                block = share[:, column * HALF : (column + 1) * HALF]
                start = (part + column) * rows
                out_ref[target, start : start + rows, :] = block
                entries = block.astype(full)
                squares = squares + eight_rows(entries * entries)
    square_ref[...] = jnp.broadcast_to(jnp.sum(squares, keepdims=True), square_ref.shape)


def settle(owners, qkv, wide_parts, down):
    wide = lax.axis_size("wide")
    shape = (wide, 2 * D // wide, HALF)
    return pl.pallas_call(
        settle_kernel,
        grid_spec=pltpu.PrefetchScalarGridSpec(
            num_scalar_prefetch=1,
            grid=(1,),
            in_specs=[whole(qkv.shape), whole(wide_parts.shape), whole(down.shape)],
            out_specs=[whole(shape), whole((8, 128))],
        ),
        out_shape=[jax.ShapeDtypeStruct(shape, low), jax.ShapeDtypeStruct((8, 128), full)],
        cost_estimate=pl.CostEstimate(
            flops=4 * D * D, bytes_accessed=6 * D * D, transcendentals=0
        ),
        compiler_params=params(),
        name="settle",
    )(owners, qkv, wide_parts, down)


FINISH_ROWS = 192


def finish_kernel(
    plain, owners_ref, came_ref, sums_ref, vec_moment_ref, vec_square_ref, vec_master_ref,
    moment_ref, square_ref, master_ref,
    master_out, moment_out, square_out, vec_grad_out, vec_moment_out, vec_square_out,
    vec_master_out, norm_out, grad_ref
):
    step = pl.program_id(0)
    place = lax.axis_index("wide")
    here = lax.axis_index("narrow")
    wide = came_ref.shape[0]
    narrow = sums_ref.shape[0]
    total = sums_ref[here]
    for index in range(1, narrow):
        total = total + sums_ref[lax.rem(here - index + narrow, narrow)]
    vec, total = total[:VROWS], total[VROWS:, 0:1]
    norm = jnp.sqrt(total + jnp.sum(vec * vec, keepdims=True))
    clip = jnp.minimum(1.0, 1.0 / (norm + 1e-06))

    @pl.when(step == 0)
    def _():
        if plain:
            grad_ref[...] = came_ref[...]
        for kind in range(0 if plain else 4):

            @pl.when(owners_ref[kind] == place)
            def _(kind=kind):
                for source, part, start, rows, where, column in slot_pieces(kind, wide):
                    block = came_ref[source, start : start + rows, :].astype(full)
                    for index in range(HALF // LANES):
                        piece = block[:, index * LANES : (index + 1) * LANES]
                        if kind == 0 and part < 2:
                            piece = swapped_halves(piece)
                        grad_ref[column // LANES + index, where, :] = piece

        norm_out[...] = norm
        vec_clipped = vec * clip
        vec_grad_out[...] = vec_clipped
        vec_moment_out[...], vec_square_out[...], vec_master_out[...] = adam(
            vec_clipped, vec_moment_ref[...], vec_square_ref[...], vec_master_ref[...],
            0.0, vector_rate,
        )

    used = jnp.int32(0)
    for kind in range(4):
        rows = D // 4 * (PARTS[kind] if kind < 3 else 4)
        used = jnp.where(owners_ref[kind] == place, rows, used)
    row = step * FINISH_ROWS + lax.broadcasted_iota(jnp.int32, (FINISH_ROWS, D), 0)
    start = pl.multiple_of(step * FINISH_ROWS, FINISH_ROWS)
    grad = jnp.concatenate(
        [grad_ref[index, pl.ds(start, FINISH_ROWS), :] for index in range(D // LANES)], axis=1
    )
    moment_new, square_new, master_new = adam(
        grad * clip,
        moment_ref[...], square_ref[...], master_ref[...], decay_rate, learn_rate,
    )
    kept = row < used
    master_out[...] = jnp.where(kept, master_new, 0.0)
    moment_out[...] = jnp.where(kept, moment_new, 0.0)
    square_out[...] = jnp.where(kept, square_new, 0.0)


def finish(plain, owners, came, sums, vec_states, states):
    rows = states[0].shape[0]
    state_spec = pl.BlockSpec((FINISH_ROWS, D), lambda i, *_: (i, 0))
    vec_spec = whole((VROWS, D))
    state = jax.ShapeDtypeStruct((rows, D), full)
    vec = jax.ShapeDtypeStruct((VROWS, D), full)
    return pl.pallas_call(
        partial(finish_kernel, plain),
        grid_spec=pltpu.PrefetchScalarGridSpec(
            num_scalar_prefetch=1,
            grid=(rows // FINISH_ROWS,),
            in_specs=[whole(came.shape), whole(sums.shape), *[vec_spec] * 3, *[state_spec] * 3],
            out_specs=[*[state_spec] * 3, *[vec_spec] * 4, whole((1, 1))],
            scratch_shapes=[pltpu.VMEM((D // LANES, rows, LANES), full)],
        ),
        out_shape=[state] * 3 + [vec] * 4 + [jax.ShapeDtypeStruct((1, 1), full)],
        cost_estimate=pl.CostEstimate(
            flops=20 * D * D, bytes_accessed=26 * D * D, transcendentals=0
        ),
        compiler_params=params(),
        name="finish",
    )(owners, came, sums, *vec_states, *states)


def turn_tables():
    positions = jnp.arange(SEQ, dtype=jnp.int32).astype(full)
    exponents = jnp.arange(HEAD_DIM // 2, dtype=full) * (2.0 / HEAD_DIM)
    angles = positions[:, None] * (rope_base ** (-exponents))[None, :]
    cos = jnp.cos(angles)
    sin = jnp.sin(angles)
    return (
        jnp.concatenate([cos, cos, cos, cos], axis=1),
        jnp.concatenate([-sin, -sin, sin, sin], axis=1),
    )


def adam(grad, moment, square, master, decay, rate):
    moment_new = moment_decay * moment + (1.0 - moment_decay) * grad
    square_new = moment_decay * square + (1.0 - moment_decay) * grad * grad
    correction = 1.0 - moment_decay**STEP
    master_new = master * (1.0 - rate * decay) - rate * (moment_new / correction) / (
        jnp.sqrt(square_new / correction) + adam_eps
    )
    return (moment_new, square_new, master_new)


def flip(value, axis, bits):
    count = lax.axis_size(axis)
    return lax.ppermute(value, axis, [(i, i ^ bits) for i in range(count)])


def planes_groups():
    count = lax.axis_size("wide")
    return [list(range(start, count, 2)) for start in range(2)]


def shift(value, step):
    count = lax.axis_size("narrow")
    return lax.ppermute(value, "narrow", [(i, (i + step) % count) for i in range(count)])


def swap_planes(blocks):
    return lax.all_to_all(blocks, "wide", 0, 0, axis_index_groups=planes_groups())


def copies(value, count):
    return jnp.broadcast_to(value[None], (count, *value.shape))


def after(value, *others):
    return lax.optimization_barrier((value, *others))[0]


def gather_narrow(share):
    return [share] + [shift(share, step) for step in range(1, lax.axis_size("narrow"))]


def gather_planes(held):
    held = swap_planes(copies(jnp.stack(held), lax.axis_size("wide") // 2))
    if held.shape[3] % 16 == 0:
        return held
    narrow, parts, columns = held.shape[1], held.shape[2], held.shape[4]
    order = (lax.axis_index("narrow") - jnp.arange(narrow)) % narrow
    held = jnp.take(held, order, axis=1)
    return held.transpose(2, 1, 0, 3, 4).reshape(1, 1, parts, -1, columns)


def total(blocks):
    return jnp.sum(blocks.astype(full), axis=0).astype(low)


def reduce_planes(matrix):
    planes, narrow = lax.axis_size("wide") // 2, lax.axis_size("narrow")
    if matrix.shape[0] != planes:
        parts, columns = matrix.shape[2], matrix.shape[4]
        matrix = matrix.reshape(parts, narrow, planes, -1, columns)
        matrix = matrix.transpose(2, 1, 0, 3, 4)
    return total(swap_planes(matrix))


def narrow_pieces(held):
    count = lax.axis_size("narrow")
    place = lax.axis_index("narrow")

    def part(step):
        return lax.dynamic_index_in_dim(held, (place + step) % count, 0, keepdims=False)

    return [part(0)] + [shift(part(step), step) for step in range(1, count)]


def swap_halves(matrix):
    pairs = matrix.reshape(*matrix.shape[:-1], -1, 2, 2, HEAD_DIM // 2)
    return jnp.swapaxes(pairs, -3, -2).reshape(matrix.shape)


def plain_layouts(slot_rows):
    wide = lax.axis_size("wide")
    planes, most = wide // 2, 2 * D // wide
    rows, deep = D // 4 // planes, HALF // planes

    def pack_columns(kind, slot):
        parts = PARTS[kind]
        blocks = slot[: rows * planes * parts].reshape(planes, rows, parts, 2, HALF)
        blocks = blocks.transpose(0, 3, 2, 1, 4)
        if kind == 0:
            blocks = jnp.concatenate([swap_halves(blocks[:, :, :2]), blocks[:, :, 2:]], axis=2)
        blocks = blocks.reshape(wide, parts * rows, HALF)
        return jnp.pad(blocks, ((0, 0), (0, most - parts * rows), (0, 0)))

    def unpack_columns(kind, blocks):
        parts = PARTS[kind]
        blocks = blocks[:, : parts * rows].reshape(planes, 2, parts, rows, HALF)
        if kind == 0:
            blocks = jnp.concatenate([swap_halves(blocks[:, :, :2]), blocks[:, :, 2:]], axis=2)
        flat = blocks.transpose(0, 3, 2, 1, 4).reshape(planes * rows * parts, D)
        return jnp.pad(flat, ((0, slot_rows - flat.shape[0]), (0, 0)))

    def pack_down(slot):
        blocks = slot.reshape(2, planes, deep, 2, HALF)
        return blocks.transpose(1, 0, 3, 2, 4).reshape(wide, 2 * deep, HALF)

    def unpack_down(blocks):
        blocks = blocks.reshape(planes, 2, 2, deep, HALF)
        return blocks.transpose(1, 0, 3, 2, 4).reshape(slot_rows, D)

    packs = [partial(pack_columns, kind) for kind in range(3)] + [pack_down]
    unpacks = [partial(unpack_columns, kind) for kind in range(3)] + [unpack_down]
    packs.append(lambda slot: jnp.zeros((wide, most, HALF), slot.dtype))
    unpacks.append(lambda blocks: jnp.zeros((slot_rows, D), blocks.dtype))
    return packs, unpacks


def plain_pack(kind, slot):
    return lax.switch(kind, plain_layouts(slot.shape[0])[0], slot.astype(low))


def plain_settle(owners, qkv, wide_parts, down):
    wide = lax.axis_size("wide")
    qkv, wide_parts, down = total(qkv), total(wide_parts), total(down)
    down = jnp.stack([down[0, :, :HALF], down[0, :, HALF:]])
    places = jnp.arange(wide, dtype=jnp.int32)[:, None, None]
    sent = jnp.zeros((wide, 2 * D // wide, HALF), low)
    squares = jnp.zeros((), full)
    shares = (qkv, wide_parts[UP_ROWS:], wide_parts[:UP_ROWS], down)
    for kind, share in enumerate(shares):
        share = share.reshape(-1, HALF)
        squares = squares + jnp.sum(jnp.square(share.astype(full)))
        block = jnp.pad(share, ((0, sent.shape[1] - share.shape[0]), (0, 0)))[None]
        sent = jnp.where(places == owners[kind], block, sent)
    return sent, jnp.broadcast_to(squares, (8, 128))


def plain_unpack(kind, slot_rows, came):
    slot = lax.switch(kind, plain_layouts(slot_rows)[1], came).astype(full)
    return jnp.swapaxes(slot.reshape(slot_rows, D // LANES, LANES), 0, 1)


def sum_over_wide(value):
    wide = lax.axis_size("wide")
    bit = 1
    while bit < wide:
        value = value + flip(value, "wide", bit)
        bit *= 2
    return value


def vectors_over_wide(value):
    return jnp.sum(lax.all_to_all(copies(value, lax.axis_size("wide")), "wide", 0, 0), axis=0)


def local(
    tokens,
    cotangent,
    lengths,
    levels,
    owners,
    master_slots,
    moment_slots,
    square_slots,
    vec_master,
    vec_moment,
    vec_square,
):
    narrow = lax.axis_size("narrow")
    wide = lax.axis_size("wide")
    side = lax.axis_index("wide") & 1
    planes = wide // 2
    rows = D // (narrow * planes)
    deep = FF // 2 // (narrow * planes)

    plain = rows % 16 != 0
    owned = owners == lax.axis_index("wide")
    kind = jnp.where(jnp.any(owned), jnp.argmax(owned), 4).astype(jnp.int32)
    if plain:
        packed = plain_pack(kind, master_slots[0])
    else:
        packed = pack(owners, master_slots[0])
    came = lax.all_to_all(packed, "wide", 0, 0)

    def share(kind, count):
        return lax.dynamic_index_in_dim(came, owners[kind], 0, keepdims=False)[:count]

    qkv_share = share(0, 3 * rows).reshape(3, rows, HALF)
    wide_share = jnp.concatenate([share(2, 4 * rows), share(1, rows)])
    wide_share = wide_share.reshape(UP_ROWS + 1, rows, HALF)
    down_share = share(3, 2 * deep)
    down_share = jnp.concatenate([down_share[:deep], down_share[deep:]], axis=1)[None]

    tokens = tokens.reshape(ROWS, D)
    cotangent = cotangent.reshape(ROWS, D)
    levels = levels.reshape(-1)
    here = jnp.stack([side, lax.axis_index("narrow")]).astype(jnp.int32)
    cos, sin = turn_tables()
    bias = vec_master[3 : 3 + UP_ROWS].reshape(UP_ROWS, 2, HALF)
    bias = jnp.stack([bias[:, 0], bias[:, 1]])
    bias = jnp.where(side == 1, bias[::-1], bias).reshape(1, FF)
    half_pairs = GROUPS // 2
    scalars = [
        jnp.stack([lengths[0], half_pairs * half]) for half in (side, 1 - side)
    ]
    attn_in = norm_one(levels, tokens, vec_master)

    qkv_plane = gather_narrow(after(qkv_share, attn_in, cos, sin, bias, *scalars))
    qkv_mine = gather_planes(qkv_plane)
    down_plane = gather_narrow(after(down_share, *qkv_plane))
    qkv_other = flip(qkv_mine, "wide", 1)
    heads_mine = project(here, attn_in, qkv_mine, cos, sin)
    down_mine = gather_planes(after(down_plane, qkv_mine))
    wide_plane = gather_narrow(after(wide_share, qkv_mine))
    before = attend(scalars[0], heads_mine, None)
    wide_mine = gather_planes(after(wide_plane, before[0], down_mine))
    down_other = flip(after(down_mine, before[0]), "wide", 1)
    heads_other = project(here, after(attn_in, before[0]), qkv_other, cos, sin)
    attended, logs = attend(scalars[1], heads_other, before)
    wide_other = flip(after(wide_mine, attended), "wide", 1)
    output, mlp_in, act, pre_grad, resid_grad, resid_low, attended_grad, sums, up_sums = feed(
        levels,
        here,
        tokens,
        attended,
        cotangent,
        vec_master,
        bias,
        (wide_mine, wide_other, down_mine, down_other),
    )

    blocks = (1, 1) if plain else (planes, narrow)
    down_theirs = flip(grad_of_rows(blocks, act, cotangent, 4, 4), "wide", 1)
    wide_theirs = grad_of_wide(
        blocks, mlp_in, pre_grad, 4, attended, resid_low, 1 - side
    )
    wide_came = flip(wide_theirs, "wide", 1)
    down_grad = grad_of_rows(blocks, act, after(cotangent, wide_theirs), 0, 4, down_theirs)
    down_planes = reduce_planes(down_grad)
    wide_grad = grad_of_wide(
        blocks, mlp_in, after(pre_grad, down_grad), 0, attended, resid_low, side, wide_came
    )
    grad_other = attend_back(
        scalars[1], heads_other, attended, after(attended_grad, wide_grad), logs, cos, sin
    )
    wide_planes = reduce_planes(after(wide_grad, down_planes))
    down_pieces = narrow_pieces(down_planes)
    qkv_theirs = grad_of_columns(blocks, attn_in, grad_other, 0, 3)
    grad_mine = attend_back(
        scalars[0], heads_mine, attended, after(attended_grad, qkv_theirs, down_planes), logs, cos, sin
    )
    qkv_grad = grad_of_columns(
        blocks, attn_in, grad_mine, 0, 3, flip(qkv_theirs, "wide", 1)
    )
    wide_pieces = narrow_pieces(after(wide_planes, qkv_grad, *down_pieces))
    qkv_planes = reduce_planes(after(qkv_grad, wide_planes))
    input_grad, gain_sums, table_grad = entry(
        levels, here, tokens, resid_grad, vec_master,
        (after(grad_mine, qkv_grad, wide_planes, *down_pieces), grad_other),
        (qkv_mine, qkv_other),
    )
    qkv_pieces = narrow_pieces(after(qkv_planes, input_grad, *wide_pieces))
    up_sums = up_sums.sum(axis=0).reshape(2, UP_ROWS, HALF)
    up_sums = jnp.where(side == 1, up_sums[::-1], up_sums)
    up_sums = jnp.swapaxes(up_sums, 0, 1).reshape(UP_ROWS, D)
    vec_local = (
        jnp.concatenate(
            [
                gain_sums.sum(axis=0)[None],
                sums[:8].sum(axis=0)[None],
                sums[8:].sum(axis=0)[None],
                up_sums,
                table_grad,
            ],
            axis=0,
        )
        * row_scale
    )
    vec_wide = vectors_over_wide(after(vec_local, qkv_planes))
    sent, squares = (plain_settle if plain else settle)(
        owners, jnp.stack(qkv_pieces), jnp.stack(wide_pieces), jnp.stack(down_pieces)
    )
    came = lax.all_to_all(after(sent, vec_wide), "wide", 0, 0)
    if plain:
        came = plain_unpack(kind, master_slots.shape[1], came)
    squares = jnp.tile(sum_over_wide(squares)[:1], (1, D // LANES))
    all_sums = jnp.stack(gather_narrow(jnp.concatenate([vec_wide, squares])))
    (
        master_new, moment_new, square_new,
        vec_grad, vec_moment_new, vec_square_new, vec_master_new, norm_value,
    ) = finish(
        plain, owners, came, all_sums, (vec_moment, vec_square, vec_master),
        (moment_slots[0], square_slots[0], master_slots[0]),
    )
    return (
        output[None],
        input_grad[None],
        master_new[None],
        moment_new[None],
        square_new[None],
        vec_grad,
        vec_moment_new,
        vec_square_new,
        vec_master_new,
        norm_value.reshape(1),
    )


def solution(mesh):
    placed = (
        P(("wide", "narrow"), None, None),
        P(("wide", "narrow"), None, None),
        P(("wide", "narrow")),
        P(("wide", "narrow"), None),
        P(),
        P("wide", "narrow", None),
        P("wide", "narrow", None),
        P("wide", "narrow", None),
        P(),
        P(),
        P(),
    )
    return jax.shard_map(
        local,
        mesh=mesh,
        in_specs=placed,
        out_specs=(
            P(("wide", "narrow"), None, None),
            P(("wide", "narrow"), None, None),
            P("wide", "narrow", None),
            P("wide", "narrow", None),
            P("wide", "narrow", None),
            P(),
            P(),
            P(),
            P(),
            P(),
        ),
        check_vma=False,
    )
```

time: 1090 us -> 480 us (0.44)
  waiting for transfers between devices: 437 us -> 58 us
  blocking collectives: 184 us -> 0 us
  starting transfers between devices: 0.36 us -> 76.9 us
  local copies, waits for them, and re-layouts: 65 us -> 17.3 us
  other arithmetic: 61.7 us -> 14.7 us
  between operations: 22.9 us -> 9.9 us
  Pallas kernels: 308 us -> 296 us
    all_gather x4 -> x0, waiting for transfers between devices: 199 us -> none  [local(): lax.all_gather(shards, 'narrow', axis=0, tiled=True)]
    psum x2 -> x0, blocking collectives: 184 us -> none  [the longest x1 144 us: local(): lax.psum((narrow_shares[0], narrow_shares[1], narrow_shares[2], narrow_sh...]
    reduce_scatter x4 -> x0, waiting for transfers between devices: 159 us -> none  [local(): lax.psum_scatter(grad, 'narrow', scatter_dimension=0, tiled=True)]
    psum x1 -> x0, waiting for transfers between devices: 77.2 us -> none  [spread(): return lax.psum(kept, axis)]
    ppermute x0 -> x30, waiting for transfers between devices: none -> 48 us  [the longest x21 24.9 us: shift(): lax.ppermute(value, 'narrow', [(i, (i + step) % count) for i in range(cou...]
    ppermute x0 -> x30, starting transfers between devices: none -> 39.6 us  [the longest x21 34.4 us: shift(): lax.ppermute(value, 'narrow', [(i, (i + step) % count) for i in range(cou...]
    all_to_all x0 -> x9, starting transfers between devices: none -> 37.3 us  [the longest x6 23.9 us: swap_planes(): lax.all_to_all(blocks, 'wide', 0, 0, axis_index_groups=planes_groups())]
    pallas_call x1 -> x2, Pallas kernels: 89.6 us -> 64.6 us  [attend_back(): pl.pallas_call(attend_back_kernel, grid_spec=pltpu.PrefetchScalarGridSpec...]
  transfers between devices with their start and end apart: 9 -> 39, of which waited for: 6 -> 16; matrix products, arithmetic and copies ran while one was open for 4% -> 5% of each run, Pallas kernels for 22% -> 44%
where the time goes in v2:
time: 480 us; the launch traced here: 473 us
  Pallas kernels  296 us (62%)
  starting transfers between devices  76.9 us (16%)
  waiting for transfers between devices  58 us (12%)
  local copies, waits for them, and re-layouts  17.3 us (4%)
  other arithmetic  14.7 us (3%)
  between operations  9.9 us (2%)
    pallas_call x1, Pallas kernels, feed(): pl.pallas_call(feed_kernel, grid_spec=pltpu.PrefetchScalarGridSpec(num_sc...  64.8 us
    pallas_call x2, Pallas kernels, attend_back(): pl.pallas_call(attend_back_kernel, grid_spec=pltpu.PrefetchScalarGridSpec...  64.6 us
    pallas_call x2, Pallas kernels, attend(): pl.pallas_call(partial(attend_kernel, aliased), grid_spec=pltpu.PrefetchS...  40.6 us
    pallas_call x4, Pallas kernels, weight_call(): pl.pallas_call(partial(weight_kernel, added is not None), grid_spec=pltpu...  36.5 us
    ppermute x21, starting transfers between devices, shift(): lax.ppermute(value, 'narrow', [(i, (i + step) % count) for i in range(cou...  34.4 us
    pallas_call x2, Pallas kernels, grad_of_wide(): pl.pallas_call(partial(wide_kernel, added is not None), grid_spec=pltpu.P...  26.8 us
    ppermute x21, waiting for transfers between devices, shift(): lax.ppermute(value, 'narrow', [(i, (i + step) % count) for i in range(cou...  24.9 us
    all_to_all x6, starting transfers between devices, swap_planes(): lax.all_to_all(blocks, 'wide', 0, 0, axis_index_groups=planes_groups())  23.9 us
  transfers between devices with their start and end apart: 39, of which 16 were waited for; matrix products, arithmetic and copies ran while one was open for 5% of the time, Pallas kernels for 44%

profile of v2, /device:TPU:0, one launch (start us, length us, event | category | flops | bytes accessed | tf_op | source)
XLA Modules:
  0.0 473.2 jit_solution(5528518288296202095)
XLA Ops:
  4.5 5.0 %all-to-all-start = ((bf16[8,192,384]{2,1,0:T(8,128)(2,1)}), bf16[8,192,384]{2,1,0:T(8,128)(2,1)S(1)}, u32[]{:S(2)}, u32[]{:S(2)}) async-start(bf16[8,192,384]{2,1,0:T(8,128)(2,1)} %pack.1), calls=%async_computation | async-start | bytes 2359296 | tf_op jit(solution)/shard_map/all_to_all | solution.py:1281
  14.1 7.8 %norm_one.1.a_ref.x_ref = bf16[2048,768]{1,0:T(8,128)(2,1)} custom-call(s32[64]{0:T(128)} %bitcast.131, bf16[2048,768]{1,0:T(8,128)(2,1)} %bitcast.93, f32[15,768]{1,0:T(8,128)} %vec_master_ref.1), custom_call_target="tpu_custom_call" | custom-call | flops 15728640 | bytes 6291456 | tf_op jit(solution)/shard_map/norm_one/pallas_call | solution.py:145
  34.1 4.4 collective-permute-done.1
  54.5 5.0 %collective-permute-done.8 = bf16[1,96,768]{2,1,0:T(8,128)(2,1)S(1)} collective-permute-done((bf16[1,96,768]{2,1,0:T(8,128)(2,1)S(1)}, bf16[1,96,768]{2,1,0:T(8,128)(2,1)S(1)}, u32[]{:S(2)}, u32[]{:S(2)}) %collective-permute-start.8) | collective-permute-done | bytes 147488 | tf_op jit(solution)/shard_map/ppermute | solution.py:1122
  59.5 5.7 %all-to-all-done.1.w_hbm.refs_2_ = bf16[4,4,3,48,384]{4,3,2,1,0:T(8,128)(2,1)S(1)} async-done(((bf16[4,4,3,48,384]{4,3,2,1,0:T(8,128)(2,1)}), bf16[4,4,3,48,384]{4,3,2,1,0:T(8,128)(2,1)S(1)}, u32[]{:S(2)}, u32[]{:S(2)}) %all-to-all-start.1) | async-done | bytes 1769504 | tf_op jit(solution)/shard_map/all_to_all | solution.py:1126
  81.3 10.1 %project.2.q_ref.k_ref.v_ref = bf16[2048,1152]{1,0:T(8,128)(2,1)} custom-call(s32[2]{0:T(128)} %pad_add_fusion.place_ref.side_ref, bf16[2048,768]{1,0:T(8,128)(2,1)} %norm_one.1.a_ref.x_ref, bf16[4,4,3,48,384]{4,3,2,1,0:T(8,128)(2,1)} %copy-done.4, f32[1024,128]{1,0:T(8,128)} %get-tuple-element.139.cos_ref, f32[1024,128]{1,0:T(8,128)} %get-tuple-element.140.sin_ref), custom_call_target="tpu_custom_call" | custom-call | flops 3623878656 | bytes 12582912 | tf_op jit(solution)/shard_map/project/pallas_call | solution.py:197
  91.4 20.3 %attend.2 = (bf16[2048,768]{1,0:T(8,128)(2,1)}, f32[6,2,2048]{2,1,0:T(2,128)}) custom-call(s32[2]{0:T(128)} %get-tuple-element.138.scalar_ref, bf16[2048,1152]{1,0:T(8,128)(2,1)} %project.2.q_ref.k_ref.v_ref, bf16[2048,1152]{1,0:T(8,128)(2,1)} %project.2.q_ref.k_ref.v_ref, bf16[2048,1152]{1,0:T(8,128)(2,1)} %project.2.q_ref.k_ref.v_ref), custom_call_target="tpu_custom_call" | custom-call | flops 9663676416 | bytes 6291456 | tf_op jit(solution)/shard_map/attend/pallas_call | solution.py:355
  114.1 4.3 all-to-all-start.3
  118.4 10.1 %project.3.q_ref.k_ref.v_ref = bf16[2048,1152]{1,0:T(8,128)(2,1)} custom-call(s32[2]{0:T(128)} %pad_add_fusion.place_ref.side_ref, bf16[2048,768]{1,0:T(8,128)(2,1)} %norm_one.1.a_ref.x_ref, bf16[4,4,3,48,384]{4,3,2,1,0:T(8,128)(2,1)} %collective-permute-done.3.w_hbm.refs_3_, f32[1024,128]{1,0:T(8,128)} %get-tuple-element.139.cos_ref, ...), custom_call_target="tpu_custom_call" | custom-call | flops 3623878656 | bytes 12582912 | tf_op jit(solution)/shard_map/project/pallas_call | solution.py:197
  128.5 20.3 %attend.3 = (bf16[2048,768]{1,0:T(8,128)(2,1)}, f32[6,2,2048]{2,1,0:T(2,128)}) custom-call(s32[2]{0:T(128)} %get-tuple-element.137.scalar_ref, bf16[2048,1152]{1,0:T(8,128)(2,1)} %project.3.q_ref.k_ref.v_ref, bf16[2048,1152]{1,0:T(8,128)(2,1)} %project.3.q_ref.k_ref.v_ref, ...), custom_call_target="tpu_custom_call", output_to_operand_aliasing={{0}: (4, {}), {1}: (5, {})} | custom-call | flops 9663676416 | bytes 6291456 | tf_op jit(solution)/shard_map/attend/pallas_call | solution.py:355
  154.6 7.2 %collective-permute-done.11.down_other_hbm = bf16[4,4,1,96,768]{4,3,2,1,0:T(8,128)(2,1)S(1)} collective-permute-done((bf16[4,4,1,96,768]{4,3,2,1,0:T(8,128)(2,1)}, bf16[4,4,1,96,768]{4,3,2,1,0:T(8,128)(2,1)S(1)}, u32[]{:S(2)}, u32[]{:S(2)}) %collective-permute-start.11) | collective-permute-done | bytes 2359328 | tf_op jit(solution)/shard_map/ppermute | solution.py:1112
  164.7 64.8 %feed.1 = (bf16[2048,768]{1,0:T(8,128)(2,1)}, bf16[2048,768]{1,0:T(8,128)(2,1)}, bf16[2048,3072]{1,0:T(8,128)(2,1)}, bf16[2048,3072]{1,0:T(8,128)(2,1)}, f32[204...) custom-call(s32[64]{0:T(128)} %bitcast.132, ...), custom_call_target="tpu_custom_call" | custom-call | flops 43486543872 | bytes 47185920 | tf_op jit(solution)/shard_map/feed/pallas_call | solution.py:632
  229.5 9.2 %grad_of_rows.2 = bf16[4,4,1,96,768]{4,3,2,1,0:T(8,128)(2,1)} custom-call(s32[1]{0:T(128)} %constant.106.clone.1.scalar_ref, bf16[2048,3072]{1,0:T(8,128)(2,1)} %get-tuple-element.83.x_ref, bf16[2048,768]{1,0:T(8,128)(2,1)} %bitcast.135), custom_call_target="tpu_custom_call" | custom-call | flops 9663676416 | bytes 12582912 | tf_op jit(solution)/shard_map/grad_of_rows/pallas_call | solution.py:673
  239.1 13.3 %grad_of_wide.2 = bf16[4,4,5,48,384]{4,3,2,1,0:T(8,128)(2,1)} custom-call(s32[2]{0:T(128)} %pad_add_fusion.4.side_ref, bf16[2048,768]{1,0:T(8,128)(2,1)} %get-tuple-element.81.x_ref, bf16[2048,3072]{1,0:T(8,128)(2,1)} %get-tuple-element.86.y_ref, bf16[2048,768]{1,0:T(8,128)(2,1)} %get-tuple-element.65.o_ref.o_hbm, bf16[2048,768]{1,0:T(8,128)(2,1)} %get-tuple-element.84.dr_hbm), custom_call_target="tpu_custom_call" | custom-call | flops 12079595520 | bytes 12582912 | tf_op jit(solution)/shard_map/grad_of_wide/pallas_call | solution.py:748
  255.9 9.6 %grad_of_rows.3 = bf16[4,4,1,96,768]{4,3,2,1,0:T(8,128)(2,1)} custom-call(s32[1]{0:T(128)} %constant.105.clone.1.scalar_ref, bf16[2048,3072]{1,0:T(8,128)(2,1)} %get-tuple-element.83.x_ref, bf16[2048,768]{1,0:T(8,128)(2,1)} %bitcast.136, bf16[4,4,1,96,768]{4,3,2,1,0:T(8,128)(2,1)} %copy-done.12), custom_call_target="tpu_custom_call" | custom-call | flops 9663676416 | bytes 12582912 | tf_op jit(solution)/shard_map/grad_of_rows/pallas_call | solution.py:673
  269.1 13.5 %grad_of_wide.3 = bf16[4,4,5,48,384]{4,3,2,1,0:T(8,128)(2,1)} custom-call(s32[2]{0:T(128)} %pad_add_fusion.3.side_ref, bf16[2048,768]{1,0:T(8,128)(2,1)} %get-tuple-element.81.x_ref, bf16[2048,3072]{1,0:T(8,128)(2,1)} %get-tuple-element.86.y_ref, bf16[2048,768]{1,0:T(8,128)(2,1)} %get-tuple-element.65.o_ref.o_hbm, ...), custom_call_target="tpu_custom_call" | custom-call | flops 12079595520 | bytes 12582912 | tf_op jit(solution)/shard_map/grad_of_wide/pallas_call | solution.py:748
  282.6 32.4 %attend_back.2.y_ref.refs_1_ = bf16[3,2048,384]{2,1,0:T(8,128)(2,1)} custom-call(s32[2]{0:T(128)} %get-tuple-element.137.scalar_ref, bf16[2048,1152]{1,0:T(8,128)(2,1)} %project.3.q_ref.k_ref.v_ref, bf16[2048,1152]{1,0:T(8,128)(2,1)} %project.3.q_ref.k_ref.v_ref, bf16[2048,1152]{1,0:T(8,128)(2,1)} %project.3.q_ref.k_ref.v_ref, ...), custom_call_target="tpu_custom_call" | custom-call | flops 24159191040 | bytes 12582912 | tf_op jit(solution)/shard_map/attend_back/pallas_call | solution.py:474
  315.0 8.7 %grad_of_columns.2 = bf16[4,4,3,48,384]{4,3,2,1,0:T(8,128)(2,1)} custom-call(s32[1]{0:T(128)} %constant.105.clone.1.scalar_ref, bf16[2048,768]{1,0:T(8,128)(2,1)} %norm_one.1.a_ref.x_ref, bf16[3,2048,384]{2,1,0:T(8,128)(2,1)} %attend_back.2.y_ref.refs_1_), custom_call_target="tpu_custom_call" | custom-call | flops 7247757312 | bytes 12582912 | tf_op jit(solution)/shard_map/grad_of_columns/pallas_call | solution.py:673
  333.4 32.2 %attend_back.3.y_ref.refs_0_ = bf16[3,2048,384]{2,1,0:T(8,128)(2,1)} custom-call(s32[2]{0:T(128)} %get-tuple-element.138.scalar_ref, bf16[2048,1152]{1,0:T(8,128)(2,1)} %project.2.q_ref.k_ref.v_ref, bf16[2048,1152]{1,0:T(8,128)(2,1)} %project.2.q_ref.k_ref.v_ref, bf16[2048,1152]{1,0:T(8,128)(2,1)} %project.2.q_ref.k_ref.v_ref, ...), custom_call_target="tpu_custom_call" | custom-call | flops 24159191040 | bytes 12582912 | tf_op jit(solution)/shard_map/attend_back/pallas_call | solution.py:474
  365.7 8.9 %grad_of_columns.3 = bf16[4,4,3,48,384]{4,3,2,1,0:T(8,128)(2,1)} custom-call(s32[1]{0:T(128)} %constant.105.clone.1.scalar_ref, bf16[2048,768]{1,0:T(8,128)(2,1)} %norm_one.1.a_ref.x_ref, bf16[3,2048,384]{2,1,0:T(8,128)(2,1)} %attend_back.3.y_ref.refs_0_, bf16[4,4,3,48,384]{4,3,2,1,0:T(8,128)(2,1)} %collective-permute-done.14.refs_0_), custom_call_target="tpu_custom_call" | custom-call | flops 7247757312 | bytes 12582912 | tf_op jit(solution)/shard_map/grad_of_columns/pallas_call | solution.py:673
  376.1 4.6 all-to-all-start.6
  388.3 18.3 %entry.1 = (f32[2048,768]{1,0:T(8,128)}, f32[8,768]{1,0:T(8,128)}, f32[8,768]{1,0:T(8,128)}) custom-call(s32[64]{0:T(128)} %bitcast.133, s32[2]{0:T(128)} %pad_add_fusion.place_ref.side_ref, bf16[2048,768]{1,0:T(8,128)(2,1)} %bitcast.95, f32[2048,768]{1,0:T(8,128)} %get-tuple-element.79.dr_ref, f32[15,768]{1,0:T(8,128)} %vec_master_ref.1, ...), custom_call_target="tpu_custom_call" | custom-call | flops 7247757312 | bytes 31457280 | tf_op jit(solution)/shard_map/entry/pallas_call | solution.py:845
  437.3 12.8 %collective-permute-done.25 = f32[8,128]{1,0:T(8,128)S(1)} collective-permute-done((f32[8,128]{1,0:T(8,128)S(1)}, f32[8,128]{1,0:T(8,128)S(1)}, u32[]{:S(2)}, u32[]{:S(2)}) %collective-permute-start.25) | collective-permute-done | bytes 4128 | tf_op jit(solution)/shard_map/ppermute | solution.py:1112
  463.2 9.6 %finish.1 = (f32[768,768]{1,0:T(8,128)}, f32[768,768]{1,0:T(8,128)}, f32[768,768]{1,0:T(8,128)}, f32[15,768]{1,0:T(8,128)}, f32[15,768]{1,0:T(8,128)}, /*index=5...) custom-call(s32[4]{0:T(128)} %owners_ref.5, bf16[8,192,384]{2,1,0:T(8,128)(2,1)} %copy-done, ...), custom_call_target="tpu_custom_call" | custom-call | flops 11796480 | bytes 15335424 | tf_op jit(solution)/shard_map/finish/pallas_call | solution.py:1070
  (156 shorter events, 125.4 us)
Async XLA Ops:
  4.5 21.8 %all-to-all-start = ((bf16[8,192,384]{2,1,0:T(8,128)(2,1)}), bf16[8,192,384]{2,1,0:T(8,128)(2,1)S(1)}, u32[]{:S(2)}, u32[]{:S(2)}) async-start(bf16[8,192,384]{2,1,0:T(8,128)(2,1)} %pack.1), calls=%async_computation | async-start | bytes 2359296 | tf_op jit(solution)/shard_map/all_to_all | solution.py:1281
  39.9 25.3 %all-to-all-start.1 = ((bf16[4,4,3,48,384]{4,3,2,1,0:T(8,128)(2,1)}), bf16[4,4,3,48,384]{4,3,2,1,0:T(8,128)(2,1)S(1)}, u32[]{:S(2)}, u32[]{:S(2)}) async-start(bf16[4,4,3,48,384]{4,3,2,1,0:T(8,128)(2,1)} %broadcast_in_dim.55), calls=%async_computation.1 | async-start | bytes 3538944 | tf_op jit(solution)/shard_map/all_to_all | solution.py:1126
  67.2 44.5 %all-to-all-start.2 = ((bf16[4,4,1,96,768]{4,3,2,1,0:T(8,128)(2,1)}), bf16[4,4,1,96,768]{4,3,2,1,0:T(8,128)(2,1)S(1)}, u32[]{:S(2)}, u32[]{:S(2)}) async-start(bf16[4,4,1,96,768]{4,3,2,1,0:T(8,128)(2,1)} %broadcast_in_dim.58), calls=%async_computation.2 | async-start | bytes 4718592 | tf_op jit(solution)/shard_map/all_to_all | solution.py:1126
  75.4 36.3 %collective-permute-start.4 = (bf16[5,48,384]{2,1,0:T(8,128)(2,1)S(1)}, bf16[5,48,384]{2,1,0:T(8,128)(2,1)S(1)}, u32[]{:S(2)}, u32[]{:S(2)}) collective-permute-start(bf16[5,48,384]{2,1,0:T(8,128)(2,1)S(1)} %bitcast.98), channel_id=1, source_target_pairs={{0,1},{1,2},{2,3},{3,0},{4,5},{5,6},{6,7},{7,4},{8,9},{9,10},{10,1... | collective-permute-start | bytes 552968 | tf_op jit(solution)/shard_map/ppermute | solution.py:1122
  78.3 33.3 %collective-permute-start.5 = (bf16[5,48,384]{2,1,0:T(8,128)(2,1)S(1)}, bf16[5,48,384]{2,1,0:T(8,128)(2,1)S(1)}, u32[]{:S(2)}, u32[]{:S(2)}) collective-permute-start(bf16[5,48,384]{2,1,0:T(8,128)(2,1)S(1)} %bitcast.99), channel_id=1, source_target_pairs={{0,2},{1,3},{2,0},{3,1},{4,6},{5,7},{6,4},{7,5},{8,10},{9,11},{10,... | collective-permute-start | bytes 552968 | tf_op jit(solution)/shard_map/ppermute | solution.py:1122
  79.6 32.1 %collective-permute-start.6 = (bf16[5,48,384]{2,1,0:T(8,128)(2,1)S(1)}, bf16[5,48,384]{2,1,0:T(8,128)(2,1)S(1)}, u32[]{:S(2)}, u32[]{:S(2)}) collective-permute-start(bf16[5,48,384]{2,1,0:T(8,128)(2,1)S(1)} %bitcast.100), channel_id=1, source_target_pairs={{0,3},{1,0},{2,1},{3,2},{4,7},{5,4},{6,5},{7,6},{8,11},{9,8},{10,9... | collective-permute-start | bytes 552968 | tf_op jit(solution)/shard_map/ppermute | solution.py:1122
  81.3 37.1 %collective-permute-start.3 = (bf16[4,4,3,48,384]{4,3,2,1,0:T(8,128)(2,1)}, bf16[4,4,3,48,384]{4,3,2,1,0:T(8,128)(2,1)}, u32[]{:S(2)}, u32[]{:S(2)}) collective-permute-start(bf16[4,4,3,48,384]{4,3,2,1,0:T(8,128)(2,1)} %copy-done.4), channel_id=1, source_target_pairs={{0,4},{4,0},{8,12},{12,8},{16,20},{20,16},{24,28},{28,24},{1,5},{5... | collective-permute-start | bytes 5308424 | tf_op jit(solution)/shard_map/ppermute | solution.py:1112
  114.1 39.1 %all-to-all-start.3 = ((bf16[4,4,5,48,384]{4,3,2,1,0:T(8,128)(2,1)}), bf16[4,4,5,48,384]{4,3,2,1,0:T(8,128)(2,1)S(1)}, u32[]{:S(2)}, u32[]{:S(2)}) async-start(bf16[4,4,5,48,384]{4,3,2,1,0:T(8,128)(2,1)} %broadcast_in_dim.59), calls=%async_computation.3 | async-start | bytes 5898240 | tf_op jit(solution)/shard_map/all_to_all | solution.py:1126
  238.7 15.8 %collective-permute-start.12 = (bf16[4,4,1,96,768]{4,3,2,1,0:T(8,128)(2,1)}, bf16[4,4,1,96,768]{4,3,2,1,0:T(8,128)(2,1)S(1)}, u32[]{:S(2)}, u32[]{:S(2)}) collective-permute-start(bf16[4,4,1,96,768]{4,3,2,1,0:T(8,128)(2,1)} %grad_of_rows.2), channel_id=1, source_target_pairs={{0,4},{4,0},{8,12},{12,8},{16,20},{20,16},{24,28},{28,24},{1,5},{5... | collective-permute-start | bytes 7077896 | tf_op jit(solution)/shard_map/ppermute | solution.py:1112
  252.5 16.7 %collective-permute-start.13 = (bf16[4,4,5,48,384]{4,3,2,1,0:T(8,128)(2,1)}, bf16[4,4,5,48,384]{4,3,2,1,0:T(8,128)(2,1)}, u32[]{:S(2)}, u32[]{:S(2)}) collective-permute-start(bf16[4,4,5,48,384]{4,3,2,1,0:T(8,128)(2,1)} %grad_of_wide.2), channel_id=1, source_target_pairs={{0,4},{4,0},{8,12},{12,8},{16,20},{20,16},{24,28},{28,24},{1,5},{5... | collective-permute-start | bytes 8847368 | tf_op jit(solution)/shard_map/ppermute | solution.py:1112
  265.5 58.7 %all-to-all-start.4 = ((bf16[4,4,1,96,768]{4,3,2,1,0:T(8,128)(2,1)}), bf16[4,4,1,96,768]{4,3,2,1,0:T(8,128)(2,1)S(1)}, u32[]{:S(2)}, u32[]{:S(2)}) async-start(bf16[4,4,1,96,768]{4,3,2,1,0:T(8,128)(2,1)} %grad_of_rows.3), calls=%async_computation.4 | async-start | bytes 4718592 | tf_op jit(solution)/shard_map/all_to_all | solution.py:1126
  323.7 41.9 %collective-permute-start.14 = (bf16[4,4,3,48,384]{4,3,2,1,0:T(8,128)(2,1)}, bf16[4,4,3,48,384]{4,3,2,1,0:T(8,128)(2,1)}, u32[]{:S(2)}, u32[]{:S(2)}) collective-permute-start(bf16[4,4,3,48,384]{4,3,2,1,0:T(8,128)(2,1)} %grad_of_columns.2), channel_id=1, source_target_pairs={{0,4},{4,0},{8,12},{12,8},{16,20},{20,16},{24,28},{28,24},{1,5},{5... | collective-permute-start | bytes 5308424 | tf_op jit(solution)/shard_map/ppermute | solution.py:1112
  325.5 55.2 %collective-permute-start.15 = (bf16[1,96,768]{2,1,0:T(8,128)(2,1)}, bf16[1,96,768]{2,1,0:T(8,128)(2,1)S(1)}, u32[]{:S(2)}, u32[]{:S(2)}) collective-permute-start(bf16[1,96,768]{2,1,0:T(8,128)(2,1)} %get-tuple-element.122), channel_id=1, source_target_pairs={{0,1},{1,2},{2,3},{3,0},{4,5},{5,6},{6,7},{7,4},{8,9},{9,10},{10,1... | collective-permute-start | bytes 442376 | tf_op jit(solution)/shard_map/ppermute | solution.py:1122
  326.4 54.3 %collective-permute-start.16 = (bf16[1,96,768]{2,1,0:T(8,128)(2,1)S(1)}, bf16[1,96,768]{2,1,0:T(8,128)(2,1)}, u32[]{:S(2)}, u32[]{:S(2)}) collective-permute-start(bf16[1,96,768]{2,1,0:T(8,128)(2,1)S(1)} %get-tuple-element.121), channel_id=1, source_target_pairs={{0,2},{1,3},{2,0},{3,1},{4,6},{5,7},{6,4},{7,5},{8,10},{9,11},{10,... | collective-permute-start | bytes 442376 | tf_op jit(solution)/shard_map/ppermute | solution.py:1122
  328.0 52.7 %collective-permute-start.17 = (bf16[1,96,768]{2,1,0:T(8,128)(2,1)S(1)}, bf16[1,96,768]{2,1,0:T(8,128)(2,1)}, u32[]{:S(2)}, u32[]{:S(2)}) collective-permute-start(bf16[1,96,768]{2,1,0:T(8,128)(2,1)S(1)} %get-tuple-element.120), channel_id=1, source_target_pairs={{0,3},{1,0},{2,1},{3,2},{4,7},{5,4},{6,5},{7,6},{8,11},{9,8},{10,9... | collective-permute-start | bytes 442376 | tf_op jit(solution)/shard_map/ppermute | solution.py:1122
  329.6 45.1 %all-to-all-start.5 = ((bf16[4,4,5,48,384]{4,3,2,1,0:T(8,128)(2,1)}), bf16[4,4,5,48,384]{4,3,2,1,0:T(8,128)(2,1)S(1)}, u32[]{:S(2)}, u32[]{:S(2)}) async-start(bf16[4,4,5,48,384]{4,3,2,1,0:T(8,128)(2,1)} %grad_of_wide.3), calls=%async_computation.5 | async-start | bytes 5898240 | tf_op jit(solution)/shard_map/all_to_all | solution.py:1126
  376.1 32.2 %all-to-all-start.6 = ((bf16[4,4,3,48,384]{4,3,2,1,0:T(8,128)(2,1)}), bf16[4,4,3,48,384]{4,3,2,1,0:T(8,128)(2,1)S(1)}, u32[]{:S(2)}, u32[]{:S(2)}) async-start(bf16[4,4,3,48,384]{4,3,2,1,0:T(8,128)(2,1)} %grad_of_columns.3), calls=%async_computation.6 | async-start | bytes 3538944 | tf_op jit(solution)/shard_map/all_to_all | solution.py:1126
  383.4 25.4 %collective-permute-start.18 = (bf16[5,48,384]{2,1,0:T(8,128)(2,1)}, bf16[5,48,384]{2,1,0:T(8,128)(2,1)S(1)}, u32[]{:S(2)}, u32[]{:S(2)}) collective-permute-start(bf16[5,48,384]{2,1,0:T(8,128)(2,1)} %get-tuple-element.119), channel_id=1, source_target_pairs={{0,1},{1,2},{2,3},{3,0},{4,5},{5,6},{6,7},{7,4},{8,9},{9,10},{10,1... | collective-permute-start | bytes 552968 | tf_op jit(solution)/shard_map/ppermute | solution.py:1122
  384.1 24.7 %collective-permute-start.19 = (bf16[5,48,384]{2,1,0:T(8,128)(2,1)S(1)}, bf16[5,48,384]{2,1,0:T(8,128)(2,1)S(1)}, u32[]{:S(2)}, u32[]{:S(2)}) collective-permute-start(bf16[5,48,384]{2,1,0:T(8,128)(2,1)S(1)} %get-tuple-element.118), channel_id=1, source_target_pairs={{0,2},{1,3},{2,0},{3,1},{4,6},{5,7},{6,4},{7,5},{8,10},{9,11},{10,... | collective-permute-start | bytes 552968 | tf_op jit(solution)/shard_map/ppermute | solution.py:1122
  385.4 23.4 %collective-permute-start.20 = (bf16[5,48,384]{2,1,0:T(8,128)(2,1)S(1)}, bf16[5,48,384]{2,1,0:T(8,128)(2,1)S(1)}, u32[]{:S(2)}, u32[]{:S(2)}) collective-permute-start(bf16[5,48,384]{2,1,0:T(8,128)(2,1)S(1)} %get-tuple-element.117), channel_id=1, source_target_pairs={{0,3},{1,0},{2,1},{3,2},{4,7},{5,4},{6,5},{7,6},{8,11},{9,8},{10,9... | collective-permute-start | bytes 552968 | tf_op jit(solution)/shard_map/ppermute | solution.py:1122
  409.6 20.2 %all-to-all-start.7 = ((f32[8,15,768]{2,1,0:T(8,128)}), f32[8,15,768]{2,1,0:T(8,128)S(1)}, u32[]{:S(2)}, u32[]{:S(2)}) async-start(f32[8,15,768]{2,1,0:T(8,128)} %broadcast_in_dim.65), calls=%async_computation.7 | async-start | bytes 786432 | tf_op jit(solution)/shard_map/all_to_all | solution.py:1251
  413.9 11.6 %collective-permute-start.22 = (bf16[3,48,384]{2,1,0:T(8,128)(2,1)S(1)}, bf16[3,48,384]{2,1,0:T(8,128)(2,1)S(1)}, u32[]{:S(2)}, u32[]{:S(2)}) collective-permute-start(bf16[3,48,384]{2,1,0:T(8,128)(2,1)S(1)} %get-tuple-element.126), channel_id=1, source_target_pairs={{0,2},{1,3},{2,0},{3,1},{4,6},{5,7},{6,4},{7,5},{8,10},{9,11},{10,... | collective-permute-start | bytes 331784 | tf_op jit(solution)/shard_map/ppermute | solution.py:1122
  429.8 32.3 %all-to-all-start.8 = ((bf16[8,192,384]{2,1,0:T(8,128)(2,1)}), bf16[8,192,384]{2,1,0:T(8,128)(2,1)S(1)}, u32[]{:S(2)}, u32[]{:S(2)}) async-start(bf16[8,192,384]{2,1,0:T(8,128)(2,1)} %get-tuple-element.102), calls=%async_computation.8 | async-start | bytes 2359296 | tf_op jit(solution)/shard_map/all_to_all | solution.py:1381
  435.4 14.6 %collective-permute-start.25 = (f32[8,128]{1,0:T(8,128)S(1)}, f32[8,128]{1,0:T(8,128)S(1)}, u32[]{:S(2)}, u32[]{:S(2)}) collective-permute-start(f32[8,128]{1,0:T(8,128)S(1)} %add.96), channel_id=1, source_target_pairs={{0,8},{4,12},{8,0},{12,4},{16,24},{20,28},{24,16},{28,20},{1,9},{5... | collective-permute-start | bytes 12296 | tf_op jit(solution)/shard_map/ppermute | solution.py:1112
  (29 other events, 203.8 us)

commit v3 on v2

--- a/solution.py
+++ b/solution.py
@@ -46,7 +46,7 @@
     return lax.rem(here - place + narrow, narrow) if narrow > 1 else 0
 
 
-anywhere = pl.BlockSpec(memory_space=pl.ANY)
+anywhere = pl.BlockSpec(memory_space=pltpu.HBM)
 
 
 def copies_in_order(source, target, here, semaphores):
@@ -64,10 +64,15 @@
     return found
 
 
-def bring(sources, targets, here, semaphores):
+def all_copies(sources, targets, here, semaphores):
     found = []
     for index, (source, target) in enumerate(zip(sources, targets)):
         found += copies_in_order(source, target, here, semaphores.at[index])
+    return found
+
+
+def bring(sources, targets, here, semaphores):
+    found = all_copies(sources, targets, here, semaphores)
     for copy in found:
         copy.start()
     for copy in found:
@@ -89,7 +94,7 @@
     return jnp.concatenate([ref[part] for part in parts], axis=1)
 
 
-def params(limit=56):
+def params(limit=62):
     return pltpu.CompilerParams(vmem_limit_bytes=limit * 2**20)
 
 
@@ -183,9 +188,9 @@
                 columns = slice(start, start + PAIR)
                 result = projected[:, columns]
                 if part < 2:
-                    result = turn(result, cos, sin).astype(low)
+                    result = turn(result, cos, sin)
                 if part == 0:
-                    result = result.astype(full) * HEAD_DIM**-0.5
+                    result = result * HEAD_DIM**-0.5
                 out_ref[rows, columns] = result.astype(low)
 
 
@@ -343,22 +348,33 @@
     return pl.BlockSpec((ROWS, PAIR), lambda g, *_: (0, offset + g))
 
 
-pair_spec = pl.BlockSpec((ROWS, PAIR), lambda g, scalars: (0, scalars[1] + g))
-log_spec = pl.BlockSpec((1, 2, ROWS), lambda g, scalars: (scalars[1] + g, 0, 0))
+def pair_spec_from(first):
+    return pl.BlockSpec((ROWS, PAIR), lambda g, scalars: (0, scalars[1] + first + g))
+
+
+def log_spec_from(first):
+    return pl.BlockSpec((1, 2, ROWS), lambda g, scalars: (scalars[1] + first + g, 0, 0))
+
+
+pair_spec = pair_spec_from(0)
+log_spec = log_spec_from(0)
 PAIRS_SEEN = 1572864
 
 
-def attend(scalars, qkv, before):
+def attend(scalars, qkv, before, first=0, count=None):
     pairs = qkv.shape[1] // (3 * PAIR)
+    count = count or pairs
     aliased = before is not None
     kept = [pl.BlockSpec(memory_space=pl.ANY)] * 2 if aliased else []
     return pl.pallas_call(
         partial(attend_kernel, aliased),
         grid_spec=pltpu.PrefetchScalarGridSpec(
             num_scalar_prefetch=1,
-            grid=(pairs,),
-            in_specs=[column_spec(0), column_spec(pairs), column_spec(2 * pairs), *kept],
-            out_specs=[pair_spec, log_spec],
+            grid=(count,),
+            in_specs=[
+                column_spec(first), column_spec(pairs + first), column_spec(2 * pairs + first), *kept
+            ],
+            out_specs=[pair_spec_from(first), log_spec_from(first)],
             scratch_shapes=bias_scratch,
         ),
         out_shape=[
@@ -367,8 +383,8 @@
         ],
         input_output_aliases={4: 0, 5: 1} if aliased else {},
         cost_estimate=pl.CostEstimate(
-            flops=16 * PAIRS_SEEN * PAIR * pairs,
-            bytes_accessed=8 * ROWS * PAIR * pairs,
+            flops=16 * PAIRS_SEEN * PAIR * count,
+            bytes_accessed=8 * ROWS * PAIR * count,
             transcendentals=0,
         ),
         compiler_params=params(),
@@ -377,10 +393,16 @@
 
 
 def attend_back_kernel(
-    scalar_ref, q_ref, k_ref, v_ref, o_ref, grad_ref, log_ref, cos_ref, sin_ref,
-    grad_out_ref, q_acc, k_acc, v_acc, delta_acc, prob_ref, score_ref, own_prob_ref,
-    own_score_ref, *biases
+    weighted, scalar_ref, q_ref, k_ref, v_ref, o_ref, grad_ref, log_ref, cos_ref, sin_ref, *refs
 ):
+    a_ref, weight_ref = None, None
+    if weighted:
+        a_ref, grad_out_ref, weight_ref, *refs = refs
+    else:
+        grad_out_ref, *refs = refs
+    q_acc, k_acc, v_acc, delta_acc, prob_ref, score_ref, own_prob_ref, own_score_ref = refs[:8]
+    biases = refs[8:]
+
     @pl.when(pl.program_id(0) == 0)
     def _():
         fill_bias(scalar_ref[0], *biases)
@@ -466,21 +488,39 @@
         grad_out_ref[0, rows, :] = turn(q_acc[rows, :] * HEAD_DIM**-0.5, cos, sin).astype(low)
         grad_out_ref[1, rows, :] = turn(k_acc[rows, :], cos, sin).astype(low)
         grad_out_ref[2, rows, :] = v_acc[rows, :].astype(low)
-
-
-def attend_back(scalars, qkv, attended, grad, logs, cos, sin):
+    if weighted:
+        parts = jnp.concatenate([grad_out_ref[part] for part in range(3)], axis=1)
+        result = dot(a_ref[...], parts, 0, 0) * row_scale
+        planes, narrow, _, rows, _ = weight_ref.shape
+        for place in range(narrow):
+            for plane in range(planes):
+                start = (place * planes + plane) * rows
+                for part in range(3):
+                    block = result[start : start + rows, part * PAIR : (part + 1) * PAIR]
+                    weight_ref[plane, place, part] = block.astype(low)
+
+
+def attend_back(scalars, qkv, attended, grad, logs, cos, sin, attn_in=None, blocks=None):
     pairs = qkv.shape[1] // (3 * PAIR)
     table = whole((SEQ, PAIR))
+    weighted = attn_in is not None
+    out_specs = [pl.BlockSpec((3, ROWS, PAIR), lambda g, *_: (0, 0, g))]
+    out_shape = [jax.ShapeDtypeStruct((3, ROWS, pairs * PAIR), low)]
+    if weighted:
+        shape = (*blocks, 3, D // (blocks[0] * blocks[1]))
+        out_specs.append(pl.BlockSpec((*shape, PAIR), lambda g, *_: (0, 0, 0, 0, g)))
+        out_shape.append(jax.ShapeDtypeStruct((*shape, pairs * PAIR), low))
     return pl.pallas_call(
-        attend_back_kernel,
+        partial(attend_back_kernel, weighted),
         grid_spec=pltpu.PrefetchScalarGridSpec(
             num_scalar_prefetch=1,
             grid=(pairs,),
             in_specs=[
                 column_spec(0), column_spec(pairs), column_spec(2 * pairs),
                 pair_spec, pair_spec, log_spec, table, table,
+                *([whole((ROWS, D))] if weighted else []),
             ],
-            out_specs=pl.BlockSpec((3, ROWS, PAIR), lambda g, *_: (0, 0, g)),
+            out_specs=out_specs,
             scratch_shapes=[
                 pltpu.VMEM((ROWS, PAIR), full),
                 pltpu.VMEM((ROWS, PAIR), full),
@@ -493,7 +533,7 @@
                 *bias_scratch,
             ],
         ),
-        out_shape=jax.ShapeDtypeStruct((3, ROWS, pairs * PAIR), low),
+        out_shape=out_shape,
         cost_estimate=pl.CostEstimate(
             flops=40 * PAIRS_SEEN * PAIR * pairs,
             bytes_accessed=16 * ROWS * PAIR * pairs,
@@ -501,7 +541,10 @@
         ),
         compiler_params=params(),
         name="attend_back",
-    )(scalars, qkv, qkv, qkv, attended, grad, logs, cos, sin)
+    )(
+        scalars, qkv, qkv, qkv, attended, grad, logs, cos, sin,
+        *([attn_in] if weighted else []),
+    )
 
 
 root_two_pi = 0.7978845608028654
@@ -522,16 +565,21 @@
     y_ref, b_ref, gl_ref, du_ref, dr_ref, drb_ref, do_ref, sums_ref, upsum_ref,
     wide_mine, wide_other, down_mine, down_other, semaphores
 ):
+    copies = all_copies(
+        [wide_mine_hbm, wide_other_hbm, down_mine_hbm, down_other_hbm],
+        [wide_mine, wide_other, down_mine, down_other],
+        side_ref[1],
+        semaphores,
+    )
+
     @pl.when(pl.program_id(0) == 0)
     def _():
+        for copy in copies:
+            copy.start()
         sums_ref[...] = jnp.zeros_like(sums_ref)
         upsum_ref[...] = jnp.zeros_like(upsum_ref)
-        bring(
-            [wide_mine_hbm, wide_other_hbm, down_mine_hbm, down_other_hbm],
-            [wide_mine, wide_other, down_mine, down_other],
-            side_ref[1],
-            semaphores,
-        )
+        for copy in copies[: len(copies) // 2]:
+            copy.wait()
 
     swapped = side_ref[0] == 1
     gain = vec_ref[1:2, :]
@@ -614,6 +662,12 @@
         ).astype(low)
 
     state = head(0)
+
+    @pl.when(pl.program_id(0) == 0)
+    def _():
+        for copy in copies[len(copies) // 2 :]:
+            copy.wait()
+
     for sub in range(subs):
         normed, scaling, mlp_in, result = state
         result, back = main(sub, mlp_in, result)
@@ -943,12 +997,12 @@
         cost_estimate=pl.CostEstimate(
             flops=D * D, bytes_accessed=6 * D * D, transcendentals=0
         ),
-        compiler_params=params(),
+        compiler_params=params(16),
         name="pack",
     )(owners, slot)
 
 
-def settle_kernel(owners_ref, qkv_ref, wide_ref, down_ref, out_ref, square_ref):
+def settle_kernel(owners_ref, qkv_ref, wide_ref, down_ref, out_ref):
     squares = jnp.zeros((8, HALF), full)
 
     def summed(ref, part):
@@ -974,42 +1028,114 @@
                 out_ref[target, start : start + rows, :] = block
                 entries = block.astype(full)
                 squares = squares + eight_rows(entries * entries)
-    square_ref[...] = jnp.broadcast_to(jnp.sum(squares, keepdims=True), square_ref.shape)
+    rest = jnp.sum(squares, keepdims=True)
+    rows = out_ref.shape[1] - 16
+    for index in range(3):
+        term = rest.astype(low)
+        rest = rest - term.astype(full)
+        terms = jnp.broadcast_to(term, (16, LANES))
+        columns = slice(index * LANES, (index + 1) * LANES)
+        for target in range(out_ref.shape[0]):
+            out_ref[target, rows:, columns] = terms
+
+
+def square_sums_kernel(came_ref, vec_ref, out_ref):
+    total = jnp.zeros((1, LANES), full)
+    for source in range(came_ref.shape[0]):
+        for index in reversed(range(3)):
+            columns = slice(index * LANES, (index + 1) * LANES)
+            total = total + came_ref[source, :, columns].astype(full)[0:1]
+    out_ref[0:VROWS, :] = vec_ref[...]
+    out_ref[VROWS:, :] = jnp.concatenate([total] * (D // LANES), axis=1)
+
+
+def square_sums(came, vec_wide):
+    wide, rows, _ = came.shape
+    return pl.pallas_call(
+        square_sums_kernel,
+        grid=(1,),
+        in_specs=[
+            pl.BlockSpec((wide, 16, HALF), lambda i: (0, rows // 16 - 1, 0)),
+            whole((VROWS, D)),
+        ],
+        out_specs=whole((VROWS + 1, D)),
+        out_shape=jax.ShapeDtypeStruct((VROWS + 1, D), full),
+        compiler_params=params(16),
+        name="square_sums",
+    )(came, vec_wide)
 
 
 def settle(owners, qkv, wide_parts, down):
     wide = lax.axis_size("wide")
-    shape = (wide, 2 * D // wide, HALF)
+    shape = (wide, 2 * D // wide + 16, HALF)
     return pl.pallas_call(
         settle_kernel,
         grid_spec=pltpu.PrefetchScalarGridSpec(
             num_scalar_prefetch=1,
             grid=(1,),
             in_specs=[whole(qkv.shape), whole(wide_parts.shape), whole(down.shape)],
-            out_specs=[whole(shape), whole((8, 128))],
-        ),
-        out_shape=[jax.ShapeDtypeStruct(shape, low), jax.ShapeDtypeStruct((8, 128), full)],
+            out_specs=whole(shape),
+        ),
+        out_shape=jax.ShapeDtypeStruct(shape, low),
         cost_estimate=pl.CostEstimate(
             flops=4 * D * D, bytes_accessed=6 * D * D, transcendentals=0
         ),
-        compiler_params=params(),
+        compiler_params=params(16),
         name="settle",
     )(owners, qkv, wide_parts, down)
 
 
 FINISH_ROWS = 192
+held = pl.BlockSpec(memory_space=pltpu.VMEM)
+
+
+def unpack_kernel(owners_ref, came_ref, out_ref, grad_ref):
+    place = lax.axis_index("wide")
+    wide = came_ref.shape[0]
+    for kind in range(4):
+
+        @pl.when(owners_ref[kind] == place)
+        def _(kind=kind):
+            for source, part, start, rows, where, column in slot_pieces(kind, wide):
+                block = came_ref[source, start : start + rows, :].astype(full)
+                for index in range(HALF // LANES):
+                    piece = block[:, index * LANES : (index + 1) * LANES]
+                    if kind == 0 and part < 2:
+                        piece = swapped_halves(piece)
+                    grad_ref[column // LANES + index, where, :] = piece
+
+    for index in range(D // LANES):
+        out_ref[:, index * LANES : (index + 1) * LANES] = grad_ref[index]
+
+
+def unpack(owners, slot_rows, came):
+    return pl.pallas_call(
+        unpack_kernel,
+        grid_spec=pltpu.PrefetchScalarGridSpec(
+            num_scalar_prefetch=1,
+            grid=(1,),
+            in_specs=[whole(came.shape)],
+            out_specs=held,
+            scratch_shapes=[pltpu.VMEM((D // LANES, slot_rows, LANES), full)],
+        ),
+        out_shape=jax.ShapeDtypeStruct((slot_rows, D), full),
+        cost_estimate=pl.CostEstimate(
+            flops=2 * D * D, bytes_accessed=6 * D * D, transcendentals=0
+        ),
+        compiler_params=params(16),
+        name="unpack",
+    )(owners, came)
 
 
 def finish_kernel(
-    plain, owners_ref, came_ref, sums_ref, vec_moment_ref, vec_square_ref, vec_master_ref,
+    owners_ref, grad_ref, sums_ref, vec_moment_ref, vec_square_ref, vec_master_ref,
     moment_ref, square_ref, master_ref,
     master_out, moment_out, square_out, vec_grad_out, vec_moment_out, vec_square_out,
-    vec_master_out, norm_out, grad_ref
+    vec_master_out, norm_out
 ):
     step = pl.program_id(0)
     place = lax.axis_index("wide")
     here = lax.axis_index("narrow")
-    wide = came_ref.shape[0]
     narrow = sums_ref.shape[0]
     total = sums_ref[here]
     for index in range(1, narrow):
@@ -1020,20 +1146,6 @@
 
     @pl.when(step == 0)
     def _():
-        if plain:
-            grad_ref[...] = came_ref[...]
-        for kind in range(0 if plain else 4):
-
-            @pl.when(owners_ref[kind] == place)
-            def _(kind=kind):
-                for source, part, start, rows, where, column in slot_pieces(kind, wide):
-                    block = came_ref[source, start : start + rows, :].astype(full)
-                    for index in range(HALF // LANES):
-                        piece = block[:, index * LANES : (index + 1) * LANES]
-                        if kind == 0 and part < 2:
-                            piece = swapped_halves(piece)
-                        grad_ref[column // LANES + index, where, :] = piece
-
         norm_out[...] = norm
         vec_clipped = vec * clip
         vec_grad_out[...] = vec_clipped
@@ -1047,42 +1159,38 @@
         rows = D // 4 * (PARTS[kind] if kind < 3 else 4)
         used = jnp.where(owners_ref[kind] == place, rows, used)
     row = step * FINISH_ROWS + lax.broadcasted_iota(jnp.int32, (FINISH_ROWS, D), 0)
-    start = pl.multiple_of(step * FINISH_ROWS, FINISH_ROWS)
-    grad = jnp.concatenate(
-        [grad_ref[index, pl.ds(start, FINISH_ROWS), :] for index in range(D // LANES)], axis=1
-    )
+    rows = pl.ds(pl.multiple_of(step * FINISH_ROWS, FINISH_ROWS), FINISH_ROWS)
+    kept = row < used
     moment_new, square_new, master_new = adam(
-        grad * clip,
-        moment_ref[...], square_ref[...], master_ref[...], decay_rate, learn_rate,
-    )
-    kept = row < used
+        jnp.where(kept, grad_ref[rows, :] * clip, 0.0),
+        moment_ref[rows, :], square_ref[rows, :], master_ref[rows, :], decay_rate, learn_rate,
+    )
     master_out[...] = jnp.where(kept, master_new, 0.0)
     moment_out[...] = jnp.where(kept, moment_new, 0.0)
     square_out[...] = jnp.where(kept, square_new, 0.0)
 
 
-def finish(plain, owners, came, sums, vec_states, states):
+def finish(owners, grad, sums, vec_states, states):
     rows = states[0].shape[0]
     state_spec = pl.BlockSpec((FINISH_ROWS, D), lambda i, *_: (i, 0))
     vec_spec = whole((VROWS, D))
     state = jax.ShapeDtypeStruct((rows, D), full)
     vec = jax.ShapeDtypeStruct((VROWS, D), full)
     return pl.pallas_call(
-        partial(finish_kernel, plain),
+        finish_kernel,
         grid_spec=pltpu.PrefetchScalarGridSpec(
             num_scalar_prefetch=1,
             grid=(rows // FINISH_ROWS,),
-            in_specs=[whole(came.shape), whole(sums.shape), *[vec_spec] * 3, *[state_spec] * 3],
+            in_specs=[held, held, *[vec_spec] * 3, *[held] * 3],
             out_specs=[*[state_spec] * 3, *[vec_spec] * 4, whole((1, 1))],
-            scratch_shapes=[pltpu.VMEM((D // LANES, rows, LANES), full)],
         ),
         out_shape=[state] * 3 + [vec] * 4 + [jax.ShapeDtypeStruct((1, 1), full)],
         cost_estimate=pl.CostEstimate(
             flops=20 * D * D, bytes_accessed=26 * D * D, transcendentals=0
         ),
-        compiler_params=params(),
+        compiler_params=params(24),
         name="finish",
-    )(owners, came, sums, *vec_states, *states)
+    )(owners, grad, sums, *vec_states, *states)
 
 
 def turn_tables():
@@ -1230,12 +1338,11 @@
         squares = squares + jnp.sum(jnp.square(share.astype(full)))
         block = jnp.pad(share, ((0, sent.shape[1] - share.shape[0]), (0, 0)))[None]
         sent = jnp.where(places == owners[kind], block, sent)
-    return sent, jnp.broadcast_to(squares, (8, 128))
+    return sent, jnp.broadcast_to(squares, (1, D))
 
 
 def plain_unpack(kind, slot_rows, came):
-    slot = lax.switch(kind, plain_layouts(slot_rows)[1], came).astype(full)
-    return jnp.swapaxes(slot.reshape(slot_rows, D // LANES, LANES), 0, 1)
+    return lax.switch(kind, plain_layouts(slot_rows)[1], came).astype(full)
 
 
 def sum_over_wide(value):
@@ -1245,10 +1352,6 @@
         value = value + flip(value, "wide", bit)
         bit *= 2
     return value
-
-
-def vectors_over_wide(value):
-    return jnp.sum(lax.all_to_all(copies(value, lax.axis_size("wide")), "wide", 0, 0), axis=0)
 
 
 def local(
@@ -1280,14 +1383,10 @@
         packed = pack(owners, master_slots[0])
     came = lax.all_to_all(packed, "wide", 0, 0)
 
-    def share(kind, count):
+    def share(came, kind, count):
         return lax.dynamic_index_in_dim(came, owners[kind], 0, keepdims=False)[:count]
 
-    qkv_share = share(0, 3 * rows).reshape(3, rows, HALF)
-    wide_share = jnp.concatenate([share(2, 4 * rows), share(1, rows)])
-    wide_share = wide_share.reshape(UP_ROWS + 1, rows, HALF)
-    down_share = share(3, 2 * deep)
-    down_share = jnp.concatenate([down_share[:deep], down_share[deep:]], axis=1)[None]
+    qkv_share = share(came, 0, 3 * rows).reshape(3, rows, HALF)
 
     tokens = tokens.reshape(ROWS, D)
     cotangent = cotangent.reshape(ROWS, D)
@@ -1305,17 +1404,24 @@
 
     qkv_plane = gather_narrow(after(qkv_share, attn_in, cos, sin, bias, *scalars))
     qkv_mine = gather_planes(qkv_plane)
-    down_plane = gather_narrow(after(down_share, *qkv_plane))
+    came = after(came, *qkv_plane)
+    down_share = share(came, 3, 2 * deep)
+    down_share = jnp.concatenate([down_share[:deep], down_share[deep:]], axis=1)[None]
+    down_plane = gather_narrow(down_share)
+    wide_share = jnp.concatenate([share(came, 2, 4 * rows), share(came, 1, rows)])
+    wide_share = wide_share.reshape(UP_ROWS + 1, rows, HALF)
+    wide_plane = gather_narrow(after(wide_share, *down_plane))
     qkv_other = flip(qkv_mine, "wide", 1)
     heads_mine = project(here, attn_in, qkv_mine, cos, sin)
     down_mine = gather_planes(after(down_plane, qkv_mine))
-    wide_plane = gather_narrow(after(wide_share, qkv_mine))
-    before = attend(scalars[0], heads_mine, None)
+    before = attend(scalars[0], heads_mine, None, 0, 1)
     wide_mine = gather_planes(after(wide_plane, before[0], down_mine))
+    before = attend(scalars[0], heads_mine, before, 1, 2)
     down_other = flip(after(down_mine, before[0]), "wide", 1)
     heads_other = project(here, after(attn_in, before[0]), qkv_other, cos, sin)
-    attended, logs = attend(scalars[1], heads_other, before)
-    wide_other = flip(after(wide_mine, attended), "wide", 1)
+    before = attend(scalars[1], heads_other, before, 0, 2)
+    wide_other = flip(after(wide_mine, before[0]), "wide", 1)
+    attended, logs = attend(scalars[1], heads_other, before, 2, 1)
     output, mlp_in, act, pre_grad, resid_grad, resid_low, attended_grad, sums, up_sums = feed(
         levels,
         here,
@@ -1338,23 +1444,24 @@
     wide_grad = grad_of_wide(
         blocks, mlp_in, after(pre_grad, down_grad), 0, attended, resid_low, side, wide_came
     )
-    grad_other = attend_back(
-        scalars[1], heads_other, attended, after(attended_grad, wide_grad), logs, cos, sin
+    grad_other, qkv_theirs = attend_back(
+        scalars[1], heads_other, attended, after(attended_grad, wide_grad), logs, cos, sin,
+        attn_in, blocks,
     )
     wide_planes = reduce_planes(after(wide_grad, down_planes))
     down_pieces = narrow_pieces(down_planes)
-    qkv_theirs = grad_of_columns(blocks, attn_in, grad_other, 0, 3)
-    grad_mine = attend_back(
+    (grad_mine,) = attend_back(
         scalars[0], heads_mine, attended, after(attended_grad, qkv_theirs, down_planes), logs, cos, sin
     )
     qkv_grad = grad_of_columns(
-        blocks, attn_in, grad_mine, 0, 3, flip(qkv_theirs, "wide", 1)
-    )
-    wide_pieces = narrow_pieces(after(wide_planes, qkv_grad, *down_pieces))
+        blocks, attn_in, after(grad_mine, wide_planes, *down_pieces), 0, 3,
+        flip(qkv_theirs, "wide", 1),
+    )
+    wide_pieces = narrow_pieces(after(wide_planes, *down_pieces))
     qkv_planes = reduce_planes(after(qkv_grad, wide_planes))
     input_grad, gain_sums, table_grad = entry(
         levels, here, tokens, resid_grad, vec_master,
-        (after(grad_mine, qkv_grad, wide_planes, *down_pieces), grad_other),
+        (after(grad_mine, qkv_grad, *wide_pieces), grad_other),
         (qkv_mine, qkv_other),
     )
     qkv_pieces = narrow_pieces(after(qkv_planes, input_grad, *wide_pieces))
@@ -1374,20 +1481,25 @@
         )
         * row_scale
     )
-    vec_wide = vectors_over_wide(after(vec_local, qkv_planes))
-    sent, squares = (plain_settle if plain else settle)(
-        owners, jnp.stack(qkv_pieces), jnp.stack(wide_pieces), jnp.stack(down_pieces)
-    )
-    came = lax.all_to_all(after(sent, vec_wide), "wide", 0, 0)
+    pieces = [jnp.stack(part) for part in (qkv_pieces, wide_pieces, down_pieces)]
     if plain:
-        came = plain_unpack(kind, master_slots.shape[1], came)
-    squares = jnp.tile(sum_over_wide(squares)[:1], (1, D // LANES))
-    all_sums = jnp.stack(gather_narrow(jnp.concatenate([vec_wide, squares])))
+        sent, squares = plain_settle(owners, *pieces)
+        came = lax.all_to_all(sent, "wide", 0, 0)
+        slot_grad = plain_unpack(kind, master_slots.shape[1], came)
+        vec_sums = sum_over_wide(jnp.concatenate([vec_local, squares]))
+        all_sums = gather_narrow(vec_sums)
+    else:
+        vec_wide = sum_over_wide(vec_local)
+        sent = settle(owners, *pieces)
+        came = lax.all_to_all(after(sent, vec_wide), "wide", 0, 0)
+        all_sums = gather_narrow(square_sums(came, vec_wide))
+        slot_grad = unpack(owners, master_slots.shape[1], came)
+    all_sums = jnp.stack(all_sums)
     (
         master_new, moment_new, square_new,
         vec_grad, vec_moment_new, vec_square_new, vec_master_new, norm_value,
     ) = finish(
-        plain, owners, came, all_sums, (vec_moment, vec_square, vec_master),
+        owners, slot_grad, all_sums, (vec_moment, vec_square, vec_master),
         (moment_slots[0], square_slots[0], master_slots[0]),
     )
     return (

time: 480 us -> 463 us (0.965)
  waiting for transfers between devices: 58 us -> 30.6 us
  blocking collectives: 0 us -> 20.5 us
  local copies, waits for them, and re-layouts: 17.3 us -> 12.5 us
    ppermute x9, waiting for transfers between devices: 23.1 us -> 2.1 us  [flip(): return lax.ppermute(value, axis, [(i, i ^ bits) for i in range(count)])]
    all_to_all x0 -> x1, blocking collectives: none -> 20.5 us  [local(): came = lax.all_to_all(after(sent, vec_wide), 'wide', 0, 0)]
    pallas_call x4 -> x3, Pallas kernels: 36.5 us -> 28 us  [weight_call(): pl.pallas_call(partial(weight_kernel, added is not None), grid_spec=pltpu...]
    all_to_all x2 -> x0, starting transfers between devices: 8.42 us -> none  [the longest x1 4.23 us: local(): came = lax.all_to_all(after(sent, vec_wide), 'wide', 0, 0)]
    pallas_call x2 -> x4, Pallas kernels: 40.6 us -> 46.8 us  [attend(): pl.pallas_call(partial(attend_kernel, aliased), grid_spec=pltpu.PrefetchS...]
    pallas_call x3 -> x5, Pallas kernels: 74.2 us -> 78.9 us  [the longest x2 71.3 us: attend_back(): pl.pallas_call(partial(attend_back_kernel, weighted), grid_spec=pltpu.Pre...]
  transfers between devices with their start and end apart: 39 -> 37, of which waited for: 16 -> 12; matrix products, arithmetic and copies ran while one was open for 5% -> 5% of each run, Pallas kernels for 44% -> 46%
where the time goes in v3:
time: 463 us; the launch traced here: 456 us
  Pallas kernels  295 us (64%)
  starting transfers between devices  73 us (16%)
  waiting for transfers between devices  30.6 us (7%)
  blocking collectives  20.5 us (4%)
  other arithmetic  14.8 us (3%)
  local copies, waits for them, and re-layouts  12.5 us (3%)
  between operations  10.1 us (2%)
    pallas_call x2, Pallas kernels, attend_back(): pl.pallas_call(partial(attend_back_kernel, weighted), grid_spec=pltpu.Pre...  71.3 us
    pallas_call x1, Pallas kernels, feed(): pl.pallas_call(feed_kernel, grid_spec=pltpu.PrefetchScalarGridSpec(num_sc...  64.8 us
    pallas_call x4, Pallas kernels, attend(): pl.pallas_call(partial(attend_kernel, aliased), grid_spec=pltpu.PrefetchS...  46.8 us
    ppermute x21, starting transfers between devices, shift(): lax.ppermute(value, 'narrow', [(i, (i + step) % count) for i in range(cou...  34.7 us
    pallas_call x3, Pallas kernels, weight_call(): pl.pallas_call(partial(weight_kernel, added is not None), grid_spec=pltpu...  28 us
    all_to_all x6, starting transfers between devices, swap_planes(): lax.all_to_all(blocks, 'wide', 0, 0, axis_index_groups=planes_groups())  27.5 us
    pallas_call x2, Pallas kernels, grad_of_wide(): pl.pallas_call(partial(wide_kernel, added is not None), grid_spec=pltpu.P...  26.8 us
    ppermute x21, waiting for transfers between devices, shift(): lax.ppermute(value, 'narrow', [(i, (i + step) % count) for i in range(cou...  22.5 us
  transfers between devices with their start and end apart: 37, of which 12 were waited for; matrix products, arithmetic and copies ran while one was open for 5% of the time, Pallas kernels for 46%

profile of v3, /device:TPU:0, one launch (start us, length us, event | category | flops | bytes accessed | tf_op | source)
XLA Modules:
  0.0 456.1 jit_solution(17745978155539487586)
XLA Ops:
  5.1 4.8 %all-to-all-start = ((bf16[8,192,384]{2,1,0:T(8,128)(2,1)}), bf16[8,192,384]{2,1,0:T(8,128)(2,1)S(1)}, u32[]{:S(2)}, u32[]{:S(2)}) async-start(bf16[8,192,384]{2,1,0:T(8,128)(2,1)} %pack.1), calls=%async_computation | async-start | bytes 2359296 | tf_op jit(solution)/shard_map/all_to_all | solution.py:1384
  14.5 7.7 %norm_one.1.a_ref.refs_0_.x_ref = bf16[2048,768]{1,0:T(8,128)(2,1)} custom-call(s32[64]{0:T(128)} %bitcast.121, bf16[2048,768]{1,0:T(8,128)(2,1)} %bitcast.88, f32[15,768]{1,0:T(8,128)} %vec_master_ref.1), custom_call_target="tpu_custom_call" | custom-call | flops 15728640 | bytes 6291456 | tf_op jit(solution)/shard_map/norm_one/pallas_call | solution.py:150
  55.5 5.2 %collective-permute-done.5 = bf16[1,96,768]{2,1,0:T(8,128)(2,1)S(1)} collective-permute-done((bf16[1,96,768]{2,1,0:T(8,128)(2,1)S(1)}, bf16[1,96,768]{2,1,0:T(8,128)(2,1)S(1)}, u32[]{:S(2)}, u32[]{:S(2)}) %collective-permute-start.5) | collective-permute-done | bytes 147488 | tf_op jit(solution)/shard_map/ppermute | solution.py:1230
  60.7 5.8 %all-to-all-done.1.w_hbm.refs_2_ = bf16[4,4,3,48,384]{4,3,2,1,0:T(8,128)(2,1)} async-done(((bf16[4,4,3,48,384]{4,3,2,1,0:T(8,128)(2,1)}), bf16[4,4,3,48,384]{4,3,2,1,0:T(8,128)(2,1)}, u32[]{:S(2)}, u32[]{:S(2)}) %all-to-all-start.1) | async-done | bytes 1769504 | tf_op jit(solution)/shard_map/all_to_all | solution.py:1234
  83.0 10.1 %project.2.q_ref.k_ref.v_ref = bf16[2048,1152]{1,0:T(8,128)(2,1)} custom-call(s32[2]{0:T(128)} %pad_add_fusion.place_ref.side_ref, bf16[2048,768]{1,0:T(8,128)(2,1)} %norm_one.1.a_ref.refs_0_.x_ref, bf16[4,4,3,48,384]{4,3,2,1,0:T(8,128)(2,1)} %all-to-all-done.1.w_hbm.refs_2_, f32[1024,128]{1,0:T(8,128)} %get-tuple-element.147.cos_ref, ...), custom_call_target="tpu_custom_call" | custom-call | flops 3623878656 | bytes 12582912 | tf_op jit(solution)/shard_map/project/pallas_call | solution.py:202
  93.2 8.7 %attend.4 = (bf16[2048,768]{1,0:T(8,128)(2,1)}, f32[6,2,2048]{2,1,0:T(2,128)}) custom-call(s32[2]{0:T(128)} %get-tuple-element.146.scalar_ref, bf16[2048,1152]{1,0:T(8,128)(2,1)} %project.2.q_ref.k_ref.v_ref, bf16[2048,1152]{1,0:T(8,128)(2,1)} %project.2.q_ref.k_ref.v_ref, bf16[2048,1152]{1,0:T(8,128)(2,1)} %project.2.q_ref.k_ref.v_ref), custom_call_target="tpu_custom_call" | custom-call | flops 3221225472 | bytes 2097152 | tf_op jit(solution)/shard_map/attend/pallas_call | solution.py:369
  103.9 5.1 %all-to-all-start.3 = ((bf16[4,4,5,48,384]{4,3,2,1,0:T(8,128)(2,1)}), bf16[4,4,5,48,384]{4,3,2,1,0:T(8,128)(2,1)}, u32[]{:S(2)}, u32[]{:S(2)}) async-start(bf16[4,4,5,48,384]{4,3,2,1,0:T(8,128)(2,1)} %broadcast_in_dim.53), calls=%async_computation.3 | async-start | bytes 5898240 | tf_op jit(solution)/shard_map/all_to_all | solution.py:1234
  109.0 14.6 %attend.5 = (bf16[2048,768]{1,0:T(8,128)(2,1)}, f32[6,2,2048]{2,1,0:T(2,128)}) custom-call(s32[2]{0:T(128)} %get-tuple-element.146.scalar_ref, bf16[2048,1152]{1,0:T(8,128)(2,1)} %project.2.q_ref.k_ref.v_ref, bf16[2048,1152]{1,0:T(8,128)(2,1)} %project.2.q_ref.k_ref.v_ref, ...), custom_call_target="tpu_custom_call", output_to_operand_aliasing={{0}: (4, {}), {1}: (5, {})} | custom-call | flops 6442450944 | bytes 4194304 | tf_op jit(solution)/shard_map/attend/pallas_call | solution.py:369
  123.6 10.1 %project.3.q_ref.k_ref.v_ref = bf16[2048,1152]{1,0:T(8,128)(2,1)} custom-call(s32[2]{0:T(128)} %pad_add_fusion.place_ref.side_ref, bf16[2048,768]{1,0:T(8,128)(2,1)} %norm_one.1.a_ref.refs_0_.x_ref, bf16[4,4,3,48,384]{4,3,2,1,0:T(8,128)(2,1)} %collective-permute-done.3.w_hbm.refs_3_, f32[1024,128]{1,0:T(8,128)} %get-tuple-element.147.cos_ref, ...), custom_call_target="tpu_custom_call" | custom-call | flops 3623878656 | bytes 12582912 | tf_op jit(solution)/shard_map/project/pallas_call | solution.py:202
  133.7 14.8 %attend.6 = (bf16[2048,768]{1,0:T(8,128)(2,1)}, f32[6,2,2048]{2,1,0:T(2,128)}) custom-call(s32[2]{0:T(128)} %get-tuple-element.145.scalar_ref, bf16[2048,1152]{1,0:T(8,128)(2,1)} %project.3.q_ref.k_ref.v_ref, bf16[2048,1152]{1,0:T(8,128)(2,1)} %project.3.q_ref.k_ref.v_ref, ...), custom_call_target="tpu_custom_call", output_to_operand_aliasing={{0}: (4, {}), {1}: (5, {})} | custom-call | flops 6442450944 | bytes 4194304 | tf_op jit(solution)/shard_map/attend/pallas_call | solution.py:369
  149.9 8.7 %attend.7 = (bf16[2048,768]{1,0:T(8,128)(2,1)}, f32[6,2,2048]{2,1,0:T(2,128)}) custom-call(s32[2]{0:T(128)} %get-tuple-element.145.scalar_ref, bf16[2048,1152]{1,0:T(8,128)(2,1)} %project.3.q_ref.k_ref.v_ref, bf16[2048,1152]{1,0:T(8,128)(2,1)} %project.3.q_ref.k_ref.v_ref, ...), custom_call_target="tpu_custom_call", output_to_operand_aliasing={{0}: (4, {}), {1}: (5, {})} | custom-call | flops 3221225472 | bytes 2097152 | tf_op jit(solution)/shard_map/attend/pallas_call | solution.py:369
  158.6 64.8 %feed.1 = (bf16[2048,768]{1,0:T(8,128)(2,1)}, bf16[2048,768]{1,0:T(8,128)(2,1)}, bf16[2048,3072]{1,0:T(8,128)(2,1)}, bf16[2048,3072]{1,0:T(8,128)(2,1)}, f32[204...) custom-call(s32[64]{0:T(128)} %bitcast.122, ...), custom_call_target="tpu_custom_call" | custom-call | flops 43486543872 | bytes 47185920 | tf_op jit(solution)/shard_map/feed/pallas_call | solution.py:686
  223.4 9.2 %grad_of_rows.2 = bf16[4,4,1,96,768]{4,3,2,1,0:T(8,128)(2,1)} custom-call(s32[1]{0:T(128)} %constant.106.clone.1.scalar_ref, bf16[2048,3072]{1,0:T(8,128)(2,1)} %get-tuple-element.91.x_ref, bf16[2048,768]{1,0:T(8,128)(2,1)} %bitcast.125), custom_call_target="tpu_custom_call" | custom-call | flops 9663676416 | bytes 12582912 | tf_op jit(solution)/shard_map/grad_of_rows/pallas_call | solution.py:727
  233.1 13.3 %grad_of_wide.2 = bf16[4,4,5,48,384]{4,3,2,1,0:T(8,128)(2,1)} custom-call(s32[2]{0:T(128)} %pad_add_fusion.4.side_ref, bf16[2048,768]{1,0:T(8,128)(2,1)} %get-tuple-element.89.x_ref, bf16[2048,3072]{1,0:T(8,128)(2,1)} %get-tuple-element.94.y_ref, bf16[2048,768]{1,0:T(8,128)(2,1)} %get-tuple-element.73.o_ref.o_hbm, bf16[2048,768]{1,0:T(8,128)(2,1)} %get-tuple-element.92.dr_hbm), custom_call_target="tpu_custom_call" | custom-call | flops 12079595520 | bytes 12582912 | tf_op jit(solution)/shard_map/grad_of_wide/pallas_call | solution.py:802
  247.3 9.6 %grad_of_rows.3 = bf16[4,4,1,96,768]{4,3,2,1,0:T(8,128)(2,1)} custom-call(s32[1]{0:T(128)} %constant.105.clone.1.scalar_ref, bf16[2048,3072]{1,0:T(8,128)(2,1)} %get-tuple-element.91.x_ref, bf16[2048,768]{1,0:T(8,128)(2,1)} %bitcast.126, bf16[4,4,1,96,768]{4,3,2,1,0:T(8,128)(2,1)} %collective-permute-done.12.refs_0_), custom_call_target="tpu_custom_call" | custom-call | flops 9663676416 | bytes 12582912 | tf_op jit(solution)/shard_map/grad_of_rows/pallas_call | solution.py:727
  256.9 4.5 all-to-all-start.4
  261.4 13.5 %grad_of_wide.3 = bf16[4,4,5,48,384]{4,3,2,1,0:T(8,128)(2,1)} custom-call(s32[2]{0:T(128)} %pad_add_fusion.3.side_ref, bf16[2048,768]{1,0:T(8,128)(2,1)} %get-tuple-element.89.x_ref, bf16[2048,3072]{1,0:T(8,128)(2,1)} %get-tuple-element.94.y_ref, bf16[2048,768]{1,0:T(8,128)(2,1)} %get-tuple-element.73.o_ref.o_hbm, ...), custom_call_target="tpu_custom_call" | custom-call | flops 12079595520 | bytes 12582912 | tf_op jit(solution)/shard_map/grad_of_wide/pallas_call | solution.py:802
  274.9 39.2 %attend_back.2 = (bf16[3,2048,384]{2,1,0:T(8,128)(2,1)}, bf16[4,4,3,48,384]{4,3,2,1,0:T(8,128)(2,1)}) custom-call(s32[2]{0:T(128)} %get-tuple-element.145.scalar_ref, bf16[2048,1152]{1,0:T(8,128)(2,1)} %project.3.q_ref.k_ref.v_ref, bf16[2048,1152]{1,0:T(8,128)(2,1)} %project.3.q_ref.k_ref.v_ref, bf16[2048,1152]{1,0:T(8,128)(2,1)} %project.3.q_ref.k_ref.v_ref, ...), custom_call_target="tpu_custom_call" | custom-call | flops 24159191040 | bytes 12582912 | tf_op jit(solution)/shard_map/attend_back/pallas_call | solution.py:513
  316.7 4.6 %all-to-all-start.5 = ((bf16[4,4,5,48,384]{4,3,2,1,0:T(8,128)(2,1)}), bf16[4,4,5,48,384]{4,3,2,1,0:T(8,128)(2,1)}, u32[]{:S(2)}, u32[]{:S(2)}) async-start(bf16[4,4,5,48,384]{4,3,2,1,0:T(8,128)(2,1)} %grad_of_wide.3), calls=%async_computation.5 | async-start | bytes 5898240 | tf_op jit(solution)/shard_map/all_to_all | solution.py:1234
  325.9 32.2 %attend_back.3.y_ref.refs_0_ = bf16[3,2048,384]{2,1,0:T(8,128)(2,1)} custom-call(s32[2]{0:T(128)} %get-tuple-element.146.scalar_ref, bf16[2048,1152]{1,0:T(8,128)(2,1)} %project.2.q_ref.k_ref.v_ref, bf16[2048,1152]{1,0:T(8,128)(2,1)} %project.2.q_ref.k_ref.v_ref, bf16[2048,1152]{1,0:T(8,128)(2,1)} %project.2.q_ref.k_ref.v_ref, ...), custom_call_target="tpu_custom_call" | custom-call | flops 24159191040 | bytes 12582912 | tf_op jit(solution)/shard_map/attend_back/pallas_call | solution.py:513
  367.0 9.2 %grad_of_columns.1 = bf16[4,4,3,48,384]{4,3,2,1,0:T(8,128)(2,1)} custom-call(s32[1]{0:T(128)} %constant.105.clone.1.scalar_ref, bf16[2048,768]{1,0:T(8,128)(2,1)} %norm_one.1.a_ref.refs_0_.x_ref, bf16[3,2048,384]{2,1,0:T(8,128)(2,1)} %attend_back.3.y_ref.refs_0_, bf16[4,4,3,48,384]{4,3,2,1,0:T(8,128)(2,1)} %collective-permute-done.17.refs_0_), custom_call_target="tpu_custom_call" | custom-call | flops 7247757312 | bytes 12582912 | tf_op jit(solution)/shard_map/grad_of_columns/pallas_call | solution.py:727
  380.5 18.1 %entry.1 = (f32[2048,768]{1,0:T(8,128)}, f32[8,768]{1,0:T(8,128)}, f32[8,768]{1,0:T(8,128)}) custom-call(s32[64]{0:T(128)} %bitcast.123, s32[2]{0:T(128)} %pad_add_fusion.place_ref.side_ref, bf16[2048,768]{1,0:T(8,128)(2,1)} %bitcast.90, f32[2048,768]{1,0:T(8,128)} %get-tuple-element.87.dr_ref, f32[15,768]{1,0:T(8,128)} %vec_master_ref.1, ...), custom_call_target="tpu_custom_call" | custom-call | flops 7247757312 | bytes 31457280 | tf_op jit(solution)/shard_map/entry/pallas_call | solution.py:899
  420.1 20.5 %all_to_all.40.came_ref = bf16[8,208,384]{2,1,0:T(8,128)(2,1)S(1)} all-to-all(bf16[8,208,384]{2,1,0:T(8,128)(2,1)S(1)} %settle.1), channel_id=1, replica_groups=mesh['wide'=8,'narrow'=4] {'wide'}, dimensions={0} | all-to-all | bytes 2555904 | tf_op jit(solution)/shard_map/all_to_all | solution.py:1494
  449.2 6.4 %finish.1 = (f32[768,768]{1,0:T(8,128)}, f32[768,768]{1,0:T(8,128)}, f32[768,768]{1,0:T(8,128)}, f32[15,768]{1,0:T(8,128)}, f32[15,768]{1,0:T(8,128)}, /*index=5...) custom-call(s32[4]{0:T(128)S(1)} %copy-done.9, f32[768,768]{1,0:T(8,128)S(1)} %unpack.1.grad_ref, ...), custom_call_target="tpu_custom_call" | custom-call | flops 11796480 | bytes 15335424 | tf_op jit(solution)/shard_map/finish/pallas_call | solution.py:1179
  (151 shorter events, 105.1 us)
Async XLA Ops:
  5.1 21.6 %all-to-all-start = ((bf16[8,192,384]{2,1,0:T(8,128)(2,1)}), bf16[8,192,384]{2,1,0:T(8,128)(2,1)S(1)}, u32[]{:S(2)}, u32[]{:S(2)}) async-start(bf16[8,192,384]{2,1,0:T(8,128)(2,1)} %pack.1), calls=%async_computation | async-start | bytes 2359296 | tf_op jit(solution)/shard_map/all_to_all | solution.py:1384
  28.5 10.4 %collective-permute-start.1 = (bf16[3,48,384]{2,1,0:T(8,128)(2,1)S(1)}, bf16[3,48,384]{2,1,0:T(8,128)(2,1)S(1)}, u32[]{:S(2)}, u32[]{:S(2)}) collective-permute-start(bf16[3,48,384]{2,1,0:T(8,128)(2,1)S(1)} %bitcast.98), channel_id=1, source_target_pairs={{0,2},{1,3},{2,0},{3,1},{4,6},{5,7},{6,4},{7,5},{8,10},{9,11},{10,... | collective-permute-start | bytes 331784 | tf_op jit(solution)/shard_map/ppermute | solution.py:1230
  40.4 26.2 %all-to-all-start.1 = ((bf16[4,4,3,48,384]{4,3,2,1,0:T(8,128)(2,1)}), bf16[4,4,3,48,384]{4,3,2,1,0:T(8,128)(2,1)}, u32[]{:S(2)}, u32[]{:S(2)}) async-start(bf16[4,4,3,48,384]{4,3,2,1,0:T(8,128)(2,1)} %broadcast_in_dim.49), calls=%async_computation.1 | async-start | bytes 3538944 | tf_op jit(solution)/shard_map/all_to_all | solution.py:1234
  49.7 11.1 %collective-permute-start.5 = (bf16[1,96,768]{2,1,0:T(8,128)(2,1)S(1)}, bf16[1,96,768]{2,1,0:T(8,128)(2,1)S(1)}, u32[]{:S(2)}, u32[]{:S(2)}) collective-permute-start(bf16[1,96,768]{2,1,0:T(8,128)(2,1)S(1)} %maximum_bitcast_fusion.1), channel_id=1, source_target_pairs={{0,2},{1,3},{2,0},{3,1},{4,6},{5,7},{6,4},{7,5},{8,10},{9,11},{10,... | collective-permute-start | bytes 442376 | tf_op jit(solution)/shard_map/ppermute | solution.py:1230
  68.3 33.6 %all-to-all-start.2 = ((bf16[4,4,1,96,768]{4,3,2,1,0:T(8,128)(2,1)}), bf16[4,4,1,96,768]{4,3,2,1,0:T(8,128)(2,1)}, u32[]{:S(2)}, u32[]{:S(2)}) async-start(bf16[4,4,1,96,768]{4,3,2,1,0:T(8,128)(2,1)} %broadcast_in_dim.52), calls=%async_computation.2 | async-start | bytes 4718592 | tf_op jit(solution)/shard_map/all_to_all | solution.py:1234
  77.3 24.5 %collective-permute-start.7 = (bf16[5,48,384]{2,1,0:T(8,128)(2,1)S(1)}, bf16[5,48,384]{2,1,0:T(8,128)(2,1)S(1)}, u32[]{:S(2)}, u32[]{:S(2)}) collective-permute-start(bf16[5,48,384]{2,1,0:T(8,128)(2,1)S(1)} %bitcast.91), channel_id=1, source_target_pairs={{0,1},{1,2},{2,3},{3,0},{4,5},{5,6},{6,7},{7,4},{8,9},{9,10},{10,1... | collective-permute-start | bytes 552968 | tf_op jit(solution)/shard_map/ppermute | solution.py:1230
  80.3 21.5 %collective-permute-start.8 = (bf16[5,48,384]{2,1,0:T(8,128)(2,1)S(1)}, bf16[5,48,384]{2,1,0:T(8,128)(2,1)S(1)}, u32[]{:S(2)}, u32[]{:S(2)}) collective-permute-start(bf16[5,48,384]{2,1,0:T(8,128)(2,1)S(1)} %bitcast.92), channel_id=1, source_target_pairs={{0,2},{1,3},{2,0},{3,1},{4,6},{5,7},{6,4},{7,5},{8,10},{9,11},{10,... | collective-permute-start | bytes 552968 | tf_op jit(solution)/shard_map/ppermute | solution.py:1230
  81.5 20.4 %collective-permute-start.9 = (bf16[5,48,384]{2,1,0:T(8,128)(2,1)S(1)}, bf16[5,48,384]{2,1,0:T(8,128)(2,1)S(1)}, u32[]{:S(2)}, u32[]{:S(2)}) collective-permute-start(bf16[5,48,384]{2,1,0:T(8,128)(2,1)S(1)} %bitcast.93), channel_id=1, source_target_pairs={{0,3},{1,0},{2,1},{3,2},{4,7},{5,4},{6,5},{7,6},{8,11},{9,8},{10,9... | collective-permute-start | bytes 552968 | tf_op jit(solution)/shard_map/ppermute | solution.py:1230
  83.0 40.6 %collective-permute-start.3 = (bf16[4,4,3,48,384]{4,3,2,1,0:T(8,128)(2,1)}, bf16[4,4,3,48,384]{4,3,2,1,0:T(8,128)(2,1)}, u32[]{:S(2)}, u32[]{:S(2)}) collective-permute-start(bf16[4,4,3,48,384]{4,3,2,1,0:T(8,128)(2,1)} %all-to-all-done.1.w_hbm.refs_2_), channel_id=1, source_target_pairs={{0,4},{4,0},{8,12},{12,8},{16,20},{20,16},{24,28},{28,24},{1,5},{5... | collective-permute-start | bytes 5308424 | tf_op jit(solution)/shard_map/ppermute | solution.py:1220
  103.9 44.6 %all-to-all-start.3 = ((bf16[4,4,5,48,384]{4,3,2,1,0:T(8,128)(2,1)}), bf16[4,4,5,48,384]{4,3,2,1,0:T(8,128)(2,1)}, u32[]{:S(2)}, u32[]{:S(2)}) async-start(bf16[4,4,5,48,384]{4,3,2,1,0:T(8,128)(2,1)} %broadcast_in_dim.53), calls=%async_computation.3 | async-start | bytes 5898240 | tf_op jit(solution)/shard_map/all_to_all | solution.py:1234
  148.5 10.1 %collective-permute-start.10 = (bf16[4,4,5,48,384]{4,3,2,1,0:T(8,128)(2,1)}, bf16[4,4,5,48,384]{4,3,2,1,0:T(8,128)(2,1)}, u32[]{:S(2)}, u32[]{:S(2)}) collective-permute-start(bf16[4,4,5,48,384]{4,3,2,1,0:T(8,128)(2,1)} %all-to-all-done.3.wide_mine_hbm), channel_id=1, source_target_pairs={{0,4},{4,0},{8,12},{12,8},{16,20},{20,16},{24,28},{28,24},{1,5},{5... | collective-permute-start | bytes 8847368 | tf_op jit(solution)/shard_map/ppermute | solution.py:1220
  149.1 9.5 %collective-permute-start.11 = (bf16[4,4,1,96,768]{4,3,2,1,0:T(8,128)(2,1)}, bf16[4,4,1,96,768]{4,3,2,1,0:T(8,128)(2,1)}, u32[]{:S(2)}, u32[]{:S(2)}) collective-permute-start(bf16[4,4,1,96,768]{4,3,2,1,0:T(8,128)(2,1)} %all-to-all-done.2.down_mine_hbm), channel_id=1, source_target_pairs={{0,4},{4,0},{8,12},{12,8},{16,20},{20,16},{24,28},{28,24},{1,5},{5... | collective-permute-start | bytes 7077896 | tf_op jit(solution)/shard_map/ppermute | solution.py:1220
  232.6 14.6 %collective-permute-start.12 = (bf16[4,4,1,96,768]{4,3,2,1,0:T(8,128)(2,1)}, bf16[4,4,1,96,768]{4,3,2,1,0:T(8,128)(2,1)}, u32[]{:S(2)}, u32[]{:S(2)}) collective-permute-start(bf16[4,4,1,96,768]{4,3,2,1,0:T(8,128)(2,1)} %grad_of_rows.2), channel_id=1, source_target_pairs={{0,4},{4,0},{8,12},{12,8},{16,20},{20,16},{24,28},{28,24},{1,5},{5... | collective-permute-start | bytes 7077896 | tf_op jit(solution)/shard_map/ppermute | solution.py:1220
  246.5 15.0 %collective-permute-start.13 = (bf16[4,4,5,48,384]{4,3,2,1,0:T(8,128)(2,1)}, bf16[4,4,5,48,384]{4,3,2,1,0:T(8,128)(2,1)}, u32[]{:S(2)}, u32[]{:S(2)}) collective-permute-start(bf16[4,4,5,48,384]{4,3,2,1,0:T(8,128)(2,1)} %grad_of_wide.2), channel_id=1, source_target_pairs={{0,4},{4,0},{8,12},{12,8},{16,20},{20,16},{24,28},{28,24},{1,5},{5... | collective-permute-start | bytes 8847368 | tf_op jit(solution)/shard_map/ppermute | solution.py:1220
  256.9 57.7 %all-to-all-start.4 = ((bf16[4,4,1,96,768]{4,3,2,1,0:T(8,128)(2,1)}), bf16[4,4,1,96,768]{4,3,2,1,0:T(8,128)(2,1)}, u32[]{:S(2)}, u32[]{:S(2)}) async-start(bf16[4,4,1,96,768]{4,3,2,1,0:T(8,128)(2,1)} %grad_of_rows.3), calls=%async_computation.4 | async-start | bytes 4718592 | tf_op jit(solution)/shard_map/all_to_all | solution.py:1234
  314.1 52.9 %collective-permute-start.17 = (bf16[4,4,3,48,384]{4,3,2,1,0:T(8,128)(2,1)}, bf16[4,4,3,48,384]{4,3,2,1,0:T(8,128)(2,1)}, u32[]{:S(2)}, u32[]{:S(2)}) collective-permute-start(bf16[4,4,3,48,384]{4,3,2,1,0:T(8,128)(2,1)} %get-tuple-element.97), channel_id=1, source_target_pairs={{0,4},{4,0},{8,12},{12,8},{16,20},{20,16},{24,28},{28,24},{1,5},{5... | collective-permute-start | bytes 5308424 | tf_op jit(solution)/shard_map/ppermute | solution.py:1220
  316.7 41.4 %all-to-all-start.5 = ((bf16[4,4,5,48,384]{4,3,2,1,0:T(8,128)(2,1)}), bf16[4,4,5,48,384]{4,3,2,1,0:T(8,128)(2,1)}, u32[]{:S(2)}, u32[]{:S(2)}) async-start(bf16[4,4,5,48,384]{4,3,2,1,0:T(8,128)(2,1)} %grad_of_wide.3), calls=%async_computation.5 | async-start | bytes 5898240 | tf_op jit(solution)/shard_map/all_to_all | solution.py:1234
  322.0 38.4 %collective-permute-start.14 = (bf16[1,96,768]{2,1,0:T(8,128)(2,1)S(1)}, bf16[1,96,768]{2,1,0:T(8,128)(2,1)S(1)}, u32[]{:S(2)}, u32[]{:S(2)}) collective-permute-start(bf16[1,96,768]{2,1,0:T(8,128)(2,1)S(1)} %get-tuple-element.130), channel_id=1, source_target_pairs={{0,1},{1,2},{2,3},{3,0},{4,5},{5,6},{6,7},{7,4},{8,9},{9,10},{10,1... | collective-permute-start | bytes 442376 | tf_op jit(solution)/shard_map/ppermute | solution.py:1230
  322.8 37.7 %collective-permute-start.15 = (bf16[1,96,768]{2,1,0:T(8,128)(2,1)S(1)}, bf16[1,96,768]{2,1,0:T(8,128)(2,1)S(1)}, u32[]{:S(2)}, u32[]{:S(2)}) collective-permute-start(bf16[1,96,768]{2,1,0:T(8,128)(2,1)S(1)} %get-tuple-element.129), channel_id=1, source_target_pairs={{0,2},{1,3},{2,0},{3,1},{4,6},{5,7},{6,4},{7,5},{8,10},{9,11},{10,... | collective-permute-start | bytes 442376 | tf_op jit(solution)/shard_map/ppermute | solution.py:1230
  324.5 36.0 %collective-permute-start.16 = (bf16[1,96,768]{2,1,0:T(8,128)(2,1)S(1)}, bf16[1,96,768]{2,1,0:T(8,128)(2,1)S(1)}, u32[]{:S(2)}, u32[]{:S(2)}) collective-permute-start(bf16[1,96,768]{2,1,0:T(8,128)(2,1)S(1)} %get-tuple-element.128), channel_id=1, source_target_pairs={{0,3},{1,0},{2,1},{3,2},{4,7},{5,4},{6,5},{7,6},{8,11},{9,8},{10,9... | collective-permute-start | bytes 442376 | tf_op jit(solution)/shard_map/ppermute | solution.py:1230
  362.1 18.5 %collective-permute-start.18 = (bf16[5,48,384]{2,1,0:T(8,128)(2,1)}, bf16[5,48,384]{2,1,0:T(8,128)(2,1)}, u32[]{:S(2)}, u32[]{:S(2)}) collective-permute-start(bf16[5,48,384]{2,1,0:T(8,128)(2,1)} %get-tuple-element.126), channel_id=1, source_target_pairs={{0,1},{1,2},{2,3},{3,0},{4,5},{5,6},{6,7},{7,4},{8,9},{9,10},{10,1... | collective-permute-start | bytes 552968 | tf_op jit(solution)/shard_map/ppermute | solution.py:1230
  362.7 17.8 %collective-permute-start.19 = (bf16[5,48,384]{2,1,0:T(8,128)(2,1)}, bf16[5,48,384]{2,1,0:T(8,128)(2,1)}, u32[]{:S(2)}, u32[]{:S(2)}) collective-permute-start(bf16[5,48,384]{2,1,0:T(8,128)(2,1)} %get-tuple-element.125), channel_id=1, source_target_pairs={{0,2},{1,3},{2,0},{3,1},{4,6},{5,7},{6,4},{7,5},{8,10},{9,11},{10,... | collective-permute-start | bytes 552968 | tf_op jit(solution)/shard_map/ppermute | solution.py:1230
  364.1 16.4 %collective-permute-start.20 = (bf16[5,48,384]{2,1,0:T(8,128)(2,1)}, bf16[5,48,384]{2,1,0:T(8,128)(2,1)}, u32[]{:S(2)}, u32[]{:S(2)}) collective-permute-start(bf16[5,48,384]{2,1,0:T(8,128)(2,1)} %get-tuple-element.124), channel_id=1, source_target_pairs={{0,3},{1,0},{2,1},{3,2},{4,7},{5,4},{6,5},{7,6},{8,11},{9,8},{10,9... | collective-permute-start | bytes 552968 | tf_op jit(solution)/shard_map/ppermute | solution.py:1230
  376.2 31.7 %all-to-all-start.6 = ((bf16[4,4,3,48,384]{4,3,2,1,0:T(8,128)(2,1)}), bf16[4,4,3,48,384]{4,3,2,1,0:T(8,128)(2,1)S(1)}, u32[]{:S(2)}, u32[]{:S(2)}) async-start(bf16[4,4,3,48,384]{4,3,2,1,0:T(8,128)(2,1)} %grad_of_columns.1), calls=%async_computation.6 | async-start | bytes 3538944 | tf_op jit(solution)/shard_map/all_to_all | solution.py:1234
  (28 other events, 217.0 us)

commit v4 on v3

--- a/solution.py
+++ b/solution.py
@@ -222,6 +222,18 @@
 SHORTEST = 256
 
 
+OWN = 128
+
+
+def by_parts(left, right, dim_left, dim_right, joined):
+    parts = []
+    for start in range(0, QT, OWN):
+        here = slice(start, start + OWN)
+        chosen = left[here, :] if left.shape[0] == QT else left[:, here]
+        parts.append(dot(chosen, right[here, :], dim_left, dim_right))
+    return jnp.concatenate(parts, axis=joined)
+
+
 def fill_bias(length, same_ref, earlier_ref, causal_ref, length_ref):
     key = lax.broadcasted_iota(jnp.int32, (QT, QT), 0)
     query = lax.broadcasted_iota(jnp.int32, (QT, QT), 1)
@@ -230,7 +242,10 @@
     for tile in range(TILES):
         kept = key + tile * QT < length
         own = kept | (key == query)
-        same_ref[tile] = jnp.where((key_block == query_block) & own, 0.0, masked_score)
+        own_key = (query // OWN) * OWN + lax.broadcasted_iota(jnp.int32, (QT, QT), 0) % OWN
+        own_kept = (own_key + tile * QT < length) | (own_key == query)
+        same = (own_key // BLOCK == query_block) & own_kept
+        same_ref[tile] = jnp.where(same, 0.0, masked_score)[:OWN]
         earlier_ref[tile] = jnp.where((key_block < query_block) & kept, 0.0, masked_score)
         causal_ref[tile] = jnp.where((key_block <= query_block) & own, 0.0, masked_score)
     position = lax.broadcasted_iota(jnp.int32, (SEQ, QT), 0)
@@ -238,7 +253,7 @@
 
 
 bias_scratch = [
-    pltpu.VMEM((TILES, QT, QT), full),
+    pltpu.VMEM((TILES, OWN, QT), full),
     pltpu.VMEM((TILES, QT, QT), full),
     pltpu.VMEM((TILES, QT, QT), full),
     pltpu.VMEM((SEQ, QT), full),
@@ -301,7 +316,11 @@
         query = jnp.where(halves, q_ref[row : row + QT, :], jnp.zeros((), low))
         parts = []
         for start, count, kind in segments(tile, noised):
-            scores = dot(k_ref[start : start + count, :], query, 1, 1)
+            keys = k_ref[start : start + count, :]
+            if kind == "same":
+                scores = by_parts(keys, query, 1, 1, 1)
+            else:
+                scores = dot(keys, query, 1, 1)
             parts.append((start, count, masked(scores, kind, tile, start, count, biases)))
         return parts
 
@@ -326,7 +345,11 @@
         row = tile * QT + (0 if noised else SEQ)
         attended = None
         for start, count, expo in weights:
-            product = dot(expo, v_ref[start : start + count, :], 0, 0)
+            values = v_ref[start : start + count, :]
+            if start < SEQ:
+                product = by_parts(expo, values, 0, 0, 0)
+            else:
+                product = dot(expo, values, 0, 0)
             attended = product if attended is None else attended + product
         inverse = jnp.transpose(jnp.broadcast_to(1.0 / total, (PAIR, QT)))
         result = (attended * inverse).astype(low)
@@ -419,8 +442,10 @@
         zero = jnp.zeros((), low)
         query = jnp.where(halves, q_ref[row : row + QT, :], zero)
         grad = jnp.where(plain, grad_ref[row : row + QT, :], zero)
-        scores = dot(k_ref[start : start + count, :], query, 1, 1)
-        return scores, dot(v_ref[start : start + count, :], grad, 1, 1)
+        keys, values = k_ref[start : start + count, :], v_ref[start : start + count, :]
+        if start < SEQ:
+            return by_parts(keys, query, 1, 1, 1), by_parts(values, grad, 1, 1, 1)
+        return dot(keys, query, 1, 1), dot(values, grad, 1, 1)
 
     def keep(head, tile, noised, start, count, kind, pair):
         row = tile * QT + (0 if noised else SEQ)
@@ -430,8 +455,9 @@
         delta = delta_acc[head : head + 1, row : row + QT]
         score_grad = (probs * (prob_grad - delta)).astype(low)
         if kind == "same":
-            own_prob_ref[start : start + count, :] = probs.astype(low)
-            own_score_ref[start : start + count, :] = score_grad
+            own = slice(tile * OWN, (tile + 1) * OWN)
+            own_prob_ref[own, :] = probs.astype(low)
+            own_score_ref[own, :] = score_grad
         else:
             key = start - SEQ
             prob_ref[key : key + count, row : row + QT] = probs.astype(low)
@@ -445,8 +471,10 @@
         row = tile * QT
         rows, clean_rows = slice(row, row + QT), slice(SEQ + row, SEQ + row + QT)
         seen = (slice(row, SEQ), slice(SEQ + row, ROWS))
-        put(v_acc, row, plain, dot(own_prob_ref[rows, :], grad_ref[rows, :]))
-        put(k_acc, row, halves, dot(own_score_ref[rows, :], q_ref[rows, :]))
+        own = slice(tile * OWN, (tile + 1) * OWN)
+        own_prob, own_score = own_prob_ref[own, :], own_score_ref[own, :]
+        put(v_acc, row, plain, by_parts(own_prob, grad_ref[rows, :], 1, 0, 0))
+        put(k_acc, row, halves, by_parts(own_score, q_ref[rows, :], 1, 0, 0))
         put(
             v_acc, SEQ + row, plain,
             dot(prob_ref[rows, seen[0]], grad_ref[seen[0], :])
@@ -461,7 +489,7 @@
         put(
             q_acc, row, halves,
             dot(score_ref[: row + QT, rows], keys, 0, 0)
-            + dot(own_score_ref[rows, :], k_ref[rows, :], 0, 0),
+            + by_parts(own_score, k_ref[rows, :], 0, 0, 0),
         )
         put(q_acc, SEQ + row, halves, dot(score_ref[: row + QT, clean_rows], keys, 0, 0))
 
@@ -528,8 +556,8 @@
                 pltpu.VMEM((8, ROWS), full),
                 pltpu.VMEM((SEQ, ROWS), low),
                 pltpu.VMEM((SEQ, ROWS), low),
-                pltpu.VMEM((SEQ, QT), low),
-                pltpu.VMEM((SEQ, QT), low),
+                pltpu.VMEM((TILES * OWN, QT), low),
+                pltpu.VMEM((TILES * OWN, QT), low),
                 *bias_scratch,
             ],
         ),

time: 463 us -> 460 us (level)
  transfers between devices with their start and end apart: 37 -> 37, of which waited for: 12 -> 13; matrix products, arithmetic and copies ran while one was open for 5% -> 5% of each run, Pallas kernels for 46% -> 46%
where the time goes in v4:
time: 460 us; the launch traced here: 453 us
  Pallas kernels  291 us (63%)
  starting transfers between devices  73.7 us (16%)
  waiting for transfers between devices  31 us (7%)
  blocking collectives  20.5 us (4%)
  other arithmetic  14.8 us (3%)
  local copies, waits for them, and re-layouts  12.5 us (3%)
  between operations  10 us (2%)
    pallas_call x2, Pallas kernels, attend_back(): pl.pallas_call(partial(attend_back_kernel, weighted), grid_spec=pltpu.Pre...  69.9 us
    pallas_call x1, Pallas kernels, feed(): pl.pallas_call(feed_kernel, grid_spec=pltpu.PrefetchScalarGridSpec(num_sc...  64.8 us
    pallas_call x4, Pallas kernels, attend(): pl.pallas_call(partial(attend_kernel, aliased), grid_spec=pltpu.PrefetchS...  45.2 us
    ppermute x21, starting transfers between devices, shift(): lax.ppermute(value, 'narrow', [(i, (i + step) % count) for i in range(cou...  34.5 us
    pallas_call x3, Pallas kernels, weight_call(): pl.pallas_call(partial(weight_kernel, added is not None), grid_spec=pltpu...  28 us
    all_to_all x6, starting transfers between devices, swap_planes(): lax.all_to_all(blocks, 'wide', 0, 0, axis_index_groups=planes_groups())  27.7 us
    pallas_call x2, Pallas kernels, grad_of_wide(): pl.pallas_call(partial(wide_kernel, added is not None), grid_spec=pltpu.P...  26.8 us
    ppermute x21, waiting for transfers between devices, shift(): lax.ppermute(value, 'narrow', [(i, (i + step) % count) for i in range(cou...  23 us
  transfers between devices with their start and end apart: 37, of which 13 were waited for; matrix products, arithmetic and copies ran while one was open for 5% of the time, Pallas kernels for 46%

profile of v4, /device:TPU:0, one launch (start us, length us, event | category | flops | bytes accessed | tf_op | source)
XLA Modules:
  0.0 453.5 jit_solution(11770610175329899237)
XLA Ops:
  4.7 5.5 %all-to-all-start = ((bf16[8,192,384]{2,1,0:T(8,128)(2,1)}), bf16[8,192,384]{2,1,0:T(8,128)(2,1)S(1)}, u32[]{:S(2)}, u32[]{:S(2)}) async-start(bf16[8,192,384]{2,1,0:T(8,128)(2,1)} %pack.1), calls=%async_computation | async-start | bytes 2359296 | tf_op jit(solution)/shard_map/all_to_all | solution.py:1412
  14.8 7.7 %norm_one.1.a_ref.refs_0_.x_ref = bf16[2048,768]{1,0:T(8,128)(2,1)} custom-call(s32[64]{0:T(128)} %bitcast.121, bf16[2048,768]{1,0:T(8,128)(2,1)} %bitcast.88, f32[15,768]{1,0:T(8,128)} %vec_master_ref.1), custom_call_target="tpu_custom_call" | custom-call | flops 15728640 | bytes 6291456 | tf_op jit(solution)/shard_map/norm_one/pallas_call | solution.py:150
  55.8 5.3 %collective-permute-done.5 = bf16[1,96,768]{2,1,0:T(8,128)(2,1)S(1)} collective-permute-done((bf16[1,96,768]{2,1,0:T(8,128)(2,1)S(1)}, bf16[1,96,768]{2,1,0:T(8,128)(2,1)S(1)}, u32[]{:S(2)}, u32[]{:S(2)}) %collective-permute-start.5) | collective-permute-done | bytes 147488 | tf_op jit(solution)/shard_map/ppermute | solution.py:1258
  61.1 5.8 %all-to-all-done.1.w_hbm.refs_2_ = bf16[4,4,3,48,384]{4,3,2,1,0:T(8,128)(2,1)} async-done(((bf16[4,4,3,48,384]{4,3,2,1,0:T(8,128)(2,1)}), bf16[4,4,3,48,384]{4,3,2,1,0:T(8,128)(2,1)}, u32[]{:S(2)}, u32[]{:S(2)}) %all-to-all-start.1) | async-done | bytes 1769504 | tf_op jit(solution)/shard_map/all_to_all | solution.py:1262
  83.3 10.1 %project.2.q_ref.k_ref.v_ref = bf16[2048,1152]{1,0:T(8,128)(2,1)} custom-call(s32[2]{0:T(128)} %pad_add_fusion.place_ref.side_ref, bf16[2048,768]{1,0:T(8,128)(2,1)} %norm_one.1.a_ref.refs_0_.x_ref, bf16[4,4,3,48,384]{4,3,2,1,0:T(8,128)(2,1)} %all-to-all-done.1.w_hbm.refs_2_, f32[1024,128]{1,0:T(8,128)} %get-tuple-element.147.cos_ref, ...), custom_call_target="tpu_custom_call" | custom-call | flops 3623878656 | bytes 12582912 | tf_op jit(solution)/shard_map/project/pallas_call | solution.py:202
  93.4 8.5 %attend.4 = (bf16[2048,768]{1,0:T(8,128)(2,1)}, f32[6,2,2048]{2,1,0:T(2,128)}) custom-call(s32[2]{0:T(128)} %get-tuple-element.146.scalar_ref, bf16[2048,1152]{1,0:T(8,128)(2,1)} %project.2.q_ref.k_ref.v_ref, bf16[2048,1152]{1,0:T(8,128)(2,1)} %project.2.q_ref.k_ref.v_ref, bf16[2048,1152]{1,0:T(8,128)(2,1)} %project.2.q_ref.k_ref.v_ref), custom_call_target="tpu_custom_call" | custom-call | flops 3221225472 | bytes 2097152 | tf_op jit(solution)/shard_map/attend/pallas_call | solution.py:392
  103.9 5.1 %all-to-all-start.3 = ((bf16[4,4,5,48,384]{4,3,2,1,0:T(8,128)(2,1)}), bf16[4,4,5,48,384]{4,3,2,1,0:T(8,128)(2,1)}, u32[]{:S(2)}, u32[]{:S(2)}) async-start(bf16[4,4,5,48,384]{4,3,2,1,0:T(8,128)(2,1)} %broadcast_in_dim.53), calls=%async_computation.3 | async-start | bytes 5898240 | tf_op jit(solution)/shard_map/all_to_all | solution.py:1262
  109.1 14.0 %attend.5 = (bf16[2048,768]{1,0:T(8,128)(2,1)}, f32[6,2,2048]{2,1,0:T(2,128)}) custom-call(s32[2]{0:T(128)} %get-tuple-element.146.scalar_ref, bf16[2048,1152]{1,0:T(8,128)(2,1)} %project.2.q_ref.k_ref.v_ref, bf16[2048,1152]{1,0:T(8,128)(2,1)} %project.2.q_ref.k_ref.v_ref, ...), custom_call_target="tpu_custom_call", output_to_operand_aliasing={{0}: (4, {}), {1}: (5, {})} | custom-call | flops 6442450944 | bytes 4194304 | tf_op jit(solution)/shard_map/attend/pallas_call | solution.py:392
  123.1 10.1 %project.3.q_ref.k_ref.v_ref = bf16[2048,1152]{1,0:T(8,128)(2,1)} custom-call(s32[2]{0:T(128)} %pad_add_fusion.place_ref.side_ref, bf16[2048,768]{1,0:T(8,128)(2,1)} %norm_one.1.a_ref.refs_0_.x_ref, bf16[4,4,3,48,384]{4,3,2,1,0:T(8,128)(2,1)} %collective-permute-done.3.w_hbm.refs_3_, f32[1024,128]{1,0:T(8,128)} %get-tuple-element.147.cos_ref, ...), custom_call_target="tpu_custom_call" | custom-call | flops 3623878656 | bytes 12582912 | tf_op jit(solution)/shard_map/project/pallas_call | solution.py:202
  133.2 14.2 %attend.6 = (bf16[2048,768]{1,0:T(8,128)(2,1)}, f32[6,2,2048]{2,1,0:T(2,128)}) custom-call(s32[2]{0:T(128)} %get-tuple-element.145.scalar_ref, bf16[2048,1152]{1,0:T(8,128)(2,1)} %project.3.q_ref.k_ref.v_ref, bf16[2048,1152]{1,0:T(8,128)(2,1)} %project.3.q_ref.k_ref.v_ref, ...), custom_call_target="tpu_custom_call", output_to_operand_aliasing={{0}: (4, {}), {1}: (5, {})} | custom-call | flops 6442450944 | bytes 4194304 | tf_op jit(solution)/shard_map/attend/pallas_call | solution.py:392
  148.8 8.5 %attend.7 = (bf16[2048,768]{1,0:T(8,128)(2,1)}, f32[6,2,2048]{2,1,0:T(2,128)}) custom-call(s32[2]{0:T(128)} %get-tuple-element.145.scalar_ref, bf16[2048,1152]{1,0:T(8,128)(2,1)} %project.3.q_ref.k_ref.v_ref, bf16[2048,1152]{1,0:T(8,128)(2,1)} %project.3.q_ref.k_ref.v_ref, ...), custom_call_target="tpu_custom_call", output_to_operand_aliasing={{0}: (4, {}), {1}: (5, {})} | custom-call | flops 3221225472 | bytes 2097152 | tf_op jit(solution)/shard_map/attend/pallas_call | solution.py:392
  157.3 64.8 %feed.1 = (bf16[2048,768]{1,0:T(8,128)(2,1)}, bf16[2048,768]{1,0:T(8,128)(2,1)}, bf16[2048,3072]{1,0:T(8,128)(2,1)}, bf16[2048,3072]{1,0:T(8,128)(2,1)}, f32[204...) custom-call(s32[64]{0:T(128)} %bitcast.122, ...), custom_call_target="tpu_custom_call" | custom-call | flops 43486543872 | bytes 47185920 | tf_op jit(solution)/shard_map/feed/pallas_call | solution.py:714
  222.1 9.2 %grad_of_rows.2 = bf16[4,4,1,96,768]{4,3,2,1,0:T(8,128)(2,1)} custom-call(s32[1]{0:T(128)} %constant.106.clone.1.scalar_ref, bf16[2048,3072]{1,0:T(8,128)(2,1)} %get-tuple-element.91.x_ref, bf16[2048,768]{1,0:T(8,128)(2,1)} %bitcast.125), custom_call_target="tpu_custom_call" | custom-call | flops 9663676416 | bytes 12582912 | tf_op jit(solution)/shard_map/grad_of_rows/pallas_call | solution.py:755
  231.7 13.3 %grad_of_wide.2 = bf16[4,4,5,48,384]{4,3,2,1,0:T(8,128)(2,1)} custom-call(s32[2]{0:T(128)} %pad_add_fusion.4.side_ref, bf16[2048,768]{1,0:T(8,128)(2,1)} %get-tuple-element.89.x_ref, bf16[2048,3072]{1,0:T(8,128)(2,1)} %get-tuple-element.94.y_ref, bf16[2048,768]{1,0:T(8,128)(2,1)} %get-tuple-element.73.o_ref.o_hbm, bf16[2048,768]{1,0:T(8,128)(2,1)} %get-tuple-element.92.dr_hbm), custom_call_target="tpu_custom_call" | custom-call | flops 12079595520 | bytes 12582912 | tf_op jit(solution)/shard_map/grad_of_wide/pallas_call | solution.py:830
  245.9 9.6 %grad_of_rows.3 = bf16[4,4,1,96,768]{4,3,2,1,0:T(8,128)(2,1)} custom-call(s32[1]{0:T(128)} %constant.105.clone.1.scalar_ref, bf16[2048,3072]{1,0:T(8,128)(2,1)} %get-tuple-element.91.x_ref, bf16[2048,768]{1,0:T(8,128)(2,1)} %bitcast.126, bf16[4,4,1,96,768]{4,3,2,1,0:T(8,128)(2,1)} %collective-permute-done.12.refs_0_), custom_call_target="tpu_custom_call" | custom-call | flops 9663676416 | bytes 12582912 | tf_op jit(solution)/shard_map/grad_of_rows/pallas_call | solution.py:755
  255.5 4.5 all-to-all-start.4
  260.1 13.5 %grad_of_wide.3 = bf16[4,4,5,48,384]{4,3,2,1,0:T(8,128)(2,1)} custom-call(s32[2]{0:T(128)} %pad_add_fusion.3.side_ref, bf16[2048,768]{1,0:T(8,128)(2,1)} %get-tuple-element.89.x_ref, bf16[2048,3072]{1,0:T(8,128)(2,1)} %get-tuple-element.94.y_ref, bf16[2048,768]{1,0:T(8,128)(2,1)} %get-tuple-element.73.o_ref.o_hbm, ...), custom_call_target="tpu_custom_call" | custom-call | flops 12079595520 | bytes 12582912 | tf_op jit(solution)/shard_map/grad_of_wide/pallas_call | solution.py:830
  273.6 38.3 %attend_back.2 = (bf16[3,2048,384]{2,1,0:T(8,128)(2,1)}, bf16[4,4,3,48,384]{4,3,2,1,0:T(8,128)(2,1)}) custom-call(s32[2]{0:T(128)} %get-tuple-element.145.scalar_ref, bf16[2048,1152]{1,0:T(8,128)(2,1)} %project.3.q_ref.k_ref.v_ref, bf16[2048,1152]{1,0:T(8,128)(2,1)} %project.3.q_ref.k_ref.v_ref, bf16[2048,1152]{1,0:T(8,128)(2,1)} %project.3.q_ref.k_ref.v_ref, ...), custom_call_target="tpu_custom_call" | custom-call | flops 24159191040 | bytes 12582912 | tf_op jit(solution)/shard_map/attend_back/pallas_call | solution.py:541
  314.4 4.9 %all-to-all-start.5 = ((bf16[4,4,5,48,384]{4,3,2,1,0:T(8,128)(2,1)}), bf16[4,4,5,48,384]{4,3,2,1,0:T(8,128)(2,1)}, u32[]{:S(2)}, u32[]{:S(2)}) async-start(bf16[4,4,5,48,384]{4,3,2,1,0:T(8,128)(2,1)} %grad_of_wide.3), calls=%async_computation.5 | async-start | bytes 5898240 | tf_op jit(solution)/shard_map/all_to_all | solution.py:1262
  323.8 31.5 %attend_back.3.y_ref.refs_0_ = bf16[3,2048,384]{2,1,0:T(8,128)(2,1)} custom-call(s32[2]{0:T(128)} %get-tuple-element.146.scalar_ref, bf16[2048,1152]{1,0:T(8,128)(2,1)} %project.2.q_ref.k_ref.v_ref, bf16[2048,1152]{1,0:T(8,128)(2,1)} %project.2.q_ref.k_ref.v_ref, bf16[2048,1152]{1,0:T(8,128)(2,1)} %project.2.q_ref.k_ref.v_ref, ...), custom_call_target="tpu_custom_call" | custom-call | flops 24159191040 | bytes 12582912 | tf_op jit(solution)/shard_map/attend_back/pallas_call | solution.py:541
  364.3 9.2 %grad_of_columns.1 = bf16[4,4,3,48,384]{4,3,2,1,0:T(8,128)(2,1)} custom-call(s32[1]{0:T(128)} %constant.105.clone.1.scalar_ref, bf16[2048,768]{1,0:T(8,128)(2,1)} %norm_one.1.a_ref.refs_0_.x_ref, bf16[3,2048,384]{2,1,0:T(8,128)(2,1)} %attend_back.3.y_ref.refs_0_, bf16[4,4,3,48,384]{4,3,2,1,0:T(8,128)(2,1)} %collective-permute-done.17.refs_0_), custom_call_target="tpu_custom_call" | custom-call | flops 7247757312 | bytes 12582912 | tf_op jit(solution)/shard_map/grad_of_columns/pallas_call | solution.py:755
  377.9 18.1 %entry.1 = (f32[2048,768]{1,0:T(8,128)}, f32[8,768]{1,0:T(8,128)}, f32[8,768]{1,0:T(8,128)}) custom-call(s32[64]{0:T(128)} %bitcast.123, s32[2]{0:T(128)} %pad_add_fusion.place_ref.side_ref, bf16[2048,768]{1,0:T(8,128)(2,1)} %bitcast.90, f32[2048,768]{1,0:T(8,128)} %get-tuple-element.87.dr_ref, f32[15,768]{1,0:T(8,128)} %vec_master_ref.1, ...), custom_call_target="tpu_custom_call" | custom-call | flops 7247757312 | bytes 31457280 | tf_op jit(solution)/shard_map/entry/pallas_call | solution.py:927
  417.5 20.5 %all_to_all.40.came_ref = bf16[8,208,384]{2,1,0:T(8,128)(2,1)S(1)} all-to-all(bf16[8,208,384]{2,1,0:T(8,128)(2,1)S(1)} %settle.1), channel_id=1, replica_groups=mesh['wide'=8,'narrow'=4] {'wide'}, dimensions={0} | all-to-all | bytes 2555904 | tf_op jit(solution)/shard_map/all_to_all | solution.py:1522
  446.6 6.4 %finish.1 = (f32[768,768]{1,0:T(8,128)}, f32[768,768]{1,0:T(8,128)}, f32[768,768]{1,0:T(8,128)}, f32[15,768]{1,0:T(8,128)}, f32[15,768]{1,0:T(8,128)}, /*index=5...) custom-call(s32[4]{0:T(128)S(1)} %copy-done.9, f32[768,768]{1,0:T(8,128)S(1)} %unpack.1.grad_ref, ...), custom_call_target="tpu_custom_call" | custom-call | flops 11796480 | bytes 15335424 | tf_op jit(solution)/shard_map/finish/pallas_call | solution.py:1207
  (151 shorter events, 104.6 us)
Async XLA Ops:
  4.7 22.3 %all-to-all-start = ((bf16[8,192,384]{2,1,0:T(8,128)(2,1)}), bf16[8,192,384]{2,1,0:T(8,128)(2,1)S(1)}, u32[]{:S(2)}, u32[]{:S(2)}) async-start(bf16[8,192,384]{2,1,0:T(8,128)(2,1)} %pack.1), calls=%async_computation | async-start | bytes 2359296 | tf_op jit(solution)/shard_map/all_to_all | solution.py:1412
  28.7 10.5 %collective-permute-start.1 = (bf16[3,48,384]{2,1,0:T(8,128)(2,1)S(1)}, bf16[3,48,384]{2,1,0:T(8,128)(2,1)S(1)}, u32[]{:S(2)}, u32[]{:S(2)}) collective-permute-start(bf16[3,48,384]{2,1,0:T(8,128)(2,1)S(1)} %bitcast.98), channel_id=1, source_target_pairs={{0,2},{1,3},{2,0},{3,1},{4,6},{5,7},{6,4},{7,5},{8,10},{9,11},{10,... | collective-permute-start | bytes 331784 | tf_op jit(solution)/shard_map/ppermute | solution.py:1258
  40.6 26.2 %all-to-all-start.1 = ((bf16[4,4,3,48,384]{4,3,2,1,0:T(8,128)(2,1)}), bf16[4,4,3,48,384]{4,3,2,1,0:T(8,128)(2,1)}, u32[]{:S(2)}, u32[]{:S(2)}) async-start(bf16[4,4,3,48,384]{4,3,2,1,0:T(8,128)(2,1)} %broadcast_in_dim.49), calls=%async_computation.1 | async-start | bytes 3538944 | tf_op jit(solution)/shard_map/all_to_all | solution.py:1262
  49.9 11.2 %collective-permute-start.5 = (bf16[1,96,768]{2,1,0:T(8,128)(2,1)S(1)}, bf16[1,96,768]{2,1,0:T(8,128)(2,1)S(1)}, u32[]{:S(2)}, u32[]{:S(2)}) collective-permute-start(bf16[1,96,768]{2,1,0:T(8,128)(2,1)S(1)} %maximum_bitcast_fusion.1), channel_id=1, source_target_pairs={{0,2},{1,3},{2,0},{3,1},{4,6},{5,7},{6,4},{7,5},{8,10},{9,11},{10,... | collective-permute-start | bytes 442376 | tf_op jit(solution)/shard_map/ppermute | solution.py:1258
  51.6 9.5 %collective-permute-start.6 = (bf16[1,96,768]{2,1,0:T(8,128)(2,1)S(1)}, bf16[1,96,768]{2,1,0:T(8,128)(2,1)S(1)}, u32[]{:S(2)}, u32[]{:S(2)}) collective-permute-start(bf16[1,96,768]{2,1,0:T(8,128)(2,1)S(1)} %maximum_bitcast_fusion.1), channel_id=1, source_target_pairs={{0,3},{1,0},{2,1},{3,2},{4,7},{5,4},{6,5},{7,6},{8,11},{9,8},{10,9... | collective-permute-start | bytes 442376 | tf_op jit(solution)/shard_map/ppermute | solution.py:1258
  68.6 33.4 %all-to-all-start.2 = ((bf16[4,4,1,96,768]{4,3,2,1,0:T(8,128)(2,1)}), bf16[4,4,1,96,768]{4,3,2,1,0:T(8,128)(2,1)}, u32[]{:S(2)}, u32[]{:S(2)}) async-start(bf16[4,4,1,96,768]{4,3,2,1,0:T(8,128)(2,1)} %broadcast_in_dim.52), calls=%async_computation.2 | async-start | bytes 4718592 | tf_op jit(solution)/shard_map/all_to_all | solution.py:1262
  77.6 24.3 %collective-permute-start.7 = (bf16[5,48,384]{2,1,0:T(8,128)(2,1)S(1)}, bf16[5,48,384]{2,1,0:T(8,128)(2,1)S(1)}, u32[]{:S(2)}, u32[]{:S(2)}) collective-permute-start(bf16[5,48,384]{2,1,0:T(8,128)(2,1)S(1)} %bitcast.91), channel_id=1, source_target_pairs={{0,1},{1,2},{2,3},{3,0},{4,5},{5,6},{6,7},{7,4},{8,9},{9,10},{10,1... | collective-permute-start | bytes 552968 | tf_op jit(solution)/shard_map/ppermute | solution.py:1258
  80.6 21.3 %collective-permute-start.8 = (bf16[5,48,384]{2,1,0:T(8,128)(2,1)S(1)}, bf16[5,48,384]{2,1,0:T(8,128)(2,1)S(1)}, u32[]{:S(2)}, u32[]{:S(2)}) collective-permute-start(bf16[5,48,384]{2,1,0:T(8,128)(2,1)S(1)} %bitcast.92), channel_id=1, source_target_pairs={{0,2},{1,3},{2,0},{3,1},{4,6},{5,7},{6,4},{7,5},{8,10},{9,11},{10,... | collective-permute-start | bytes 552968 | tf_op jit(solution)/shard_map/ppermute | solution.py:1258
  81.8 20.1 %collective-permute-start.9 = (bf16[5,48,384]{2,1,0:T(8,128)(2,1)S(1)}, bf16[5,48,384]{2,1,0:T(8,128)(2,1)S(1)}, u32[]{:S(2)}, u32[]{:S(2)}) collective-permute-start(bf16[5,48,384]{2,1,0:T(8,128)(2,1)S(1)} %bitcast.93), channel_id=1, source_target_pairs={{0,3},{1,0},{2,1},{3,2},{4,7},{5,4},{6,5},{7,6},{8,11},{9,8},{10,9... | collective-permute-start | bytes 552968 | tf_op jit(solution)/shard_map/ppermute | solution.py:1258
  83.3 39.8 %collective-permute-start.3 = (bf16[4,4,3,48,384]{4,3,2,1,0:T(8,128)(2,1)}, bf16[4,4,3,48,384]{4,3,2,1,0:T(8,128)(2,1)}, u32[]{:S(2)}, u32[]{:S(2)}) collective-permute-start(bf16[4,4,3,48,384]{4,3,2,1,0:T(8,128)(2,1)} %all-to-all-done.1.w_hbm.refs_2_), channel_id=1, source_target_pairs={{0,4},{4,0},{8,12},{12,8},{16,20},{20,16},{24,28},{28,24},{1,5},{5... | collective-permute-start | bytes 5308424 | tf_op jit(solution)/shard_map/ppermute | solution.py:1248
  103.9 43.4 %all-to-all-start.3 = ((bf16[4,4,5,48,384]{4,3,2,1,0:T(8,128)(2,1)}), bf16[4,4,5,48,384]{4,3,2,1,0:T(8,128)(2,1)}, u32[]{:S(2)}, u32[]{:S(2)}) async-start(bf16[4,4,5,48,384]{4,3,2,1,0:T(8,128)(2,1)} %broadcast_in_dim.53), calls=%async_computation.3 | async-start | bytes 5898240 | tf_op jit(solution)/shard_map/all_to_all | solution.py:1262
  147.4 9.9 %collective-permute-start.10 = (bf16[4,4,5,48,384]{4,3,2,1,0:T(8,128)(2,1)}, bf16[4,4,5,48,384]{4,3,2,1,0:T(8,128)(2,1)}, u32[]{:S(2)}, u32[]{:S(2)}) collective-permute-start(bf16[4,4,5,48,384]{4,3,2,1,0:T(8,128)(2,1)} %all-to-all-done.3.wide_mine_hbm), channel_id=1, source_target_pairs={{0,4},{4,0},{8,12},{12,8},{16,20},{20,16},{24,28},{28,24},{1,5},{5... | collective-permute-start | bytes 8847368 | tf_op jit(solution)/shard_map/ppermute | solution.py:1248
  231.3 14.6 %collective-permute-start.12 = (bf16[4,4,1,96,768]{4,3,2,1,0:T(8,128)(2,1)}, bf16[4,4,1,96,768]{4,3,2,1,0:T(8,128)(2,1)}, u32[]{:S(2)}, u32[]{:S(2)}) collective-permute-start(bf16[4,4,1,96,768]{4,3,2,1,0:T(8,128)(2,1)} %grad_of_rows.2), channel_id=1, source_target_pairs={{0,4},{4,0},{8,12},{12,8},{16,20},{20,16},{24,28},{28,24},{1,5},{5... | collective-permute-start | bytes 7077896 | tf_op jit(solution)/shard_map/ppermute | solution.py:1248
  245.1 15.0 %collective-permute-start.13 = (bf16[4,4,5,48,384]{4,3,2,1,0:T(8,128)(2,1)}, bf16[4,4,5,48,384]{4,3,2,1,0:T(8,128)(2,1)}, u32[]{:S(2)}, u32[]{:S(2)}) collective-permute-start(bf16[4,4,5,48,384]{4,3,2,1,0:T(8,128)(2,1)} %grad_of_wide.2), channel_id=1, source_target_pairs={{0,4},{4,0},{8,12},{12,8},{16,20},{20,16},{24,28},{28,24},{1,5},{5... | collective-permute-start | bytes 8847368 | tf_op jit(solution)/shard_map/ppermute | solution.py:1248
  255.5 56.8 %all-to-all-start.4 = ((bf16[4,4,1,96,768]{4,3,2,1,0:T(8,128)(2,1)}), bf16[4,4,1,96,768]{4,3,2,1,0:T(8,128)(2,1)}, u32[]{:S(2)}, u32[]{:S(2)}) async-start(bf16[4,4,1,96,768]{4,3,2,1,0:T(8,128)(2,1)} %grad_of_rows.3), calls=%async_computation.4 | async-start | bytes 4718592 | tf_op jit(solution)/shard_map/all_to_all | solution.py:1262
  311.9 52.4 %collective-permute-start.17 = (bf16[4,4,3,48,384]{4,3,2,1,0:T(8,128)(2,1)}, bf16[4,4,3,48,384]{4,3,2,1,0:T(8,128)(2,1)}, u32[]{:S(2)}, u32[]{:S(2)}) collective-permute-start(bf16[4,4,3,48,384]{4,3,2,1,0:T(8,128)(2,1)} %get-tuple-element.97), channel_id=1, source_target_pairs={{0,4},{4,0},{8,12},{12,8},{16,20},{20,16},{24,28},{28,24},{1,5},{5... | collective-permute-start | bytes 5308424 | tf_op jit(solution)/shard_map/ppermute | solution.py:1248
  314.4 41.0 %all-to-all-start.5 = ((bf16[4,4,5,48,384]{4,3,2,1,0:T(8,128)(2,1)}), bf16[4,4,5,48,384]{4,3,2,1,0:T(8,128)(2,1)}, u32[]{:S(2)}, u32[]{:S(2)}) async-start(bf16[4,4,5,48,384]{4,3,2,1,0:T(8,128)(2,1)} %grad_of_wide.3), calls=%async_computation.5 | async-start | bytes 5898240 | tf_op jit(solution)/shard_map/all_to_all | solution.py:1262
  320.0 37.8 %collective-permute-start.14 = (bf16[1,96,768]{2,1,0:T(8,128)(2,1)S(1)}, bf16[1,96,768]{2,1,0:T(8,128)(2,1)S(1)}, u32[]{:S(2)}, u32[]{:S(2)}) collective-permute-start(bf16[1,96,768]{2,1,0:T(8,128)(2,1)S(1)} %get-tuple-element.130), channel_id=1, source_target_pairs={{0,1},{1,2},{2,3},{3,0},{4,5},{5,6},{6,7},{7,4},{8,9},{9,10},{10,1... | collective-permute-start | bytes 442376 | tf_op jit(solution)/shard_map/ppermute | solution.py:1258
  321.0 36.8 %collective-permute-start.15 = (bf16[1,96,768]{2,1,0:T(8,128)(2,1)S(1)}, bf16[1,96,768]{2,1,0:T(8,128)(2,1)S(1)}, u32[]{:S(2)}, u32[]{:S(2)}) collective-permute-start(bf16[1,96,768]{2,1,0:T(8,128)(2,1)S(1)} %get-tuple-element.129), channel_id=1, source_target_pairs={{0,2},{1,3},{2,0},{3,1},{4,6},{5,7},{6,4},{7,5},{8,10},{9,11},{10,... | collective-permute-start | bytes 442376 | tf_op jit(solution)/shard_map/ppermute | solution.py:1258
  322.6 35.3 %collective-permute-start.16 = (bf16[1,96,768]{2,1,0:T(8,128)(2,1)S(1)}, bf16[1,96,768]{2,1,0:T(8,128)(2,1)S(1)}, u32[]{:S(2)}, u32[]{:S(2)}) collective-permute-start(bf16[1,96,768]{2,1,0:T(8,128)(2,1)S(1)} %get-tuple-element.128), channel_id=1, source_target_pairs={{0,3},{1,0},{2,1},{3,2},{4,7},{5,4},{6,5},{7,6},{8,11},{9,8},{10,9... | collective-permute-start | bytes 442376 | tf_op jit(solution)/shard_map/ppermute | solution.py:1258
  359.4 18.5 %collective-permute-start.18 = (bf16[5,48,384]{2,1,0:T(8,128)(2,1)}, bf16[5,48,384]{2,1,0:T(8,128)(2,1)}, u32[]{:S(2)}, u32[]{:S(2)}) collective-permute-start(bf16[5,48,384]{2,1,0:T(8,128)(2,1)} %get-tuple-element.126), channel_id=1, source_target_pairs={{0,1},{1,2},{2,3},{3,0},{4,5},{5,6},{6,7},{7,4},{8,9},{9,10},{10,1... | collective-permute-start | bytes 552968 | tf_op jit(solution)/shard_map/ppermute | solution.py:1258
  360.1 17.7 %collective-permute-start.19 = (bf16[5,48,384]{2,1,0:T(8,128)(2,1)}, bf16[5,48,384]{2,1,0:T(8,128)(2,1)}, u32[]{:S(2)}, u32[]{:S(2)}) collective-permute-start(bf16[5,48,384]{2,1,0:T(8,128)(2,1)} %get-tuple-element.125), channel_id=1, source_target_pairs={{0,2},{1,3},{2,0},{3,1},{4,6},{5,7},{6,4},{7,5},{8,10},{9,11},{10,... | collective-permute-start | bytes 552968 | tf_op jit(solution)/shard_map/ppermute | solution.py:1258
  361.5 16.4 %collective-permute-start.20 = (bf16[5,48,384]{2,1,0:T(8,128)(2,1)}, bf16[5,48,384]{2,1,0:T(8,128)(2,1)}, u32[]{:S(2)}, u32[]{:S(2)}) collective-permute-start(bf16[5,48,384]{2,1,0:T(8,128)(2,1)} %get-tuple-element.124), channel_id=1, source_target_pairs={{0,3},{1,0},{2,1},{3,2},{4,7},{5,4},{6,5},{7,6},{8,11},{9,8},{10,9... | collective-permute-start | bytes 552968 | tf_op jit(solution)/shard_map/ppermute | solution.py:1258
  373.5 31.8 %all-to-all-start.6 = ((bf16[4,4,3,48,384]{4,3,2,1,0:T(8,128)(2,1)}), bf16[4,4,3,48,384]{4,3,2,1,0:T(8,128)(2,1)S(1)}, u32[]{:S(2)}, u32[]{:S(2)}) async-start(bf16[4,4,3,48,384]{4,3,2,1,0:T(8,128)(2,1)} %grad_of_columns.1), calls=%async_computation.6 | async-start | bytes 3538944 | tf_op jit(solution)/shard_map/all_to_all | solution.py:1262
  (28 other events, 217.3 us)
